TPU v7x, 32 devices: a whole 2x2x4 slice. The times are simulated.
32 devices in a mesh: col: 8 (over z, core), sec: 4 (over y, x).
Axes of the slice: x: 2, y: 2, z: 4, core: 2. Of those that a mesh axis runs over, the one named last changes fastest.
Arguments:
- env_right: bfloat16 [1, 16384, 128], P(None, 'sec'), may hold values from -6 to 6
- transfer: bfloat16 [8, 1, 16384, 4, 128], P('col', None, 'sec'), may hold values from -0.25 to 0.25
- sources: int32 [8, 1, 128, 4], P('col', None, 'sec'), may hold values from 0 to 127, as said below
- env_left: bfloat16 [8, 1, 16384, 128], P('col', None, 'sec'), may hold values from -0.5 to 0.5
Outputs:
- env_out: bfloat16 [8, 1, 16384, 128], P('col', None, 'sec')
- grad: bfloat16 [8, 1, 16384, 4, 128], P('col', None, 'sec')
Inputs may be any that keep to these rules, and one draw needn't show every extreme that they name: `sources`: every source tile lies within 2 tiles of its output tile; each list holds the tiles at offsets -2 and +2 (reflected at the ends of the space) and two of the offsets -1, 0, 1.
All inputs are finite; a program needn't handle non-finite values.
Results may differ from a plain program's by a relative error of at most 0.029.
Values may be sent and summed in bfloat16 or wider, within the bound.
No kernel may reach another device: no remote copies, remote signals or barrier semaphores. Data moves between devices by JAX's collectives and lax.ppermute only.
A program may use at most 64 MiB of HBM per device.

v0:
```python
import jax
import jax.numpy as jnp
from jax import lax
from jax.sharding import PartitionSpec as P

TILE = 128
REACH = 2


def passed_along(value, axis, by):
    devices = lax.axis_size(axis)
    pairs = [(i, i + by) for i in range(devices) if 0 <= i + by < devices]
    return lax.ppermute(value, axis, pairs)


def padded(value, sides, width):
    for axis, dim in sides:
        devices, length = (lax.axis_size(axis), value.shape[dim])
        up = [(i, (i + 1) % devices) for i in range(devices - 1)]
        down = [(j, i) for i, j in up]
        last = lax.slice_in_dim(value, length - width, length, axis=dim)
        leading = lax.slice_in_dim(value, 0, width, axis=dim)
        before = lax.ppermute(last, axis, up)
        after = lax.ppermute(leading, axis, down)
        value = jnp.concatenate([before, value, after], axis=dim)
    return value


def pick_blocks(haloed, local_sources):
    batch = haloed.shape[0]
    width = haloed.shape[2]
    blocks = haloed.reshape(batch, -1, TILE, width)

    def one_row(row_blocks, row_sources):
        return row_blocks[row_sources]

    return jax.vmap(one_row)(blocks, local_sources)


def advance(block_rows, picked):
    batch = block_rows.shape[0]
    length = block_rows.shape[1]
    tiles_here = length // TILE
    blocks = block_rows.reshape(batch, tiles_here, TILE, block_rows.shape[2], block_rows.shape[3])
    fresh = jnp.einsum("rtopq,rtpqk->rtok", blocks, picked, preferred_element_type=jnp.float32)
    return fresh.reshape(batch, length, picked.shape[-1]).astype(jnp.bfloat16)


def gradient(left_rows, picked, pairs, tile_width):
    batch = left_rows.shape[0]
    length = left_rows.shape[1]
    width = left_rows.shape[2]
    left = left_rows.reshape(batch, length // TILE, TILE, width)
    block_grad = jnp.einsum("rtok,rtpqk->rtopq", left, picked, preferred_element_type=jnp.float32)
    return block_grad.reshape(batch, length, pairs, tile_width).astype(jnp.bfloat16)


def per_device(env_right, transfer, sources, env_left):
    ncol = lax.axis_size("col")
    col_index = lax.axis_index("col")
    sec_index = lax.axis_index("sec")
    rows = transfer.shape[1]
    length = transfer.shape[2]
    pairs = transfer.shape[3]
    tile_width = transfer.shape[4]
    tiles_here = length // TILE
    width = env_right.shape[2]
    is_last = col_index == ncol - 1
    block_rows = transfer[0]
    local_sources = sources[0] - sec_index * tiles_here + REACH
    picked_shape = (rows, tiles_here, pairs, TILE, width)

    def step(turn, carry):
        state, picked = carry
        received = passed_along(state, "col", -1)
        received = jnp.where(is_last, env_right, received)
        haloed = padded(received, (("sec", 1),), REACH * TILE)
        picked = pick_blocks(haloed, local_sources)
        return (advance(block_rows, picked), picked)

    start_state = jnp.zeros_like(env_right)
    start_picked = jnp.zeros(picked_shape, jnp.bfloat16)
    env_final, picked_final = lax.fori_loop(0, ncol, step, (start_state, start_picked))
    grad = gradient(env_left[0], picked_final, pairs, tile_width)
    return (env_final[None], grad[None])


def solution(mesh):
    placed = (
        P(None, "sec", None),
        P("col", None, "sec", None, None),
        P("col", None, "sec", None),
        P("col", None, "sec", None),
    )
    return jax.shard_map(
        per_device,
        mesh=mesh,
        in_specs=placed,
        out_specs=(P("col", None, "sec", None), P("col", None, "sec", None, None)),
        check_vma=False,
    )
```

profile of v0, /device:TPU:3, one launch (start us, length us, event | category | flops | bytes accessed | tf_op | source)
XLA Modules:
  0.0 283.6 jit_solution(12776081925725023060)
XLA Ops:
  2.7 256.3 %while.12 = (s32[]{:T(128)}, bf16[1,4096,128]{2,1,0:T(8,128)(2,1)S(1)}, bf16[1,32,4,128,128]{4,3,2,1,0:T(8,128)(2,1)}, pred[]{:T(512)}, bf16[1,4096,128]{2,1,0:T...) while((s32[]{:T(128)}, bf16[1,4096,128]{2,1,0:T(8,128)(2,1)S(1)}, ...), condition=%wide.region_1.2_spmd, body=%wide.region_0.1_spmd.sunk | while | flops 541459456 | bytes 28318924 | solution.py:83
  2.7 2.6 collective-permute-start
  5.3 13.6 %collective-permute-done = bf16[1,4096,128]{2,1,0:T(8,128)(2,1)S(1)} collective-permute-done((bf16[1,4096,128]{2,1,0:T(8,128)(2,1)S(1)}, bf16[1,4096,128]{2,1,0:T(8,128)(2,1)S(1)}, u32[]{:S(2)}, u32[]{:S(2)}) %collective-permute-start) | collective-permute-done | bytes 1048608 | tf_op jit(solution)/shard_map/while/body/eval_jaxpr/ppermute | solution.py:13
  19.1 2.2 collective-permute-start.1
  21.3 4.0 %collective-permute-start.2 = (bf16[1,256,128]{2,1,0:T(8,128)(2,1)S(1)}, bf16[1,256,128]{2,1,0:T(8,128)(2,1)S(1)}, u32[]{:S(2)}, u32[]{:S(2)}) collective-permute-start(bf16[1,256,128]{2,1,0:T(8,128)(2,1)S(1)} %get-tuple-element.103), channel_id=1, source_target_pairs={{0,1},{1,2},{2,3},{4,5},{5,6},{6,7},{8,9},{9,10},{10,11},{12,13},{... | collective-permute-start | bytes 196616 | tf_op jit(solution)/shard_map/while/body/eval_jaxpr/ppermute | solution.py:23
  26.7 3.1 %gather_fusion = bf16[128,128,128]{2,1,0:T(8,128)(2,1)} fusion(bf16[1,36,128,128]{3,2,1,0:T(8,128)(2,1)S(1)} %bitcast.53, s32[128]{0:T(128)S(1)} %reshape.129), kind=kCustom, calls=%fused_computation.clone.1 | custom fusion | bytes 8389632 | tf_op jit(solution)/shard_map/while/body/eval_jaxpr/vmap()/gather | solution.py:35
  29.8 4.7 %bitcast_convert_fusion.2 = bf16[32,128,128]{1,2,0:T(8,128)(2,1)S(1)} fusion(bf16[32,4,128,128]{3,2,1,0:T(8,128)(2,1)} %bitcast.55, bf16[32,128,4,128]{3,2,1,0:T(4,128)(2,1)} %bitcast.59), kind=kOutput, calls=%fused_computation.3.clone.1 | convolution fusion | flops 537395200 | bytes 9437184 | tf_op jit(solution)/shard_map/while/body/eval_jaxpr/rtopq,rtpqk->rtok/dot_general | solution.py:45
  34.6 1.9 collective-permute-start
  36.5 14.2 %collective-permute-done = bf16[1,4096,128]{2,1,0:T(8,128)(2,1)S(1)} collective-permute-done((bf16[1,4096,128]{2,1,0:T(8,128)(2,1)S(1)}, bf16[1,4096,128]{2,1,0:T(8,128)(2,1)S(1)}, u32[]{:S(2)}, u32[]{:S(2)}) %collective-permute-start) | collective-permute-done | bytes 1048608 | tf_op jit(solution)/shard_map/while/body/eval_jaxpr/ppermute | solution.py:13
  50.9 1.9 collective-permute-start.1
  52.8 4.6 %collective-permute-start.2 = (bf16[1,256,128]{2,1,0:T(8,128)(2,1)S(1)}, bf16[1,256,128]{2,1,0:T(8,128)(2,1)S(1)}, u32[]{:S(2)}, u32[]{:S(2)}) collective-permute-start(bf16[1,256,128]{2,1,0:T(8,128)(2,1)S(1)} %get-tuple-element.103), channel_id=1, source_target_pairs={{0,1},{1,2},{2,3},{4,5},{5,6},{6,7},{8,9},{9,10},{10,11},{12,13},{... | collective-permute-start | bytes 196616 | tf_op jit(solution)/shard_map/while/body/eval_jaxpr/ppermute | solution.py:23
  58.8 3.1 %gather_fusion = bf16[128,128,128]{2,1,0:T(8,128)(2,1)} fusion(bf16[1,36,128,128]{3,2,1,0:T(8,128)(2,1)S(1)} %bitcast.53, s32[128]{0:T(128)S(1)} %reshape.129), kind=kCustom, calls=%fused_computation.clone.1 | custom fusion | bytes 8389632 | tf_op jit(solution)/shard_map/while/body/eval_jaxpr/vmap()/gather | solution.py:35
  61.9 4.7 %bitcast_convert_fusion.2 = bf16[32,128,128]{1,2,0:T(8,128)(2,1)S(1)} fusion(bf16[32,4,128,128]{3,2,1,0:T(8,128)(2,1)} %bitcast.55, bf16[32,128,4,128]{3,2,1,0:T(4,128)(2,1)} %bitcast.59), kind=kOutput, calls=%fused_computation.3.clone.1 | convolution fusion | flops 537395200 | bytes 9437184 | tf_op jit(solution)/shard_map/while/body/eval_jaxpr/rtopq,rtpqk->rtok/dot_general | solution.py:45
  66.6 1.9 collective-permute-start
  68.6 14.2 %collective-permute-done = bf16[1,4096,128]{2,1,0:T(8,128)(2,1)S(1)} collective-permute-done((bf16[1,4096,128]{2,1,0:T(8,128)(2,1)S(1)}, bf16[1,4096,128]{2,1,0:T(8,128)(2,1)S(1)}, u32[]{:S(2)}, u32[]{:S(2)}) %collective-permute-start) | collective-permute-done | bytes 1048608 | tf_op jit(solution)/shard_map/while/body/eval_jaxpr/ppermute | solution.py:13
  82.9 1.9 collective-permute-start.1
  84.9 4.6 %collective-permute-start.2 = (bf16[1,256,128]{2,1,0:T(8,128)(2,1)S(1)}, bf16[1,256,128]{2,1,0:T(8,128)(2,1)S(1)}, u32[]{:S(2)}, u32[]{:S(2)}) collective-permute-start(bf16[1,256,128]{2,1,0:T(8,128)(2,1)S(1)} %get-tuple-element.103), channel_id=1, source_target_pairs={{0,1},{1,2},{2,3},{4,5},{5,6},{6,7},{8,9},{9,10},{10,11},{12,13},{... | collective-permute-start | bytes 196616 | tf_op jit(solution)/shard_map/while/body/eval_jaxpr/ppermute | solution.py:23
  90.8 3.1 %gather_fusion = bf16[128,128,128]{2,1,0:T(8,128)(2,1)} fusion(bf16[1,36,128,128]{3,2,1,0:T(8,128)(2,1)S(1)} %bitcast.53, s32[128]{0:T(128)S(1)} %reshape.129), kind=kCustom, calls=%fused_computation.clone.1 | custom fusion | bytes 8389632 | tf_op jit(solution)/shard_map/while/body/eval_jaxpr/vmap()/gather | solution.py:35
  94.0 4.7 %bitcast_convert_fusion.2 = bf16[32,128,128]{1,2,0:T(8,128)(2,1)S(1)} fusion(bf16[32,4,128,128]{3,2,1,0:T(8,128)(2,1)} %bitcast.55, bf16[32,128,4,128]{3,2,1,0:T(4,128)(2,1)} %bitcast.59), kind=kOutput, calls=%fused_computation.3.clone.1 | convolution fusion | flops 537395200 | bytes 9437184 | tf_op jit(solution)/shard_map/while/body/eval_jaxpr/rtopq,rtpqk->rtok/dot_general | solution.py:45
  98.7 1.9 collective-permute-start
  100.6 14.2 %collective-permute-done = bf16[1,4096,128]{2,1,0:T(8,128)(2,1)S(1)} collective-permute-done((bf16[1,4096,128]{2,1,0:T(8,128)(2,1)S(1)}, bf16[1,4096,128]{2,1,0:T(8,128)(2,1)S(1)}, u32[]{:S(2)}, u32[]{:S(2)}) %collective-permute-start) | collective-permute-done | bytes 1048608 | tf_op jit(solution)/shard_map/while/body/eval_jaxpr/ppermute | solution.py:13
  115.0 1.9 collective-permute-start.1
  116.9 4.6 %collective-permute-start.2 = (bf16[1,256,128]{2,1,0:T(8,128)(2,1)S(1)}, bf16[1,256,128]{2,1,0:T(8,128)(2,1)S(1)}, u32[]{:S(2)}, u32[]{:S(2)}) collective-permute-start(bf16[1,256,128]{2,1,0:T(8,128)(2,1)S(1)} %get-tuple-element.103), channel_id=1, source_target_pairs={{0,1},{1,2},{2,3},{4,5},{5,6},{6,7},{8,9},{9,10},{10,11},{12,13},{... | collective-permute-start | bytes 196616 | tf_op jit(solution)/shard_map/while/body/eval_jaxpr/ppermute | solution.py:23
  122.9 3.1 %gather_fusion = bf16[128,128,128]{2,1,0:T(8,128)(2,1)} fusion(bf16[1,36,128,128]{3,2,1,0:T(8,128)(2,1)S(1)} %bitcast.53, s32[128]{0:T(128)S(1)} %reshape.129), kind=kCustom, calls=%fused_computation.clone.1 | custom fusion | bytes 8389632 | tf_op jit(solution)/shard_map/while/body/eval_jaxpr/vmap()/gather | solution.py:35
  126.0 4.7 %bitcast_convert_fusion.2 = bf16[32,128,128]{1,2,0:T(8,128)(2,1)S(1)} fusion(bf16[32,4,128,128]{3,2,1,0:T(8,128)(2,1)} %bitcast.55, bf16[32,128,4,128]{3,2,1,0:T(4,128)(2,1)} %bitcast.59), kind=kOutput, calls=%fused_computation.3.clone.1 | convolution fusion | flops 537395200 | bytes 9437184 | tf_op jit(solution)/shard_map/while/body/eval_jaxpr/rtopq,rtpqk->rtok/dot_general | solution.py:45
  130.7 1.9 collective-permute-start
  132.7 14.2 %collective-permute-done = bf16[1,4096,128]{2,1,0:T(8,128)(2,1)S(1)} collective-permute-done((bf16[1,4096,128]{2,1,0:T(8,128)(2,1)S(1)}, bf16[1,4096,128]{2,1,0:T(8,128)(2,1)S(1)}, u32[]{:S(2)}, u32[]{:S(2)}) %collective-permute-start) | collective-permute-done | bytes 1048608 | tf_op jit(solution)/shard_map/while/body/eval_jaxpr/ppermute | solution.py:13
  147.1 1.9 collective-permute-start.1
  149.0 4.6 %collective-permute-start.2 = (bf16[1,256,128]{2,1,0:T(8,128)(2,1)S(1)}, bf16[1,256,128]{2,1,0:T(8,128)(2,1)S(1)}, u32[]{:S(2)}, u32[]{:S(2)}) collective-permute-start(bf16[1,256,128]{2,1,0:T(8,128)(2,1)S(1)} %get-tuple-element.103), channel_id=1, source_target_pairs={{0,1},{1,2},{2,3},{4,5},{5,6},{6,7},{8,9},{9,10},{10,11},{12,13},{... | collective-permute-start | bytes 196616 | tf_op jit(solution)/shard_map/while/body/eval_jaxpr/ppermute | solution.py:23
  155.0 3.1 %gather_fusion = bf16[128,128,128]{2,1,0:T(8,128)(2,1)} fusion(bf16[1,36,128,128]{3,2,1,0:T(8,128)(2,1)S(1)} %bitcast.53, s32[128]{0:T(128)S(1)} %reshape.129), kind=kCustom, calls=%fused_computation.clone.1 | custom fusion | bytes 8389632 | tf_op jit(solution)/shard_map/while/body/eval_jaxpr/vmap()/gather | solution.py:35
  158.1 4.7 %bitcast_convert_fusion.2 = bf16[32,128,128]{1,2,0:T(8,128)(2,1)S(1)} fusion(bf16[32,4,128,128]{3,2,1,0:T(8,128)(2,1)} %bitcast.55, bf16[32,128,4,128]{3,2,1,0:T(4,128)(2,1)} %bitcast.59), kind=kOutput, calls=%fused_computation.3.clone.1 | convolution fusion | flops 537395200 | bytes 9437184 | tf_op jit(solution)/shard_map/while/body/eval_jaxpr/rtopq,rtpqk->rtok/dot_general | solution.py:45
  162.8 1.9 collective-permute-start
  164.8 14.2 %collective-permute-done = bf16[1,4096,128]{2,1,0:T(8,128)(2,1)S(1)} collective-permute-done((bf16[1,4096,128]{2,1,0:T(8,128)(2,1)S(1)}, bf16[1,4096,128]{2,1,0:T(8,128)(2,1)S(1)}, u32[]{:S(2)}, u32[]{:S(2)}) %collective-permute-start) | collective-permute-done | bytes 1048608 | tf_op jit(solution)/shard_map/while/body/eval_jaxpr/ppermute | solution.py:13
  179.1 1.9 collective-permute-start.1
  181.0 4.6 %collective-permute-start.2 = (bf16[1,256,128]{2,1,0:T(8,128)(2,1)S(1)}, bf16[1,256,128]{2,1,0:T(8,128)(2,1)S(1)}, u32[]{:S(2)}, u32[]{:S(2)}) collective-permute-start(bf16[1,256,128]{2,1,0:T(8,128)(2,1)S(1)} %get-tuple-element.103), channel_id=1, source_target_pairs={{0,1},{1,2},{2,3},{4,5},{5,6},{6,7},{8,9},{9,10},{10,11},{12,13},{... | collective-permute-start | bytes 196616 | tf_op jit(solution)/shard_map/while/body/eval_jaxpr/ppermute | solution.py:23
  187.0 3.1 %gather_fusion = bf16[128,128,128]{2,1,0:T(8,128)(2,1)} fusion(bf16[1,36,128,128]{3,2,1,0:T(8,128)(2,1)S(1)} %bitcast.53, s32[128]{0:T(128)S(1)} %reshape.129), kind=kCustom, calls=%fused_computation.clone.1 | custom fusion | bytes 8389632 | tf_op jit(solution)/shard_map/while/body/eval_jaxpr/vmap()/gather | solution.py:35
  190.1 4.7 %bitcast_convert_fusion.2 = bf16[32,128,128]{1,2,0:T(8,128)(2,1)S(1)} fusion(bf16[32,4,128,128]{3,2,1,0:T(8,128)(2,1)} %bitcast.55, bf16[32,128,4,128]{3,2,1,0:T(4,128)(2,1)} %bitcast.59), kind=kOutput, calls=%fused_computation.3.clone.1 | convolution fusion | flops 537395200 | bytes 9437184 | tf_op jit(solution)/shard_map/while/body/eval_jaxpr/rtopq,rtpqk->rtok/dot_general | solution.py:45
  196.8 14.2 %collective-permute-done = bf16[1,4096,128]{2,1,0:T(8,128)(2,1)S(1)} collective-permute-done((bf16[1,4096,128]{2,1,0:T(8,128)(2,1)S(1)}, bf16[1,4096,128]{2,1,0:T(8,128)(2,1)S(1)}, u32[]{:S(2)}, u32[]{:S(2)}) %collective-permute-start) | collective-permute-done | bytes 1048608 | tf_op jit(solution)/shard_map/while/body/eval_jaxpr/ppermute | solution.py:13
  213.1 4.6 %collective-permute-start.2 = (bf16[1,256,128]{2,1,0:T(8,128)(2,1)S(1)}, bf16[1,256,128]{2,1,0:T(8,128)(2,1)S(1)}, u32[]{:S(2)}, u32[]{:S(2)}) collective-permute-start(bf16[1,256,128]{2,1,0:T(8,128)(2,1)S(1)} %get-tuple-element.103), channel_id=1, source_target_pairs={{0,1},{1,2},{2,3},{4,5},{5,6},{6,7},{8,9},{9,10},{10,11},{12,13},{... | collective-permute-start | bytes 196616 | tf_op jit(solution)/shard_map/while/body/eval_jaxpr/ppermute | solution.py:23
  219.1 3.1 %gather_fusion = bf16[128,128,128]{2,1,0:T(8,128)(2,1)} fusion(bf16[1,36,128,128]{3,2,1,0:T(8,128)(2,1)S(1)} %bitcast.53, s32[128]{0:T(128)S(1)} %reshape.129), kind=kCustom, calls=%fused_computation.clone.1 | custom fusion | bytes 8389632 | tf_op jit(solution)/shard_map/while/body/eval_jaxpr/vmap()/gather | solution.py:35
  222.2 4.7 %bitcast_convert_fusion.2 = bf16[32,128,128]{1,2,0:T(8,128)(2,1)S(1)} fusion(bf16[32,4,128,128]{3,2,1,0:T(8,128)(2,1)} %bitcast.55, bf16[32,128,4,128]{3,2,1,0:T(4,128)(2,1)} %bitcast.59), kind=kOutput, calls=%fused_computation.3.clone.1 | convolution fusion | flops 537395200 | bytes 9437184 | tf_op jit(solution)/shard_map/while/body/eval_jaxpr/rtopq,rtpqk->rtok/dot_general | solution.py:45
  228.9 14.2 %collective-permute-done = bf16[1,4096,128]{2,1,0:T(8,128)(2,1)S(1)} collective-permute-done((bf16[1,4096,128]{2,1,0:T(8,128)(2,1)S(1)}, bf16[1,4096,128]{2,1,0:T(8,128)(2,1)S(1)}, u32[]{:S(2)}, u32[]{:S(2)}) %collective-permute-start) | collective-permute-done | bytes 1048608 | tf_op jit(solution)/shard_map/while/body/eval_jaxpr/ppermute | solution.py:13
  243.2 1.9 collective-permute-start.1
  245.2 4.6 %collective-permute-start.2 = (bf16[1,256,128]{2,1,0:T(8,128)(2,1)S(1)}, bf16[1,256,128]{2,1,0:T(8,128)(2,1)S(1)}, u32[]{:S(2)}, u32[]{:S(2)}) collective-permute-start(bf16[1,256,128]{2,1,0:T(8,128)(2,1)S(1)} %get-tuple-element.103), channel_id=1, source_target_pairs={{0,1},{1,2},{2,3},{4,5},{5,6},{6,7},{8,9},{9,10},{10,11},{12,13},{... | collective-permute-start | bytes 196616 | tf_op jit(solution)/shard_map/while/body/eval_jaxpr/ppermute | solution.py:23
  251.2 3.1 %gather_fusion = bf16[128,128,128]{2,1,0:T(8,128)(2,1)} fusion(bf16[1,36,128,128]{3,2,1,0:T(8,128)(2,1)S(1)} %bitcast.53, s32[128]{0:T(128)S(1)} %reshape.129), kind=kCustom, calls=%fused_computation.clone.1 | custom fusion | bytes 8389632 | tf_op jit(solution)/shard_map/while/body/eval_jaxpr/vmap()/gather | solution.py:35
  254.3 4.7 %bitcast_convert_fusion.2 = bf16[32,128,128]{1,2,0:T(8,128)(2,1)S(1)} fusion(bf16[32,4,128,128]{3,2,1,0:T(8,128)(2,1)} %bitcast.55, bf16[32,128,4,128]{3,2,1,0:T(4,128)(2,1)} %bitcast.59), kind=kOutput, calls=%fused_computation.3.clone.1 | convolution fusion | flops 537395200 | bytes 9437184 | tf_op jit(solution)/shard_map/while/body/eval_jaxpr/rtopq,rtpqk->rtok/dot_general | solution.py:45
  259.0 3.8 %convert_bitcast_fusion = bf16[32,128,4,128]{3,1,2,0:T(8,128)(2,1)S(1)} fusion(bf16[32,128,128,1]{2,1,3,0:T(8,128)(2,1)S(1)} %bitcast.52, bf16[1,32,4,128,128]{4,3,2,1,0:T(8,128)(2,1)} %get-tuple-element.40), kind=kOutput, calls=%fused_computation.15 | convolution fusion | flops 538968064 | bytes 9437184 | tf_op jit(solution)/shard_map/rtok,rtpqk->rtopq/dot_general | solution.py:54
  263.2 20.4 %copy.11 = bf16[1,1,4096,4,128]{4,3,2,1,0:T(4,128)(2,1)} copy(bf16[1,1,4096,4,128]{4,2,3,1,0:T(8,128)(2,1)S(1)} %bitcast.54) | data formatting | bytes 8388608
  (91 shorter events, 20.6 us)
Async XLA Ops:
  0.6 1.2 copy-start
  2.7 16.2 %collective-permute-start = (bf16[1,4096,128]{2,1,0:T(8,128)(2,1)S(1)}, bf16[1,4096,128]{2,1,0:T(8,128)(2,1)S(1)}, u32[]{:S(2)}, u32[]{:S(2)}) collective-permute-start(bf16[1,4096,128]{2,1,0:T(8,128)(2,1)S(1)} %get-tuple-element.113), channel_id=1, source_target_pairs={{4,0},{8,4},{12,8},{16,12},{20,16},{24,20},{28,24},{5,1},{9,5},{13... | collective-permute-start | bytes 3145736 | tf_op jit(solution)/shard_map/while/body/eval_jaxpr/ppermute | solution.py:13
  19.1 6.4 %collective-permute-start.1 = (bf16[1,256,128]{2,1,0:T(8,128)(2,1)S(1)}, bf16[1,256,128]{2,1,0:T(8,128)(2,1)S(1)}, u32[]{:S(2)}, u32[]{:S(2)}) collective-permute-start(bf16[1,256,128]{2,1,0:T(8,128)(2,1)S(1)} %get-tuple-element.102), channel_id=1, source_target_pairs={{1,0},{2,1},{3,2},{5,4},{6,5},{7,6},{9,8},{10,9},{11,10},{13,12},{... | collective-permute-start | bytes 196616 | tf_op jit(solution)/shard_map/while/body/eval_jaxpr/ppermute | solution.py:24
  21.3 5.3 %collective-permute-start.2 = (bf16[1,256,128]{2,1,0:T(8,128)(2,1)S(1)}, bf16[1,256,128]{2,1,0:T(8,128)(2,1)S(1)}, u32[]{:S(2)}, u32[]{:S(2)}) collective-permute-start(bf16[1,256,128]{2,1,0:T(8,128)(2,1)S(1)} %get-tuple-element.103), channel_id=1, source_target_pairs={{0,1},{1,2},{2,3},{4,5},{5,6},{6,7},{8,9},{9,10},{10,11},{12,13},{... | collective-permute-start | bytes 196616 | tf_op jit(solution)/shard_map/while/body/eval_jaxpr/ppermute | solution.py:23
  34.6 16.1 %collective-permute-start = (bf16[1,4096,128]{2,1,0:T(8,128)(2,1)S(1)}, bf16[1,4096,128]{2,1,0:T(8,128)(2,1)S(1)}, u32[]{:S(2)}, u32[]{:S(2)}) collective-permute-start(bf16[1,4096,128]{2,1,0:T(8,128)(2,1)S(1)} %get-tuple-element.113), channel_id=1, source_target_pairs={{4,0},{8,4},{12,8},{16,12},{20,16},{24,20},{28,24},{5,1},{9,5},{13... | collective-permute-start | bytes 3145736 | tf_op jit(solution)/shard_map/while/body/eval_jaxpr/ppermute | solution.py:13
  50.9 6.7 %collective-permute-start.1 = (bf16[1,256,128]{2,1,0:T(8,128)(2,1)S(1)}, bf16[1,256,128]{2,1,0:T(8,128)(2,1)S(1)}, u32[]{:S(2)}, u32[]{:S(2)}) collective-permute-start(bf16[1,256,128]{2,1,0:T(8,128)(2,1)S(1)} %get-tuple-element.102), channel_id=1, source_target_pairs={{1,0},{2,1},{3,2},{5,4},{6,5},{7,6},{9,8},{10,9},{11,10},{13,12},{... | collective-permute-start | bytes 196616 | tf_op jit(solution)/shard_map/while/body/eval_jaxpr/ppermute | solution.py:24
  52.8 5.9 %collective-permute-start.2 = (bf16[1,256,128]{2,1,0:T(8,128)(2,1)S(1)}, bf16[1,256,128]{2,1,0:T(8,128)(2,1)S(1)}, u32[]{:S(2)}, u32[]{:S(2)}) collective-permute-start(bf16[1,256,128]{2,1,0:T(8,128)(2,1)S(1)} %get-tuple-element.103), channel_id=1, source_target_pairs={{0,1},{1,2},{2,3},{4,5},{5,6},{6,7},{8,9},{9,10},{10,11},{12,13},{... | collective-permute-start | bytes 196616 | tf_op jit(solution)/shard_map/while/body/eval_jaxpr/ppermute | solution.py:23
  66.6 16.1 %collective-permute-start = (bf16[1,4096,128]{2,1,0:T(8,128)(2,1)S(1)}, bf16[1,4096,128]{2,1,0:T(8,128)(2,1)S(1)}, u32[]{:S(2)}, u32[]{:S(2)}) collective-permute-start(bf16[1,4096,128]{2,1,0:T(8,128)(2,1)S(1)} %get-tuple-element.113), channel_id=1, source_target_pairs={{4,0},{8,4},{12,8},{16,12},{20,16},{24,20},{28,24},{5,1},{9,5},{13... | collective-permute-start | bytes 3145736 | tf_op jit(solution)/shard_map/while/body/eval_jaxpr/ppermute | solution.py:13
  82.9 6.7 %collective-permute-start.1 = (bf16[1,256,128]{2,1,0:T(8,128)(2,1)S(1)}, bf16[1,256,128]{2,1,0:T(8,128)(2,1)S(1)}, u32[]{:S(2)}, u32[]{:S(2)}) collective-permute-start(bf16[1,256,128]{2,1,0:T(8,128)(2,1)S(1)} %get-tuple-element.102), channel_id=1, source_target_pairs={{1,0},{2,1},{3,2},{5,4},{6,5},{7,6},{9,8},{10,9},{11,10},{13,12},{... | collective-permute-start | bytes 196616 | tf_op jit(solution)/shard_map/while/body/eval_jaxpr/ppermute | solution.py:24
  84.9 5.9 %collective-permute-start.2 = (bf16[1,256,128]{2,1,0:T(8,128)(2,1)S(1)}, bf16[1,256,128]{2,1,0:T(8,128)(2,1)S(1)}, u32[]{:S(2)}, u32[]{:S(2)}) collective-permute-start(bf16[1,256,128]{2,1,0:T(8,128)(2,1)S(1)} %get-tuple-element.103), channel_id=1, source_target_pairs={{0,1},{1,2},{2,3},{4,5},{5,6},{6,7},{8,9},{9,10},{10,11},{12,13},{... | collective-permute-start | bytes 196616 | tf_op jit(solution)/shard_map/while/body/eval_jaxpr/ppermute | solution.py:23
  98.7 16.1 %collective-permute-start = (bf16[1,4096,128]{2,1,0:T(8,128)(2,1)S(1)}, bf16[1,4096,128]{2,1,0:T(8,128)(2,1)S(1)}, u32[]{:S(2)}, u32[]{:S(2)}) collective-permute-start(bf16[1,4096,128]{2,1,0:T(8,128)(2,1)S(1)} %get-tuple-element.113), channel_id=1, source_target_pairs={{4,0},{8,4},{12,8},{16,12},{20,16},{24,20},{28,24},{5,1},{9,5},{13... | collective-permute-start | bytes 3145736 | tf_op jit(solution)/shard_map/while/body/eval_jaxpr/ppermute | solution.py:13
  115.0 6.7 %collective-permute-start.1 = (bf16[1,256,128]{2,1,0:T(8,128)(2,1)S(1)}, bf16[1,256,128]{2,1,0:T(8,128)(2,1)S(1)}, u32[]{:S(2)}, u32[]{:S(2)}) collective-permute-start(bf16[1,256,128]{2,1,0:T(8,128)(2,1)S(1)} %get-tuple-element.102), channel_id=1, source_target_pairs={{1,0},{2,1},{3,2},{5,4},{6,5},{7,6},{9,8},{10,9},{11,10},{13,12},{... | collective-permute-start | bytes 196616 | tf_op jit(solution)/shard_map/while/body/eval_jaxpr/ppermute | solution.py:24
  116.9 5.9 %collective-permute-start.2 = (bf16[1,256,128]{2,1,0:T(8,128)(2,1)S(1)}, bf16[1,256,128]{2,1,0:T(8,128)(2,1)S(1)}, u32[]{:S(2)}, u32[]{:S(2)}) collective-permute-start(bf16[1,256,128]{2,1,0:T(8,128)(2,1)S(1)} %get-tuple-element.103), channel_id=1, source_target_pairs={{0,1},{1,2},{2,3},{4,5},{5,6},{6,7},{8,9},{9,10},{10,11},{12,13},{... | collective-permute-start | bytes 196616 | tf_op jit(solution)/shard_map/while/body/eval_jaxpr/ppermute | solution.py:23
  130.7 16.1 %collective-permute-start = (bf16[1,4096,128]{2,1,0:T(8,128)(2,1)S(1)}, bf16[1,4096,128]{2,1,0:T(8,128)(2,1)S(1)}, u32[]{:S(2)}, u32[]{:S(2)}) collective-permute-start(bf16[1,4096,128]{2,1,0:T(8,128)(2,1)S(1)} %get-tuple-element.113), channel_id=1, source_target_pairs={{4,0},{8,4},{12,8},{16,12},{20,16},{24,20},{28,24},{5,1},{9,5},{13... | collective-permute-start | bytes 3145736 | tf_op jit(solution)/shard_map/while/body/eval_jaxpr/ppermute | solution.py:13
  147.1 6.7 %collective-permute-start.1 = (bf16[1,256,128]{2,1,0:T(8,128)(2,1)S(1)}, bf16[1,256,128]{2,1,0:T(8,128)(2,1)S(1)}, u32[]{:S(2)}, u32[]{:S(2)}) collective-permute-start(bf16[1,256,128]{2,1,0:T(8,128)(2,1)S(1)} %get-tuple-element.102), channel_id=1, source_target_pairs={{1,0},{2,1},{3,2},{5,4},{6,5},{7,6},{9,8},{10,9},{11,10},{13,12},{... | collective-permute-start | bytes 196616 | tf_op jit(solution)/shard_map/while/body/eval_jaxpr/ppermute | solution.py:24
  149.0 5.9 %collective-permute-start.2 = (bf16[1,256,128]{2,1,0:T(8,128)(2,1)S(1)}, bf16[1,256,128]{2,1,0:T(8,128)(2,1)S(1)}, u32[]{:S(2)}, u32[]{:S(2)}) collective-permute-start(bf16[1,256,128]{2,1,0:T(8,128)(2,1)S(1)} %get-tuple-element.103), channel_id=1, source_target_pairs={{0,1},{1,2},{2,3},{4,5},{5,6},{6,7},{8,9},{9,10},{10,11},{12,13},{... | collective-permute-start | bytes 196616 | tf_op jit(solution)/shard_map/while/body/eval_jaxpr/ppermute | solution.py:23
  162.8 16.1 %collective-permute-start = (bf16[1,4096,128]{2,1,0:T(8,128)(2,1)S(1)}, bf16[1,4096,128]{2,1,0:T(8,128)(2,1)S(1)}, u32[]{:S(2)}, u32[]{:S(2)}) collective-permute-start(bf16[1,4096,128]{2,1,0:T(8,128)(2,1)S(1)} %get-tuple-element.113), channel_id=1, source_target_pairs={{4,0},{8,4},{12,8},{16,12},{20,16},{24,20},{28,24},{5,1},{9,5},{13... | collective-permute-start | bytes 3145736 | tf_op jit(solution)/shard_map/while/body/eval_jaxpr/ppermute | solution.py:13
  179.1 6.7 %collective-permute-start.1 = (bf16[1,256,128]{2,1,0:T(8,128)(2,1)S(1)}, bf16[1,256,128]{2,1,0:T(8,128)(2,1)S(1)}, u32[]{:S(2)}, u32[]{:S(2)}) collective-permute-start(bf16[1,256,128]{2,1,0:T(8,128)(2,1)S(1)} %get-tuple-element.102), channel_id=1, source_target_pairs={{1,0},{2,1},{3,2},{5,4},{6,5},{7,6},{9,8},{10,9},{11,10},{13,12},{... | collective-permute-start | bytes 196616 | tf_op jit(solution)/shard_map/while/body/eval_jaxpr/ppermute | solution.py:24
  181.0 5.9 %collective-permute-start.2 = (bf16[1,256,128]{2,1,0:T(8,128)(2,1)S(1)}, bf16[1,256,128]{2,1,0:T(8,128)(2,1)S(1)}, u32[]{:S(2)}, u32[]{:S(2)}) collective-permute-start(bf16[1,256,128]{2,1,0:T(8,128)(2,1)S(1)} %get-tuple-element.103), channel_id=1, source_target_pairs={{0,1},{1,2},{2,3},{4,5},{5,6},{6,7},{8,9},{9,10},{10,11},{12,13},{... | collective-permute-start | bytes 196616 | tf_op jit(solution)/shard_map/while/body/eval_jaxpr/ppermute | solution.py:23
  194.9 16.1 %collective-permute-start = (bf16[1,4096,128]{2,1,0:T(8,128)(2,1)S(1)}, bf16[1,4096,128]{2,1,0:T(8,128)(2,1)S(1)}, u32[]{:S(2)}, u32[]{:S(2)}) collective-permute-start(bf16[1,4096,128]{2,1,0:T(8,128)(2,1)S(1)} %get-tuple-element.113), channel_id=1, source_target_pairs={{4,0},{8,4},{12,8},{16,12},{20,16},{24,20},{28,24},{5,1},{9,5},{13... | collective-permute-start | bytes 3145736 | tf_op jit(solution)/shard_map/while/body/eval_jaxpr/ppermute | solution.py:13
  211.2 6.7 %collective-permute-start.1 = (bf16[1,256,128]{2,1,0:T(8,128)(2,1)S(1)}, bf16[1,256,128]{2,1,0:T(8,128)(2,1)S(1)}, u32[]{:S(2)}, u32[]{:S(2)}) collective-permute-start(bf16[1,256,128]{2,1,0:T(8,128)(2,1)S(1)} %get-tuple-element.102), channel_id=1, source_target_pairs={{1,0},{2,1},{3,2},{5,4},{6,5},{7,6},{9,8},{10,9},{11,10},{13,12},{... | collective-permute-start | bytes 196616 | tf_op jit(solution)/shard_map/while/body/eval_jaxpr/ppermute | solution.py:24
  213.1 5.9 %collective-permute-start.2 = (bf16[1,256,128]{2,1,0:T(8,128)(2,1)S(1)}, bf16[1,256,128]{2,1,0:T(8,128)(2,1)S(1)}, u32[]{:S(2)}, u32[]{:S(2)}) collective-permute-start(bf16[1,256,128]{2,1,0:T(8,128)(2,1)S(1)} %get-tuple-element.103), channel_id=1, source_target_pairs={{0,1},{1,2},{2,3},{4,5},{5,6},{6,7},{8,9},{9,10},{10,11},{12,13},{... | collective-permute-start | bytes 196616 | tf_op jit(solution)/shard_map/while/body/eval_jaxpr/ppermute | solution.py:23
  226.9 16.1 %collective-permute-start = (bf16[1,4096,128]{2,1,0:T(8,128)(2,1)S(1)}, bf16[1,4096,128]{2,1,0:T(8,128)(2,1)S(1)}, u32[]{:S(2)}, u32[]{:S(2)}) collective-permute-start(bf16[1,4096,128]{2,1,0:T(8,128)(2,1)S(1)} %get-tuple-element.113), channel_id=1, source_target_pairs={{4,0},{8,4},{12,8},{16,12},{20,16},{24,20},{28,24},{5,1},{9,5},{13... | collective-permute-start | bytes 3145736 | tf_op jit(solution)/shard_map/while/body/eval_jaxpr/ppermute | solution.py:13
  243.2 6.7 %collective-permute-start.1 = (bf16[1,256,128]{2,1,0:T(8,128)(2,1)S(1)}, bf16[1,256,128]{2,1,0:T(8,128)(2,1)S(1)}, u32[]{:S(2)}, u32[]{:S(2)}) collective-permute-start(bf16[1,256,128]{2,1,0:T(8,128)(2,1)S(1)} %get-tuple-element.102), channel_id=1, source_target_pairs={{1,0},{2,1},{3,2},{5,4},{6,5},{7,6},{9,8},{10,9},{11,10},{13,12},{... | collective-permute-start | bytes 196616 | tf_op jit(solution)/shard_map/while/body/eval_jaxpr/ppermute | solution.py:24
  245.2 5.9 %collective-permute-start.2 = (bf16[1,256,128]{2,1,0:T(8,128)(2,1)S(1)}, bf16[1,256,128]{2,1,0:T(8,128)(2,1)S(1)}, u32[]{:S(2)}, u32[]{:S(2)}) collective-permute-start(bf16[1,256,128]{2,1,0:T(8,128)(2,1)S(1)} %get-tuple-element.103), channel_id=1, source_target_pairs={{0,1},{1,2},{2,3},{4,5},{5,6},{6,7},{8,9},{9,10},{10,11},{12,13},{... | collective-permute-start | bytes 196616 | tf_op jit(solution)/shard_map/while/body/eval_jaxpr/ppermute | solution.py:23
  259.0 3.8 %copy-start.1 = (bf16[1,4096,128]{2,1,0:T(8,128)(2,1)}, bf16[1,4096,128]{2,1,0:T(8,128)(2,1)S(1)}, u32[]{:S(2)}) copy-start(bf16[1,4096,128]{2,1,0:T(8,128)(2,1)S(1)} %get-tuple-element.39) | copy-start | bytes 3145732
where the time goes:
time: 286 us; the launch traced here: 284 us
  waiting for transfers between devices  122 us (43%)
  starting transfers between devices  67.8 us (24%)
  local copies, waits for them, and re-layouts  48.6 us (17%)
  matrix products  41.5 us (15%)
    ppermute x8, waiting for transfers between devices, passed_along(): return lax.ppermute(value, axis, pairs)  113 us
    dot_general x8, matrix products, advance(): jnp.einsum('rtopq,rtpqk->rtok', blocks, picked, preferred_element_type=jn...  37.6 us
    ppermute x8, starting transfers between devices, padded(): before = lax.ppermute(last, axis, up)  36.2 us
    gather x32, local copies, waits for them, and re-layouts, one_row(): return row_blocks[row_sources]  26.4 us
    unnamed x5, local copies, waits for them, and re-layouts  21.7 us
    ppermute x8, starting transfers between devices, passed_along(): return lax.ppermute(value, axis, pairs)  16 us
    ppermute x8, starting transfers between devices, padded(): after = lax.ppermute(leading, axis, down)  15.6 us
    ppermute x8, waiting for transfers between devices, padded(): before = lax.ppermute(last, axis, up)  8.73 us
  transfers between devices with their start and end apart: 24, of which 16 were waited for; matrix products, arithmetic and copies ran while one was open for 1% of the time, Pallas kernels for 0%

commit v1 on v0

v1 whole, which is shorter than its diff:
```python
import jax
import jax.numpy as jnp
from jax import lax
from jax.experimental import pallas as pl
from jax.experimental.pallas import tpu as pltpu
from jax.sharding import PartitionSpec as P

TILE = 128
REACH = 2
WIDE = 2 * REACH
GROUP = 4
VMEM = pl.BlockSpec(memory_space=pltpu.VMEM)
SMEM = pl.BlockSpec(memory_space=pltpu.SMEM)
ANY = pl.BlockSpec(memory_space=pl.ANY)


def params():
    return pltpu.CompilerParams(vmem_limit_bytes=24 * 1024 * 1024)


def rows_of(tile, count=1):
    start = tile * TILE
    if not isinstance(start, int):
        start = pl.multiple_of(start, TILE)
    return pl.ds(start, count * TILE)


def stacked(state, table, base, pairs):
    return jnp.concatenate([state[rows_of(table[base + j]), :] for j in range(pairs)], axis=0)


def product(blocks, state):
    return jnp.dot(blocks, state, preferred_element_type=jnp.float32).astype(jnp.bfloat16)


def flat(blocks, pairs):
    split = jnp.swapaxes(blocks, 0, 1)
    return jnp.concatenate([split[j] for j in range(pairs)], axis=1)


def prepare_own(tiles, extra, pairs, transfer):
    count = tiles // GROUP

    def kernel(source, packed, landed, arrived):
        copies = [
            pltpu.make_async_copy(source.at[rows_of(g * GROUP, GROUP)], landed.at[rows_of(g * GROUP, GROUP)], arrived.at[g])
            for g in range(count)
        ]
        for copy in copies:
            copy.start()
        for g in range(count):
            copies[g].wait()
            for i in range(g * GROUP, (g + 1) * GROUP):
                packed[rows_of(i), :] = flat(landed[rows_of(i)], pairs)

    return pl.pallas_call(
        kernel,
        in_specs=[ANY],
        out_specs=VMEM,
        out_shape=jax.ShapeDtypeStruct(((tiles + extra) * TILE, pairs * TILE), jnp.bfloat16),
        scratch_shapes=[pltpu.VMEM(transfer.shape, jnp.bfloat16), pltpu.SemaphoreType.DMA((count,))],
        compiler_params=params(),
        name="prepare_own",
    )(transfer)


def prepare_odd(tiles, pairs, ints, main, lower, upper, packed):
    count = tiles // GROUP

    def kernel(table, source, low, high, old, new, landed, arrived):
        @pl.when(table[2] == 1)
        def _():
            copies = [
                pltpu.make_async_copy(source.at[rows_of(g * GROUP, GROUP)], landed.at[rows_of(g * GROUP, GROUP)], arrived.at[g])
                for g in range(count)
            ]
            for copy in copies:
                copy.start()
            for i in range(REACH):
                new[rows_of(tiles + i), :] = flat(low[rows_of(i)], pairs)
                new[rows_of(2 * tiles + REACH + i), :] = flat(high[rows_of(i)], pairs)
            for g in range(count):
                copies[g].wait()
                for i in range(g * GROUP, (g + 1) * GROUP):
                    new[rows_of(tiles + REACH + i), :] = flat(landed[rows_of(i)], pairs)

    return pl.pallas_call(
        kernel,
        in_specs=[SMEM, ANY, VMEM, VMEM, VMEM],
        out_specs=VMEM,
        out_shape=jax.ShapeDtypeStruct(packed.shape, packed.dtype),
        input_output_aliases={4: 0},
        scratch_shapes=[pltpu.VMEM(main.shape, jnp.bfloat16), pltpu.SemaphoreType.DMA((count,))],
        compiler_params=params(),
        name="prepare_odd",
    )(ints, main, lower, upper, packed)


HEAD = 8


def own_step(kind, tiles, pairs, width, ints, main, lower, upper, packed, state=None):
    emit = width > 0

    def kernel(table, middle, low, high, blocks, *rest):
        kept = rest[0] if state is None else rest[1]
        outs = rest[1:] if state is None else rest[2:]

        @pl.when(table[3] == kind)
        def _():
            skip = low.shape[0] // TILE - REACH
            kept[rows_of(0, REACH), :] = low[rows_of(skip, REACH), :]
            kept[rows_of(REACH, tiles), :] = middle[...]
            kept[rows_of(REACH + tiles, REACH), :] = high[rows_of(0, REACH), :]
            if emit:
                advance_own(tiles, pairs, width, table, kept, blocks, *outs)

    return call_step(kernel, tiles, width, [ints, main, lower, upper, packed], state, main.shape[1], "own_step")


def advance_own(tiles, pairs, width, table, kept, blocks, out, first, last):
    for i in range(tiles):
        fresh = product(blocks[rows_of(i), :], stacked(kept, table, HEAD + pairs * i, pairs))
        out[rows_of(i), :] = fresh
        if i < width:
            first[rows_of(i), :] = fresh
        if i >= tiles - width:
            last[rows_of(i - (tiles - width)), :] = fresh


def call_step(kernel, tiles, width, operands, state, bond, name, scratch=()):
    def shape(count):
        return jax.ShapeDtypeStruct((count * TILE, bond), jnp.bfloat16)

    outs = [shape(tiles + 2 * REACH)]
    if width > 0:
        outs += [shape(tiles), shape(width), shape(width)]
    aliases = {}
    if state is not None:
        aliases = {len(operands): 0}
        operands = operands + [state]
    return pl.pallas_call(
        kernel,
        in_specs=[SMEM] + [VMEM] * (len(operands) - 1),
        out_specs=[VMEM] * len(outs),
        out_shape=outs,
        input_output_aliases=aliases,
        scratch_shapes=list(scratch),
        compiler_params=params(),
        name=name,
    )(*operands)


def pair_step(kind, tiles, pairs, width, ints, main, lower, upper, packed, state):
    odd = HEAD + pairs * tiles

    def kernel(table, middle, low, high, blocks, old, kept, *rest):
        outs, wide = rest[:-1], rest[-1]

        @pl.when(table[3] == kind)
        def _():
            wide[rows_of(0, WIDE), :] = low[...]
            wide[rows_of(WIDE, tiles), :] = middle[...]
            wide[rows_of(WIDE + tiles, WIDE), :] = high[...]
            for i in range(tiles + 2 * REACH):
                kept[rows_of(i), :] = product(blocks[rows_of(tiles + i), :], stacked(wide, table, odd + pairs * i, pairs))
            if width > 0:
                advance_own(tiles, pairs, width, table, kept, blocks, *outs)

    scratch = [pltpu.VMEM(((tiles + 2 * WIDE) * TILE, main.shape[1]), jnp.bfloat16)]
    return call_step(kernel, tiles, width, [ints, main, lower, upper, packed], state, main.shape[1], "pair_step", scratch)


def finish(tiles, pairs, ints, state, packed, left):
    bond = state.shape[1]
    count = tiles // GROUP

    def kernel(table, kept, blocks, rows, env, grad, staged, sent):
        copies = []
        for i in range(tiles):
            sources = stacked(kept, table, HEAD + pairs * i, pairs)
            env[rows_of(i), :] = product(blocks[rows_of(i), :], sources)
            block = lax.dot_general(rows[rows_of(i), :], sources, (((1,), (1,)), ((), ())), preferred_element_type=jnp.float32)
            block = block.astype(jnp.bfloat16)
            block = jnp.stack([block[:, j * TILE : (j + 1) * TILE] for j in range(pairs)], axis=0)
            staged[rows_of(i)] = jnp.swapaxes(block, 0, 1)
            if i % GROUP == GROUP - 1:
                span = rows_of(i + 1 - GROUP, GROUP)
                copies.append(pltpu.make_async_copy(staged.at[span], grad.at[span], sent.at[i // GROUP]))
                copies[-1].start()
        for copy in copies:
            copy.wait()

    return pl.pallas_call(
        kernel,
        in_specs=[SMEM, VMEM, VMEM, VMEM],
        out_specs=[VMEM, ANY],
        out_shape=[
            jax.ShapeDtypeStruct((tiles * TILE, bond), jnp.bfloat16),
            jax.ShapeDtypeStruct((tiles * TILE, pairs, TILE), jnp.bfloat16),
        ],
        scratch_shapes=[pltpu.VMEM((tiles * TILE, pairs, TILE), jnp.bfloat16), pltpu.SemaphoreType.DMA((count,))],
        compiler_params=params(),
        name="finish",
    )(ints, state, packed, left)


def per_device(env_right, transfer, sources, env_left):
    ncol, nsec = lax.axis_size("col"), lax.axis_size("sec")
    layers = ncol // 2
    col, sec = lax.axis_index("col"), lax.axis_index("sec")
    layer, core = col // 2, col % 2
    blocks = transfer[0, 0]
    length, pairs = blocks.shape[0], blocks.shape[1]
    tiles = length // TILE
    right, left = env_right[0], env_left[0, 0]

    def move(value, hops):
        both = [
            (a * nsec + s, b * nsec + s + by) for a, b, by in hops for s in range(nsec) if 0 <= s + by < nsec
        ]
        return lax.ppermute(value, ("col", "sec"), both)

    top = ncol - 1
    packed = prepare_own(tiles, tiles + 2 * REACH, pairs, blocks)

    lower = move(right[-REACH * TILE :], [(top - 1, top, 1)])
    upper = move(right[: REACH * TILE], [(top - 1, top, -1)])

    odd = [(2 * z + 1, 2 * z, 0) for z in range(layers - 1)]
    odd_main = move(blocks, odd)
    odd_sources = move(sources[0, 0], odd)

    def edge(block_rows, source_rows):
        coded = (source_rows - sec * tiles).astype(jnp.bfloat16)
        coded = jnp.broadcast_to(coded[:, :, None], (REACH, pairs, TILE))
        return jnp.concatenate([block_rows, coded], axis=0)

    low_edge = move(edge(blocks[-REACH * TILE :], sources[0, 0, -REACH:]), [(a, b, 1) for a, b, _ in odd])
    high_edge = move(edge(blocks[: REACH * TILE], sources[0, 0, :REACH]), [(a, b, -1) for a, b, _ in odd])
    low_sources = low_edge[REACH * TILE :, :, 0].astype(jnp.int32) - tiles
    high_sources = high_edge[REACH * TILE :, :, 0].astype(jnp.int32) + tiles

    own_local = jnp.clip(sources[0, 0] - sec * tiles + REACH, 0, tiles + 2 * REACH - 1)
    odd_local = jnp.concatenate([low_sources, odd_sources - sec * tiles, high_sources], axis=0)
    odd_local = jnp.clip(odd_local + WIDE, 0, tiles + 2 * WIDE - 1)

    kind = 2 * (layers - 1 - layer) + core
    takes_odd = jnp.logical_and(core == 0, layer < layers - 1).astype(jnp.int32)
    zero = jnp.zeros((), jnp.int32)
    head = jnp.stack([col, sec, takes_odd, kind, zero, zero, zero, zero]).astype(jnp.int32)
    own_ints = jnp.concatenate([head, own_local.reshape(-1)])
    ints = jnp.concatenate([own_ints, odd_local.reshape(-1)])

    state, main, first, last = own_step(1, tiles, pairs, REACH, own_ints, right, lower, upper, packed)
    lower = move(last, [(top, top - 1, 1)])
    upper = move(first, [(top, top - 1, -1)])
    main = move(main, [(c, c ^ 1, 0) for c in range(ncol)])
    state, main, first, last = own_step(0, tiles, pairs, WIDE, own_ints, main, lower, upper, packed, state)
    packed = prepare_odd(tiles, pairs, ints, odd_main, low_edge[: REACH * TILE], high_edge[: REACH * TILE], packed)

    for step in range(1, layers):
        above, here = 2 * (layers - step), 2 * (layers - 1 - step)
        main = move(main, [(above, here, 0)])
        lower = move(last, [(above, here, 1)])
        upper = move(first, [(above, here, -1)])
        passed = [move(value, [(c, c ^ 1, 0) for c in range(ncol)]) for value in (main, lower, upper)]
        if step < layers - 1:
            state, main, first, last = pair_step(2 * step, tiles, pairs, WIDE, ints, main, lower, upper, packed, state)
        else:
            (state,) = pair_step(2 * step, tiles, pairs, 0, ints, main, lower, upper, packed, state)
        (state,) = own_step(2 * step + 1, tiles, pairs, 0, own_ints, *passed, packed, state)

    env, grad = finish(tiles, pairs, own_ints, state, packed, left)
    return env[None, None], grad[None, None]


def solution(mesh):
    placed = (
        P(None, "sec", None),
        P("col", None, "sec", None, None),
        P("col", None, "sec", None),
        P("col", None, "sec", None),
    )
    return jax.shard_map(
        per_device,
        mesh=mesh,
        in_specs=placed,
        out_specs=(P("col", None, "sec", None), P("col", None, "sec", None, None)),
        check_vma=False,
    )
```

time: 286 us -> 120 us (0.42)
  waiting for transfers between devices: 122 us -> 2.13 us
  matrix products: 41.5 us -> 0 us
  local copies, waits for them, and re-layouts: 48.6 us -> 26.1 us
  Pallas kernels: 0 us -> 13.3 us
    ppermute x24 -> x27, waiting for transfers between devices: 122 us -> 2.13 us  [move(): return lax.ppermute(value, ('col', 'sec'), both)]
    dot_general x9 -> x0, matrix products: 41.5 us -> none  [the longest x8 37.6 us: advance(): jnp.einsum('rtopq,rtpqk->rtok', blocks, picked, preferred_element_type=jn...]
    gather x32 -> x0, local copies, waits for them, and re-layouts: 26.4 us -> none  [one_row(): return row_blocks[row_sources]]
    pallas_call x0 -> x11, Pallas kernels: none -> 13.3 us  [the longest x8 5.4 us: call_step(): pl.pallas_call(kernel, in_specs=[SMEM] + [VMEM] * (len(operands) - 1), ou...]
    unnamed x5 -> x22, local copies, waits for them, and re-layouts: 21.7 us -> 15.2 us
    slice x8 -> x4, local copies, waits for them, and re-layouts: 0.08 us -> 4.88 us  [the longest x1 1.92 us: per_device(): blocks[-REACH * TILE:]]
    ppermute x24 -> x27, starting transfers between devices: 67.8 us -> 70.4 us  [move(): return lax.ppermute(value, ('col', 'sec'), both)]
  transfers between devices with their start and end apart: 24 -> 27, of which waited for: 16 -> 3; matrix products, arithmetic and copies ran while one was open for 1% -> 14% of each run, Pallas kernels for 0% -> 6%
where the time goes in v1:
time: 120 us; the launch traced here: 118 us
  starting transfers between devices  70.4 us (59%)
  local copies, waits for them, and re-layouts  26.1 us (22%)
  Pallas kernels  13.3 us (11%)
  other arithmetic  5.3 us (4%)
  waiting for transfers between devices  2.13 us (2%)
    ppermute x27, starting transfers between devices, move(): return lax.ppermute(value, ('col', 'sec'), both)  70.4 us
    unnamed x22, local copies, waits for them, and re-layouts  15.2 us
    pallas_call x8, Pallas kernels, call_step(): pl.pallas_call(kernel, in_specs=[SMEM] + [VMEM] * (len(operands) - 1), ou...  5.4 us
    pallas_call x1, Pallas kernels, finish(): pl.pallas_call(kernel, in_specs=[SMEM, VMEM, VMEM, VMEM], out_specs=[VMEM...  4.86 us
    pallas_call x1, Pallas kernels, prepare_own(): pl.pallas_call(kernel, in_specs=[ANY], out_specs=VMEM, out_shape=jax.Shap...  2.43 us
  transfers between devices with their start and end apart: 27, of which 3 were waited for; matrix products, arithmetic and copies ran while one was open for 14% of the time, Pallas kernels for 6%

profile of v1, /device:TPU:3, one launch (start us, length us, event | category | flops | bytes accessed | tf_op | source)
XLA Modules:
  0.0 118.4 jit_solution(17832556523784575446)
XLA Ops:
  0.6 4.7 %collective-permute-start.11 = (bf16[4096,4,128]{2,1,0:T(4,128)(2,1)}, bf16[4096,4,128]{2,1,0:T(4,128)(2,1)}, u32[]{:S(2)}, u32[]{:S(2)}) collective-permute-start(bf16[4096,4,128]{2,1,0:T(4,128)(2,1)} %bitcast.24), channel_id=1, source_target_pairs={{4,0},{5,1},{6,2},{7,3},{12,8},{13,9},{14,10},{15,11},{20,16},{21,... | collective-permute-start | bytes 12582920 | tf_op jit(solution)/shard_map/ppermute | solution.py:222
  5.3 0.9 slice_bitcast_fusion.2
  6.2 0.7 collective-permute-start.4
  6.9 0.7 collective-permute-start.3
  7.5 0.7 add_clamp_fusion
  8.2 2.2 %copy-done.3 = bf16[1,1,4096,4,128]{4,3,2,1,0:T(4,128)(2,1)S(1)} copy-done((bf16[1,1,4096,4,128]{4,3,2,1,0:T(4,128)(2,1)S(1)}, bf16[1,1,4096,4,128]{4,3,2,1,0:T(4,128)(2,1)}, u32[]{:S(2)}) %copy-start.3) | copy-done | bytes 4194328
  10.4 2.4 %prepare_own.1.blocks.old = bf16[8704,512]{1,0:T(8,128)(2,1)S(1)} custom-call(bf16[4096,4,128]{2,1,0:T(4,128)(2,1)S(1)} %bitcast.25), custom_call_target="tpu_custom_call" | custom-call | tf_op jit(solution)/shard_map/prepare_own/pallas_call | solution.py:56
  12.9 3.5 %copy-done = bf16[8704,512]{1,0:T(8,128)(2,1)} copy-done((bf16[8704,512]{1,0:T(8,128)(2,1)}, bf16[8704,512]{1,0:T(8,128)(2,1)S(1)}, u32[]{:S(2)}) %copy-start) | copy-done | bytes 8912920
  17.2 3.5 %copy-done.1 = bf16[8704,512]{1,0:T(8,128)(2,1)S(1)} copy-done((bf16[8704,512]{1,0:T(8,128)(2,1)S(1)}, bf16[8704,512]{1,0:T(8,128)(2,1)}, u32[]{:S(2)}) %copy-start.1) | copy-done | bytes 8912920
  21.4 2.4 %collective-permute-start.1 = (s32[32,4]{0,1:T(4,128)S(1)}, s32[32,4]{0,1:T(4,128)S(1)}, u32[]{:S(2)}, u32[]{:S(2)}) collective-permute-start(s32[32,4]{0,1:T(4,128)S(1)} %bitcast.28), channel_id=1, source_target_pairs={{4,0},{5,1},{6,2},{7,3},{12,8},{13,9},{14,10},{15,11},{20,16},{21,... | collective-permute-start | bytes 1544 | tf_op jit(solution)/shard_map/ppermute | solution.py:222
  23.7 0.7 collective-permute-start.6
  24.4 0.7 collective-permute-start.7
  25.1 1.9 %slice_bitcast_fusion.1 = (bf16[256,4,128]{2,1,0:T(4,128)(2,1)S(1)}, bf16[256,4,128]{2,1,0:T(4,128)(2,1)}) fusion(bf16[1,1,4096,4,128]{4,3,2,1,0:T(4,128)(2,1)} %param.5), kind=kLoop, calls=%fused_computation.3 | loop fusion | bytes 1048576 | tf_op jit(solution)/shard_map/slice | solution.py:239
  27.0 1.2 %own_step.6 = (bf16[4608,128]{1,0:T(8,128)(2,1)S(1)}, bf16[4096,128]{1,0:T(8,128)(2,1)S(1)}, bf16[512,128]{1,0:T(8,128)(2,1)S(1)}, bf16[512,128]{1,0:T(8,128)(2,1)}) custom-call(s32[136]{0:T(256)S(1)} %concatenate.16.table, bf16[4096,128]{1,0:T(8,128)(2,1)S(1)} %collective-permute-done.5.middle, ...), custom_call_target="tpu_custom_call", output_to_operand_aliasing={{0}: (5, {})} | custom-call | tf_op jit(solution)/shard_map/own_step/pallas_call | solution.py:142
  28.2 0.7 copy-done.6
  28.9 0.7 collective-permute-start.8
  30.8 0.7 broadcast_in_dim.9
  31.5 1.8 %pad_maximum_fusion.1 = bf16[258,4,128]{2,1,0:T(4,128)(2,1)} fusion(bf16[2,4,128]{2,1,0:T(4,128)(2,1)S(1)} %broadcast_in_dim.9, bf16[256,4,128]{2,1,0:T(4,128)(2,1)} %get-tuple-element.39), kind=kLoop, calls=%fused_computation.1 | loop fusion | flops 132096 | bytes 528384 | tf_op jit(solution)/shard_map/concatenate | solution.py:237
  33.4 2.0 %collective-permute-start.2 = (bf16[258,4,128]{2,1,0:T(4,128)(2,1)}, bf16[258,4,128]{2,1,0:T(4,128)(2,1)}, u32[]{:S(2)}, u32[]{:S(2)}) collective-permute-start(bf16[258,4,128]{2,1,0:T(4,128)(2,1)} %pad_maximum_fusion.1), channel_id=1, source_target_pairs={{5,0},{6,1},{7,2},{13,8},{14,9},{15,10},{21,16},{22,17},{23,18}} | collective-permute-start | bytes 792584 | tf_op jit(solution)/shard_map/ppermute | solution.py:222
  35.3 1.2 %copy.20 = bf16[1,1,2,4]{3,2,1,0:T(2,128)(2,1)} copy(bf16[1,1,2,4]{2,3,1,0:T(4,128)(2,1)} %get-tuple-element.42) | data formatting | bytes 32 | tf_op jit(solution)/shard_map/convert_element_type | solution.py:235
  36.5 0.7 broadcast_in_dim.8
  37.5 1.7 %collective-permute-start = (bf16[258,4,128]{2,1,0:T(4,128)(2,1)S(1)}, bf16[258,4,128]{2,1,0:T(4,128)(2,1)S(1)}, u32[]{:S(2)}, u32[]{:S(2)}) collective-permute-start(bf16[258,4,128]{2,1,0:T(4,128)(2,1)S(1)} %pad_maximum_fusion), channel_id=1, source_target_pairs={{4,1},{5,2},{6,3},{12,9},{13,10},{14,11},{20,17},{21,18},{22,19}} | collective-permute-start | bytes 792584 | tf_op jit(solution)/shard_map/ppermute | solution.py:222
  39.8 0.7 convert_add_fusion
  40.4 0.7 collective-permute-start.9
  41.1 0.7 collective-permute-start.10
  41.8 0.7 collective-permute-done
  42.5 0.7 copy-done.7
  43.4 0.8 fusion
  44.2 0.7 copy.24
  44.9 0.8 min.25
  45.7 0.8 concatenate.20.table
  46.5 1.0 slice.59.high
  47.5 1.0 slice.58.low
  48.6 1.4 %collective-permute-start.15 = (bf16[4096,128]{1,0:T(8,128)(2,1)S(1)}, bf16[4096,128]{1,0:T(8,128)(2,1)S(1)}, u32[]{:S(2)}, u32[]{:S(2)}) collective-permute-start(bf16[4096,128]{1,0:T(8,128)(2,1)S(1)} %collective-permute-done.8.middle), channel_id=1, source_target_pairs={{0,4},{1,5},{2,6},{3,7},{4,0},{5,1},{6,2},{7,3},{8,12},{9,13},{10,... | collective-permute-start | bytes 3145736 | tf_op jit(solution)/shard_map/ppermute | solution.py:222
  50.0 3.5 %copy-done.2 = bf16[8704,512]{1,0:T(8,128)(2,1)S(1)} copy-done((bf16[8704,512]{1,0:T(8,128)(2,1)S(1)}, bf16[8704,512]{1,0:T(8,128)(2,1)}, u32[]{:S(2)}) %copy-start.2) | copy-done | bytes 8912920
  54.2 0.7 pair_step.3
  55.0 0.7 collective-permute-start.12
  55.7 3.2 %collective-permute-start.16 = (bf16[512,128]{1,0:T(8,128)(2,1)S(1)}, bf16[512,128]{1,0:T(8,128)(2,1)S(1)}, u32[]{:S(2)}, u32[]{:S(2)}) collective-permute-start(bf16[512,128]{1,0:T(8,128)(2,1)S(1)} %collective-permute-done.9.low), channel_id=1, source_target_pairs={{0,4},{1,5},{2,6},{3,7},{4,0},{5,1},{6,2},{7,3},{8,12},{9,13},{10,... | collective-permute-start | bytes 393224 | tf_op jit(solution)/shard_map/ppermute | solution.py:222
  59.9 0.7 collective-permute-start.14
  61.8 0.7 collective-permute-start.18
  62.5 1.0 collective-permute-start.24
  63.5 37.1 %collective-permute-start.19 = (bf16[4096,128]{1,0:T(8,128)(2,1)S(1)}, bf16[4096,128]{1,0:T(8,128)(2,1)S(1)}, u32[]{:S(2)}, u32[]{:S(2)}) collective-permute-start(bf16[4096,128]{1,0:T(8,128)(2,1)S(1)} %collective-permute-done.18.middle), channel_id=1, source_target_pairs={{0,4},{1,5},{2,6},{3,7},{4,0},{5,1},{6,2},{7,3},{8,12},{9,13},{10,... | collective-permute-start | bytes 3145736 | tf_op jit(solution)/shard_map/ppermute | solution.py:222
  101.2 0.7 collective-permute-start.22
  101.9 1.1 collective-permute-done.25.low
  103.0 0.7 collective-permute-start.26
  103.7 5.1 %collective-permute-start.21 = (bf16[512,128]{1,0:T(8,128)(2,1)S(1)}, bf16[512,128]{1,0:T(8,128)(2,1)S(1)}, u32[]{:S(2)}, u32[]{:S(2)}) collective-permute-start(bf16[512,128]{1,0:T(8,128)(2,1)S(1)} %collective-permute-done.20.low), channel_id=1, source_target_pairs={{0,4},{1,5},{2,6},{3,7},{4,0},{5,1},{6,2},{7,3},{8,12},{9,13},{10,... | collective-permute-start | bytes 393224 | tf_op jit(solution)/shard_map/ppermute | solution.py:222
  108.8 2.2 %collective-permute-start.23 = (bf16[512,128]{1,0:T(8,128)(2,1)S(1)}, bf16[512,128]{1,0:T(8,128)(2,1)S(1)}, u32[]{:S(2)}, u32[]{:S(2)}) collective-permute-start(bf16[512,128]{1,0:T(8,128)(2,1)S(1)} %collective-permute-done.22.high), channel_id=1, source_target_pairs={{0,4},{1,5},{2,6},{3,7},{4,0},{5,1},{6,2},{7,3},{8,12},{9,13},{10,... | collective-permute-start | bytes 393224 | tf_op jit(solution)/shard_map/ppermute | solution.py:222
  113.4 4.9 %finish.1 = (bf16[4096,128]{1,0:T(8,128)(2,1)}, bf16[4096,4,128]{2,1,0:T(4,128)(2,1)}) custom-call(s32[136]{0:T(256)S(1)} %concatenate.16.table, bf16[4608,128]{1,0:T(8,128)(2,1)S(1)} %own_step.9.kept, bf16[8704,512]{1,0:T(8,128)(2,1)S(1)} %prepare_odd.1.blocks, bf16[4096,128]{1,0:T(8,128)(2,1)S(1)} %bitcast.27), custom_call_target="tpu_custom_call" | custom-call | tf_op jit(solution)/shard_map/finish/pallas_call | solution.py:194
  (64 shorter events, 9.4 us)
Async XLA Ops:
  0.6 49.4 %collective-permute-start.11 = (bf16[4096,4,128]{2,1,0:T(4,128)(2,1)}, bf16[4096,4,128]{2,1,0:T(4,128)(2,1)}, u32[]{:S(2)}, u32[]{:S(2)}) collective-permute-start(bf16[4096,4,128]{2,1,0:T(4,128)(2,1)} %bitcast.24), channel_id=1, source_target_pairs={{4,0},{5,1},{6,2},{7,3},{12,8},{13,9},{14,10},{15,11},{20,16},{21,... | collective-permute-start | bytes 12582920 | tf_op jit(solution)/shard_map/ppermute | solution.py:222
  6.2 10.5 %collective-permute-start.4 = (bf16[256,128]{1,0:T(8,128)(2,1)S(1)}, bf16[256,128]{1,0:T(8,128)(2,1)S(1)}, u32[]{:S(2)}, u32[]{:S(2)}) collective-permute-start(bf16[256,128]{1,0:T(8,128)(2,1)S(1)} %get-tuple-element.40), channel_id=1, source_target_pairs={{25,28},{26,29},{27,30}} | collective-permute-start | bytes 196616 | tf_op jit(solution)/shard_map/ppermute | solution.py:222
  6.9 9.8 %collective-permute-start.3 = (bf16[256,128]{1,0:T(8,128)(2,1)S(1)}, bf16[256,128]{1,0:T(8,128)(2,1)S(1)}, u32[]{:S(2)}, u32[]{:S(2)}) collective-permute-start(bf16[256,128]{1,0:T(8,128)(2,1)S(1)} %get-tuple-element.41), channel_id=1, source_target_pairs={{24,29},{25,30},{26,31}} | collective-permute-start | bytes 196616 | tf_op jit(solution)/shard_map/ppermute | solution.py:222
  8.2 2.2 %copy-start.3 = (bf16[1,1,4096,4,128]{4,3,2,1,0:T(4,128)(2,1)S(1)}, bf16[1,1,4096,4,128]{4,3,2,1,0:T(4,128)(2,1)}, u32[]{:S(2)}) copy-start(bf16[1,1,4096,4,128]{4,3,2,1,0:T(4,128)(2,1)} %param.5) | copy-start | bytes 12582916
  10.4 6.7 %copy-start.4 = (bf16[1,4096,128]{2,1,0:T(8,128)(2,1)S(1)}, bf16[1,4096,128]{2,1,0:T(8,128)(2,1)}, u32[]{:S(2)}) copy-start(bf16[1,4096,128]{2,1,0:T(8,128)(2,1)} %param.4) | copy-start | bytes 3145732
  12.9 3.5 %copy-start = (bf16[8704,512]{1,0:T(8,128)(2,1)}, bf16[8704,512]{1,0:T(8,128)(2,1)S(1)}, u32[]{:S(2)}) copy-start(bf16[8704,512]{1,0:T(8,128)(2,1)S(1)} %prepare_own.1.blocks.old) | copy-start | bytes 26738692
  16.6 0.6 copy-start.9
  16.6 0.6 copy-start.10
  17.2 3.5 %copy-start.1 = (bf16[8704,512]{1,0:T(8,128)(2,1)S(1)}, bf16[8704,512]{1,0:T(8,128)(2,1)}, u32[]{:S(2)}) copy-start(bf16[8704,512]{1,0:T(8,128)(2,1)} %copy-done) | copy-start | bytes 26738692
  20.7 0.7 copy-start.8
  21.2 5.7 %collective-permute-start.5 = (bf16[4096,128]{1,0:T(8,128)(2,1)S(1)}, bf16[4096,128]{1,0:T(8,128)(2,1)S(1)}, u32[]{:S(2)}, u32[]{:S(2)}) collective-permute-start(bf16[4096,128]{1,0:T(8,128)(2,1)S(1)} %get-tuple-element.20), channel_id=1, source_target_pairs={{0,4},{1,5},{2,6},{3,7},{4,0},{5,1},{6,2},{7,3},{8,12},{9,13},{10,... | collective-permute-start | bytes 3145736 | tf_op jit(solution)/shard_map/ppermute | solution.py:222
  21.4 17.8 %collective-permute-start.1 = (s32[32,4]{0,1:T(4,128)S(1)}, s32[32,4]{0,1:T(4,128)S(1)}, u32[]{:S(2)}, u32[]{:S(2)}) collective-permute-start(s32[32,4]{0,1:T(4,128)S(1)} %bitcast.28), channel_id=1, source_target_pairs={{4,0},{5,1},{6,2},{7,3},{12,8},{13,9},{14,10},{15,11},{20,16},{21,... | collective-permute-start | bytes 1544 | tf_op jit(solution)/shard_map/ppermute | solution.py:222
  23.7 3.3 %collective-permute-start.6 = (bf16[256,128]{1,0:T(8,128)(2,1)S(1)}, bf16[256,128]{1,0:T(8,128)(2,1)S(1)}, u32[]{:S(2)}, u32[]{:S(2)}) collective-permute-start(bf16[256,128]{1,0:T(8,128)(2,1)S(1)} %get-tuple-element.21), channel_id=1, source_target_pairs={{28,25},{29,26},{30,27}} | collective-permute-start | bytes 196616 | tf_op jit(solution)/shard_map/ppermute | solution.py:222
  24.4 2.6 %collective-permute-start.7 = (bf16[256,128]{1,0:T(8,128)(2,1)S(1)}, bf16[256,128]{1,0:T(8,128)(2,1)S(1)}, u32[]{:S(2)}, u32[]{:S(2)}) collective-permute-start(bf16[256,128]{1,0:T(8,128)(2,1)S(1)} %get-tuple-element.22), channel_id=1, source_target_pairs={{29,24},{30,25},{31,26}} | collective-permute-start | bytes 196616 | tf_op jit(solution)/shard_map/ppermute | solution.py:222
  28.2 0.7 copy-start.6
  28.9 19.7 %collective-permute-start.8 = (bf16[4096,128]{1,0:T(8,128)(2,1)S(1)}, bf16[4096,128]{1,0:T(8,128)(2,1)S(1)}, u32[]{:S(2)}, u32[]{:S(2)}) collective-permute-start(bf16[4096,128]{1,0:T(8,128)(2,1)S(1)} %get-tuple-element.24), channel_id=1, source_target_pairs={{24,16},{25,17},{26,18},{27,19}} | collective-permute-start | bytes 3145736 | tf_op jit(solution)/shard_map/ppermute | solution.py:222
  33.4 6.4 %collective-permute-start.2 = (bf16[258,4,128]{2,1,0:T(4,128)(2,1)}, bf16[258,4,128]{2,1,0:T(4,128)(2,1)}, u32[]{:S(2)}, u32[]{:S(2)}) collective-permute-start(bf16[258,4,128]{2,1,0:T(4,128)(2,1)} %pad_maximum_fusion.1), channel_id=1, source_target_pairs={{5,0},{6,1},{7,2},{13,8},{14,9},{15,10},{21,16},{22,17},{23,18}} | collective-permute-start | bytes 792584 | tf_op jit(solution)/shard_map/ppermute | solution.py:222
  37.5 5.0 %collective-permute-start = (bf16[258,4,128]{2,1,0:T(4,128)(2,1)S(1)}, bf16[258,4,128]{2,1,0:T(4,128)(2,1)S(1)}, u32[]{:S(2)}, u32[]{:S(2)}) collective-permute-start(bf16[258,4,128]{2,1,0:T(4,128)(2,1)S(1)} %pad_maximum_fusion), channel_id=1, source_target_pairs={{4,1},{5,2},{6,3},{12,9},{13,10},{14,11},{20,17},{21,18},{22,19}} | collective-permute-start | bytes 792584 | tf_op jit(solution)/shard_map/ppermute | solution.py:222
  40.4 13.8 %collective-permute-start.9 = (bf16[512,128]{1,0:T(8,128)(2,1)}, bf16[512,128]{1,0:T(8,128)(2,1)S(1)}, u32[]{:S(2)}, u32[]{:S(2)}) collective-permute-start(bf16[512,128]{1,0:T(8,128)(2,1)} %get-tuple-element.25), channel_id=1, source_target_pairs={{24,17},{25,18},{26,19}} | collective-permute-start | bytes 393224 | tf_op jit(solution)/shard_map/ppermute | solution.py:222
  41.1 13.1 %collective-permute-start.10 = (bf16[512,128]{1,0:T(8,128)(2,1)}, bf16[512,128]{1,0:T(8,128)(2,1)S(1)}, u32[]{:S(2)}, u32[]{:S(2)}) collective-permute-start(bf16[512,128]{1,0:T(8,128)(2,1)} %copy-done.6), channel_id=1, source_target_pairs={{25,16},{26,17},{27,18}} | collective-permute-start | bytes 393224 | tf_op jit(solution)/shard_map/ppermute | solution.py:222
  42.5 0.7 copy-start.7
  48.6 12.0 %collective-permute-start.15 = (bf16[4096,128]{1,0:T(8,128)(2,1)S(1)}, bf16[4096,128]{1,0:T(8,128)(2,1)S(1)}, u32[]{:S(2)}, u32[]{:S(2)}) collective-permute-start(bf16[4096,128]{1,0:T(8,128)(2,1)S(1)} %collective-permute-done.8.middle), channel_id=1, source_target_pairs={{0,4},{1,5},{2,6},{3,7},{4,0},{5,1},{6,2},{7,3},{8,12},{9,13},{10,... | collective-permute-start | bytes 3145736 | tf_op jit(solution)/shard_map/ppermute | solution.py:222
  50.0 3.5 %copy-start.2 = (bf16[8704,512]{1,0:T(8,128)(2,1)S(1)}, bf16[8704,512]{1,0:T(8,128)(2,1)}, u32[]{:S(2)}) copy-start(bf16[8704,512]{1,0:T(8,128)(2,1)} %copy-done) | copy-start | bytes 26738692
  55.0 6.2 %collective-permute-start.12 = (bf16[4096,128]{1,0:T(8,128)(2,1)S(1)}, bf16[4096,128]{1,0:T(8,128)(2,1)S(1)}, u32[]{:S(2)}, u32[]{:S(2)}) collective-permute-start(bf16[4096,128]{1,0:T(8,128)(2,1)S(1)} %get-tuple-element.28), channel_id=1, source_target_pairs={{16,8},{17,9},{18,10},{19,11}} | collective-permute-start | bytes 3145736 | tf_op jit(solution)/shard_map/ppermute | solution.py:222
  55.7 4.2 %collective-permute-start.16 = (bf16[512,128]{1,0:T(8,128)(2,1)S(1)}, bf16[512,128]{1,0:T(8,128)(2,1)S(1)}, u32[]{:S(2)}, u32[]{:S(2)}) collective-permute-start(bf16[512,128]{1,0:T(8,128)(2,1)S(1)} %collective-permute-done.9.low), channel_id=1, source_target_pairs={{0,4},{1,5},{2,6},{3,7},{4,0},{5,1},{6,2},{7,3},{8,12},{9,13},{10,... | collective-permute-start | bytes 393224 | tf_op jit(solution)/shard_map/ppermute | solution.py:222
  58.9 1.7 %collective-permute-start.17 = (bf16[512,128]{1,0:T(8,128)(2,1)S(1)}, bf16[512,128]{1,0:T(8,128)(2,1)S(1)}, u32[]{:S(2)}, u32[]{:S(2)}) collective-permute-start(bf16[512,128]{1,0:T(8,128)(2,1)S(1)} %collective-permute-done.10.high), channel_id=1, source_target_pairs={{0,4},{1,5},{2,6},{3,7},{4,0},{5,1},{6,2},{7,3},{8,12},{9,13},{10,... | collective-permute-start | bytes 393224 | tf_op jit(solution)/shard_map/ppermute | solution.py:222
  59.0 2.2 %collective-permute-start.13 = (bf16[512,128]{1,0:T(8,128)(2,1)S(1)}, bf16[512,128]{1,0:T(8,128)(2,1)S(1)}, u32[]{:S(2)}, u32[]{:S(2)}) collective-permute-start(bf16[512,128]{1,0:T(8,128)(2,1)S(1)} %get-tuple-element.29), channel_id=1, source_target_pairs={{16,9},{17,10},{18,11}} | collective-permute-start | bytes 393224 | tf_op jit(solution)/shard_map/ppermute | solution.py:222
  59.9 1.3 %collective-permute-start.14 = (bf16[512,128]{1,0:T(8,128)(2,1)S(1)}, bf16[512,128]{1,0:T(8,128)(2,1)S(1)}, u32[]{:S(2)}, u32[]{:S(2)}) collective-permute-start(bf16[512,128]{1,0:T(8,128)(2,1)S(1)} %get-tuple-element.30), channel_id=1, source_target_pairs={{17,8},{18,9},{19,10}} | collective-permute-start | bytes 393224 | tf_op jit(solution)/shard_map/ppermute | solution.py:222
  61.8 1.7 %collective-permute-start.18 = (bf16[4096,128]{1,0:T(8,128)(2,1)S(1)}, bf16[4096,128]{1,0:T(8,128)(2,1)S(1)}, u32[]{:S(2)}, u32[]{:S(2)}) collective-permute-start(bf16[4096,128]{1,0:T(8,128)(2,1)S(1)} %get-tuple-element.32), channel_id=1, source_target_pairs={{8,0},{9,1},{10,2},{11,3}} | collective-permute-start | bytes 3145736 | tf_op jit(solution)/shard_map/ppermute | solution.py:222
  62.5 48.5 %collective-permute-start.24 = (bf16[4096,128]{1,0:T(8,128)(2,1)S(1)}, bf16[4096,128]{1,0:T(8,128)(2,1)S(1)}, u32[]{:S(2)}, u32[]{:S(2)}) collective-permute-start(bf16[4096,128]{1,0:T(8,128)(2,1)S(1)} %collective-permute-done.12.middle), channel_id=1, source_target_pairs={{0,4},{1,5},{2,6},{3,7},{4,0},{5,1},{6,2},{7,3},{8,12},{9,13},{10,... | collective-permute-start | bytes 3145736 | tf_op jit(solution)/shard_map/ppermute | solution.py:222
  63.5 48.7 %collective-permute-start.19 = (bf16[4096,128]{1,0:T(8,128)(2,1)S(1)}, bf16[4096,128]{1,0:T(8,128)(2,1)S(1)}, u32[]{:S(2)}, u32[]{:S(2)}) collective-permute-start(bf16[4096,128]{1,0:T(8,128)(2,1)S(1)} %collective-permute-done.18.middle), channel_id=1, source_target_pairs={{0,4},{1,5},{2,6},{3,7},{4,0},{5,1},{6,2},{7,3},{8,12},{9,13},{10,... | collective-permute-start | bytes 3145736 | tf_op jit(solution)/shard_map/ppermute | solution.py:222
  100.6 2.5 %collective-permute-start.25 = (bf16[512,128]{1,0:T(8,128)(2,1)S(1)}, bf16[512,128]{1,0:T(8,128)(2,1)S(1)}, u32[]{:S(2)}, u32[]{:S(2)}) collective-permute-start(bf16[512,128]{1,0:T(8,128)(2,1)S(1)} %collective-permute-done.13.low), channel_id=1, source_target_pairs={{0,4},{1,5},{2,6},{3,7},{4,0},{5,1},{6,2},{7,3},{8,12},{9,13},{10,... | collective-permute-start | bytes 393224 | tf_op jit(solution)/shard_map/ppermute | solution.py:222
  100.6 3.2 %collective-permute-start.20 = (bf16[512,128]{1,0:T(8,128)(2,1)S(1)}, bf16[512,128]{1,0:T(8,128)(2,1)S(1)}, u32[]{:S(2)}, u32[]{:S(2)}) collective-permute-start(bf16[512,128]{1,0:T(8,128)(2,1)S(1)} %get-tuple-element.33), channel_id=1, source_target_pairs={{8,1},{9,2},{10,3}} | collective-permute-start | bytes 393224 | tf_op jit(solution)/shard_map/ppermute | solution.py:222
  101.2 7.6 %collective-permute-start.22 = (bf16[512,128]{1,0:T(8,128)(2,1)S(1)}, bf16[512,128]{1,0:T(8,128)(2,1)S(1)}, u32[]{:S(2)}, u32[]{:S(2)}) collective-permute-start(bf16[512,128]{1,0:T(8,128)(2,1)S(1)} %get-tuple-element.34), channel_id=1, source_target_pairs={{9,0},{10,1},{11,2}} | collective-permute-start | bytes 393224 | tf_op jit(solution)/shard_map/ppermute | solution.py:222
  103.0 8.0 %collective-permute-start.26 = (bf16[512,128]{1,0:T(8,128)(2,1)S(1)}, bf16[512,128]{1,0:T(8,128)(2,1)S(1)}, u32[]{:S(2)}, u32[]{:S(2)}) collective-permute-start(bf16[512,128]{1,0:T(8,128)(2,1)S(1)} %collective-permute-done.14.high), channel_id=1, source_target_pairs={{0,4},{1,5},{2,6},{3,7},{4,0},{5,1},{6,2},{7,3},{8,12},{9,13},{10,... | collective-permute-start | bytes 393224 | tf_op jit(solution)/shard_map/ppermute | solution.py:222
  103.7 8.4 %collective-permute-start.21 = (bf16[512,128]{1,0:T(8,128)(2,1)S(1)}, bf16[512,128]{1,0:T(8,128)(2,1)S(1)}, u32[]{:S(2)}, u32[]{:S(2)}) collective-permute-start(bf16[512,128]{1,0:T(8,128)(2,1)S(1)} %collective-permute-done.20.low), channel_id=1, source_target_pairs={{0,4},{1,5},{2,6},{3,7},{4,0},{5,1},{6,2},{7,3},{8,12},{9,13},{10,... | collective-permute-start | bytes 393224 | tf_op jit(solution)/shard_map/ppermute | solution.py:222
  108.8 3.4 %collective-permute-start.23 = (bf16[512,128]{1,0:T(8,128)(2,1)S(1)}, bf16[512,128]{1,0:T(8,128)(2,1)S(1)}, u32[]{:S(2)}, u32[]{:S(2)}) collective-permute-start(bf16[512,128]{1,0:T(8,128)(2,1)S(1)} %collective-permute-done.22.high), channel_id=1, source_target_pairs={{0,4},{1,5},{2,6},{3,7},{4,0},{5,1},{6,2},{7,3},{8,12},{9,13},{10,... | collective-permute-start | bytes 393224 | tf_op jit(solution)/shard_map/ppermute | solution.py:222
  112.2 1.2 %copy-start.5 = (bf16[1,1,4096,128]{3,2,1,0:T(8,128)(2,1)S(1)}, bf16[1,1,4096,128]{3,2,1,0:T(8,128)(2,1)}, u32[]{:S(2)}) copy-start(bf16[1,1,4096,128]{3,2,1,0:T(8,128)(2,1)} %param.7) | copy-start | bytes 3145732

commit v2 on v0

v2 whole, which is shorter than its diff:
```python
import jax
import jax.numpy as jnp
from jax import lax
from jax.experimental import pallas as pl
from jax.experimental.pallas import tpu as pltpu
from jax.sharding import PartitionSpec as P

TILE = 128
REACH = 2
WIDE = 2 * REACH
BAND = 2 * REACH + 1
GROUP = 4
VMEM = pl.BlockSpec(memory_space=pltpu.VMEM)
SMEM = pl.BlockSpec(memory_space=pltpu.SMEM)
HBM = pl.BlockSpec(memory_space=pltpu.HBM)


def params():
    return pltpu.CompilerParams(vmem_limit_bytes=16 * 1024 * 1024)


def cost(flops):
    return pl.CostEstimate(flops=int(flops), bytes_accessed=0, transcendentals=0)


def rows_of(tile, count=1):
    start = tile * TILE
    if not isinstance(start, int):
        start = pl.multiple_of(start, TILE)
    return pl.ds(start, count * TILE)


def tile_rows(count, width):
    return jax.ShapeDtypeStruct((count * TILE, width), jnp.bfloat16)


def kind_here():
    ncol, col = lax.axis_size("col"), lax.axis_index("col")
    return 2 * (ncol // 2 - 1 - col // 2) + col % 2


def reversed_here():
    return lax.axis_index("sec") % 2 == 0


def partner(s):
    return s + 1 if s % 2 == 0 else s - 1


def other(s):
    return s - 1 if s % 2 == 0 else s + 1


def places(table, tiles):
    back = reversed_here()
    base = lax.axis_index("sec") * tiles
    sign, flip = jnp.where(back, -1, 1), jnp.where(back, tiles - 1, 0)
    origin = jnp.where(back, tiles - 1 + base, -base)
    return lambda j, p: sign * table[j, sign * p + flip] + origin


def stacked(state, place, p, shift, pairs):
    return jnp.concatenate([state[rows_of(place(j, p) + shift), :] for j in range(pairs)], axis=0)


def product(blocks, state):
    return jnp.dot(blocks, state, preferred_element_type=jnp.float32).astype(jnp.bfloat16)


def blocks_at(parts, cuts, p):
    k = max(k for k in range(len(cuts) - 1) if cuts[k] <= p)
    return parts[k][rows_of(p - cuts[k]), :]


def prepare(cuts, k, pairs, tiles, table, transfer):
    begin, end = cuts[k], cuts[k + 1]
    groups = [(p, min(GROUP, end - p)) for p in range(begin, end, GROUP)]
    edges = [range(REACH)] * (k == 0) + [range(tiles - REACH, tiles)] * (end == tiles)

    def kernel(table, source, packed, *rest):
        *edge_refs, landed, arrived = rest
        back = reversed_here()
        place = places(table, tiles)
        copies = []
        for g, (p, size) in enumerate(groups):
            start = jnp.where(back, tiles - p - size, p)
            copies.append(pltpu.make_async_copy(source.at[rows_of(start, size)], landed.at[rows_of(p - begin, size)], arrived.at[g]))
            copies[-1].start()
        for edge in edge_refs:
            edge[...] = jnp.zeros_like(edge)
        for g, (p, size) in enumerate(groups):
            copies[g].wait()
            for i in range(size):
                at = p - begin + jnp.where(back, size - 1 - i, i)
                split = jnp.swapaxes(landed[rows_of(at)], 0, 1)
                for j in range(pairs):
                    packed[rows_of(p + i - begin), j * TILE : (j + 1) * TILE] = split[j]
                for edge, span in zip(edge_refs, edges):
                    if p + i in span:
                        for j in range(pairs):
                            edge[rows_of(span.index(p + i)), rows_of(REACH - place(j, p + i) + p + i)] = split[j]

    size = end - begin
    return pl.pallas_call(
        kernel,
        in_specs=[SMEM, HBM],
        out_specs=[VMEM] * (1 + len(edges)),
        out_shape=[tile_rows(size, pairs * TILE)] + [tile_rows(REACH, BAND * TILE)] * len(edges),
        scratch_shapes=[pltpu.VMEM((size * TILE, pairs, TILE), jnp.bfloat16), pltpu.SemaphoreType.DMA((len(groups),))],
        compiler_params=params(),
        cost_estimate=cost(1e11 * size / tiles),
        name="prepare",
    )(table, pltpu.with_memory_space_constraint(transfer, pltpu.HBM))


def pair_step(step, k, tiles, pairs, cuts, inner, outer, tables, own, odd, edges, arrived, keeps):
    count = len(own)
    head, tail = k == 0, k == count - 1
    edges = edges[:1] * head + edges[1:] * tail
    bond = keeps[0].shape[1] if keeps else arrived[0].shape[1]
    begin, end = inner[k], inner[k + 1]
    emit = outer is not None
    out = (outer[k], outer[k + 1]) if emit else None
    begin_odd, end_odd = 0 if head else begin - REACH, tiles if tail else end - REACH
    odd_parts = [i for i in range(count) if cuts[i] < end_odd and cuts[i + 1] > begin_odd]
    own_parts = [i for i in range(count) if emit and cuts[i] < out[1] and cuts[i + 1] > out[0]]
    fixed = [*(own[i] for i in own_parts), *(odd[i] for i in odd_parts), *edges]
    first = 2 + len(fixed) + len(arrived)

    def kernel(table, odd_table, *refs):
        own_refs = dict(zip(own_parts, refs))
        odd_refs = dict(zip(odd_parts, refs[len(own_parts) :]))
        edge_refs = refs[len(own_parts) + len(odd_parts) : len(fixed)]
        came = refs[len(fixed) : first - 2]
        kept, wide, *outs = refs[first - 2 + len(keeps) :]
        kind = kind_here()
        place, odd_place = places(table, tiles), places(odd_table, tiles)

        def take_first():
            low, right, high = came
            back = reversed_here()
            for m in range(WIDE):
                wide[rows_of(jnp.where(back, tiles + 2 * WIDE - 1 - m, m)), :] = low[rows_of(m), :]
                wide[rows_of(jnp.where(back, WIDE - 1 - m, tiles + WIDE + m)), :] = high[rows_of(m), :]
            for p in range(tiles):
                wide[rows_of(WIDE + p), :] = right[rows_of(jnp.where(back, tiles - 1 - p, p)), :]

        @pl.when(kind == 2 * step)
        def _():
            if step > 0:
                wide[rows_of(WIDE + begin, end - begin), :] = came[0][...]
                for m in range(WIDE):
                    if head:
                        wide[rows_of(WIDE - 1 - m), :] = came[1][rows_of(m), :]
                    if tail:
                        wide[rows_of(tiles + 2 * WIDE - 1 - m), :] = came[-1][rows_of(m), :]
            elif head:
                take_first()
            for e in range(REACH):
                if head:
                    kept[rows_of(REACH - 1 - e), :] = product(edge_refs[0][rows_of(e), :], wide[rows_of(WIDE - 1 - e - REACH, BAND), :])
                if tail:
                    at = tiles + REACH - 1 - e
                    kept[rows_of(REACH + at), :] = product(edge_refs[-1][rows_of(e), :], wide[rows_of(WIDE + at - REACH, BAND), :])
            for p in range(begin_odd, end_odd):
                kept[rows_of(REACH + p), :] = product(blocks_at(odd_refs, cuts, p), stacked(wide, odd_place, p, WIDE, pairs))
            for p in range(*(out or (0, 0))):
                fresh = product(blocks_at(own_refs, cuts, p), stacked(kept, place, p, REACH, pairs))
                outs[0][rows_of(p - out[0]), :] = fresh
                if p < WIDE:
                    outs[1][rows_of(p), :] = fresh
                if p >= tiles - WIDE:
                    outs[-1][rows_of(p - (tiles - WIDE)), :] = fresh

        if step == 0 and head:

            @pl.when(kind == 1)
            def _():
                take_first()
                kept[...] = wide[rows_of(REACH, tiles + 2 * REACH), :]

    outs = [tile_rows(tiles + 2 * REACH, bond), tile_rows(tiles + 2 * WIDE, bond)]
    if emit:
        outs += [tile_rows(out[1] - out[0], bond)] + [tile_rows(WIDE, bond)] * (head + tail)
    return pl.pallas_call(
        kernel,
        in_specs=[SMEM] * 2 + [VMEM] * (first - 2 + len(keeps)),
        out_specs=[VMEM] * len(outs),
        out_shape=outs,
        input_output_aliases={first + i: i for i in range(len(keeps))},
        compiler_params=params(),
        cost_estimate=cost(1e10 * (end - begin) / tiles),
        name="pair_step",
    )(*tables, *fixed, *arrived, *keeps)


def finish(tiles, pairs, cuts, table, own, given, left, state):
    bond = state.shape[1]
    count = len(own)
    groups = [(p, GROUP) for p in range(0, tiles, GROUP)]

    def kernel(table, *refs):
        own_refs = refs[:count]
        given, rows, old, kept, env, grad, staged, sent = refs[count:]
        kind = kind_here()

        @pl.when((kind % 2 == 1) & (kind > 1))
        def _():
            kept[...] = given[rows_of(REACH, tiles + 2 * REACH), :]

        place = places(table, tiles)
        back = reversed_here()
        copies = []
        for g, (p, size) in enumerate(groups):
            start = jnp.where(back, tiles - p - size, p)
            for i in range(size):
                inside = jnp.where(back, size - 1 - i, i)
                sources = stacked(kept, place, p + i, REACH, pairs)
                env[rows_of(start + inside), :] = product(blocks_at(own_refs, cuts, p + i), sources)
                block = lax.dot_general(
                    rows[rows_of(start + inside), :], sources, (((1,), (1,)), ((), ())), preferred_element_type=jnp.float32
                ).astype(jnp.bfloat16)
                block = jnp.stack([block[:, j * TILE : (j + 1) * TILE] for j in range(pairs)], axis=0)
                staged[rows_of(p + inside)] = jnp.swapaxes(block, 0, 1)
            copies.append(pltpu.make_async_copy(staged.at[rows_of(p, size)], grad.at[rows_of(start, size)], sent.at[g]))
            copies[-1].start()
        for copy in copies:
            copy.wait()

    grad = jax.ShapeDtypeStruct((tiles * TILE, pairs, TILE), jnp.bfloat16)
    operands = [*own, given, left, state]
    _, env, grad = pl.pallas_call(
        kernel,
        in_specs=[SMEM] + [VMEM] * len(operands),
        out_specs=[VMEM, VMEM, HBM],
        out_shape=[tile_rows(tiles + 2 * REACH, bond), tile_rows(tiles, bond), grad],
        input_output_aliases={len(operands): 0},
        scratch_shapes=[pltpu.VMEM(grad.shape, jnp.bfloat16), pltpu.SemaphoreType.DMA((len(groups),))],
        compiler_params=params(),
        cost_estimate=cost(5e10),
        name="finish",
    )(table, *operands)
    return env, grad


def limits(tiles, crossings):
    room = WIDE * crossings
    ends = [e for e in (3 * tiles // 8, 3 * tiles // 4) if room <= e <= tiles - WIDE]
    return ends or ([tiles - WIDE] if room <= tiles - WIDE else [])


def per_device(env_right, transfer, sources, env_left):
    ncol, nsec = lax.axis_size("col"), lax.axis_size("sec")
    layers = ncol // 2
    blocks = transfer[0, 0]
    length, pairs = blocks.shape[0], blocks.shape[1]
    tiles = length // TILE
    right, left = env_right[0], env_left[0, 0]

    def move(value, hops):
        both = [(a * nsec + s, b * nsec + to(s)) for a, b, to in hops for s in range(nsec) if 0 <= to(s) < nsec]
        return lax.ppermute(value, ("col", "sec"), both)

    def same(s):
        return s

    swap = [(c, c ^ 1, same) for c in range(ncol)]
    top = ncol - 1

    low = move(right[-WIDE * TILE :], [(c - 2, c, lambda s: s + 1) for c in (top - 1, top)])
    high = move(right[: WIDE * TILE], [(c - 2, c, lambda s: s - 1) for c in (top - 1, top)])

    table = sources[0, 0].T

    ends = limits(tiles, layers - 1)
    count = len(ends) + 1
    cuts = [0] + [e + WIDE - REACH for e in ends] + [tiles]
    own, edges = [], []
    for k in range(count):
        part, *edge = prepare(cuts, k, pairs, tiles, table, blocks)
        own.append(part)
        edges += edge
    odd_cols = [(2 * z + 1, 2 * z) for z in range(layers)]
    odd = [move(part, [(a, b, same) for a, b in odd_cols]) for part in own]
    odd_table = move(table, [(a, b, same) for a, b in odd_cols])
    odd_edges = [move(edges[0], [(a, b, partner) for a, b in odd_cols]), move(edges[1], [(a, b, other) for a, b in odd_cols])]

    keeps = []
    sent = None
    for step in range(layers):
        end = step == layers - 1
        inner = [0] + [e - WIDE * (step - 1) for e in ends] + [tiles]
        outer = None if end else [0] + [e - WIDE * step for e in ends] + [tiles]
        above, here = 2 * (layers - step), 2 * (layers - 1 - step)
        leaving = []
        for k in range(count):
            if step == 0:
                came = [low, right, high] if k == 0 else []
            else:
                came = [move(sent[k][0], [(above, here, same)])]
                tail = sent[k][1:]
                if k == 0:
                    came.append(move(tail[0], [(above, here, partner)]))
                if k == count - 1:
                    came.append(move(tail[-1], [(above, here, other)]))
            result = pair_step(step, k, tiles, pairs, cuts, inner, outer, [table, odd_table], own, odd, odd_edges, came, keeps)
            keeps = result[:2]
            leaving.append(result[2:])
        sent = leaving

    given = move(keeps[1], swap)
    env, grad = finish(tiles, pairs, cuts, table, own, given, left, keeps[0])
    return env[None, None], grad[None, None]


def solution(mesh):
    placed = (
        P(None, "sec", None),
        P("col", None, "sec", None, None),
        P("col", None, "sec", None),
        P("col", None, "sec", None),
    )
    return jax.shard_map(
        per_device,
        mesh=mesh,
        in_specs=placed,
        out_specs=(P("col", None, "sec", None), P("col", None, "sec", None, None)),
        check_vma=False,
    )
```

time: 286 us -> 83.1 us (0.29)
  waiting for transfers between devices: 122 us -> 2.72 us
  local copies, waits for them, and re-layouts: 48.6 us -> 1.68 us
  matrix products: 41.5 us -> 0 us
  Pallas kernels: 0 us -> 20.2 us
  starting transfers between devices: 67.8 us -> 56.6 us
    ppermute x24, waiting for transfers between devices: 122 us -> 2.72 us  [move(): return lax.ppermute(value, ('col', 'sec'), both)]
    dot_general x9 -> x0, matrix products: 41.5 us -> none  [the longest x8 37.6 us: advance(): jnp.einsum('rtopq,rtpqk->rtok', blocks, picked, preferred_element_type=jn...]
    gather x32 -> x0, local copies, waits for them, and re-layouts: 26.4 us -> none  [one_row(): return row_blocks[row_sources]]
    unnamed x5 -> x6, local copies, waits for them, and re-layouts: 21.7 us -> 0.69 us
    pallas_call x0 -> x16, Pallas kernels: none -> 20.2 us  [the longest x3 7.73 us: prepare(): pl.pallas_call(kernel, in_specs=[SMEM, HBM], out_specs=[VMEM] * (1 + len(...]
    ppermute x24, starting transfers between devices: 67.8 us -> 56.6 us  [move(): return lax.ppermute(value, ('col', 'sec'), both)]
  transfers between devices with their start and end apart: 24 -> 24, of which waited for: 16 -> 1; matrix products, arithmetic and copies ran while one was open for 1% -> 1% of each run, Pallas kernels for 0% -> 18%
where the time goes in v2:
time: 83.1 us; the launch traced here: 82.5 us
  starting transfers between devices  56.6 us (68%)
  Pallas kernels  20.2 us (24%)
  waiting for transfers between devices  2.72 us (3%)
  local copies, waits for them, and re-layouts  1.68 us (2%)
  between operations  1.31 us (2%)
    ppermute x24, starting transfers between devices, move(): return lax.ppermute(value, ('col', 'sec'), both)  56.6 us
    pallas_call x3, Pallas kernels, prepare(): pl.pallas_call(kernel, in_specs=[SMEM, HBM], out_specs=[VMEM] * (1 + len(...  7.73 us
    pallas_call x12, Pallas kernels, pair_step(): pl.pallas_call(kernel, in_specs=[SMEM] * 2 + [VMEM] * (first - 2 + len(ke...  7.45 us
    pallas_call x1, Pallas kernels, finish(): pl.pallas_call(kernel, in_specs=[SMEM] + [VMEM] * len(operands), out_spec...  5.01 us
    ppermute x24, waiting for transfers between devices, move(): return lax.ppermute(value, ('col', 'sec'), both)  2.72 us
  transfers between devices with their start and end apart: 24, of which 1 were waited for; matrix products, arithmetic and copies ran while one was open for 1% of the time, Pallas kernels for 18%

profile of v2, /device:TPU:3, one launch (start us, length us, event | category | flops | bytes accessed | tf_op | source)
XLA Modules:
  0.0 82.5 jit_solution(17957100617592271909)
XLA Ops:
  0.6 2.6 %collective-permute-start = (s32[4,32]{1,0:T(4,128)}, s32[4,32]{1,0:T(4,128)S(1)}, u32[]{:S(2)}, u32[]{:S(2)}) collective-permute-start(s32[4,32]{1,0:T(4,128)} %bitcast.13), channel_id=1, source_target_pairs={{4,0},{5,1},{6,2},{7,3},{12,8},{13,9},{14,10},{15,11},{20,16},{21,... | collective-permute-start | bytes 1544 | tf_op jit(solution)/shard_map/ppermute | solution.py:262
  3.2 1.0 %slice_bitcast_fusion = (bf16[512,128]{1,0:T(8,128)(2,1)S(1)}, bf16[512,128]{1,0:T(8,128)(2,1)S(1)}) fusion(bf16[1,4096,128]{2,1,0:T(8,128)(2,1)} %param.4), kind=kLoop, calls=%fused_computation | loop fusion | bytes 524288 | tf_op jit(solution)/shard_map/slice | solution.py:271
  4.2 0.7 collective-permute-start.7
  4.9 0.7 collective-permute-start.6
  5.6 0.0 copy-start.1
  5.6 0.7 copy-done.1
  6.2 2.9 %prepare.3 = (bf16[1792,512]{1,0:T(8,128)(2,1)S(1)}, bf16[256,640]{1,0:T(8,128)(2,1)S(1)}) custom-call(s32[4,32]{1,0:T(4,128)S(1)} %bitcast.14, bf16[4096,4,128]{2,1,0:T(4,128)(2,1)} %bitcast.31), custom_call_target="tpu_custom_call" | custom-call | flops 43749998592 | tf_op jit(solution)/shard_map/prepare/pallas_call | solution.py:104
  9.1 1.4 %collective-permute-start.4 = (bf16[1792,512]{1,0:T(8,128)(2,1)S(1)}, bf16[1792,512]{1,0:T(8,128)(2,1)S(1)}, u32[]{:S(2)}, u32[]{:S(2)}) collective-permute-start(bf16[1792,512]{1,0:T(8,128)(2,1)S(1)} %get-tuple-element.47.refs_0_), channel_id=1, source_target_pairs={{4,0},{5,1},{6,2},{7,3},{12,8},{13,9},{14,10},{15,11},{20,16},{21,... | collective-permute-start | bytes 5505032 | tf_op jit(solution)/shard_map/ppermute | solution.py:262
  10.6 2.7 %prepare.4.refs_1_.refs_0_ = bf16[1536,512]{1,0:T(8,128)(2,1)S(1)} custom-call(s32[4,32]{1,0:T(4,128)S(1)} %bitcast.15, bf16[4096,4,128]{2,1,0:T(4,128)(2,1)} %bitcast.32), custom_call_target="tpu_custom_call" | custom-call | flops 37499998208 | tf_op jit(solution)/shard_map/prepare/pallas_call | solution.py:104
  13.2 1.4 %collective-permute-start.1 = (bf16[1536,512]{1,0:T(8,128)(2,1)S(1)}, bf16[1536,512]{1,0:T(8,128)(2,1)S(1)}, u32[]{:S(2)}, u32[]{:S(2)}) collective-permute-start(bf16[1536,512]{1,0:T(8,128)(2,1)S(1)} %prepare.4.refs_1_.refs_0_), channel_id=1, source_target_pairs={{4,0},{5,1},{6,2},{7,3},{12,8},{13,9},{14,10},{15,11},{20,16},{21,... | collective-permute-start | bytes 4718600 | tf_op jit(solution)/shard_map/ppermute | solution.py:262
  14.6 0.0 copy-start
  14.6 1.4 %collective-permute-start.5 = (bf16[256,640]{1,0:T(8,128)(2,1)S(1)}, bf16[256,640]{1,0:T(8,128)(2,1)S(1)}, u32[]{:S(2)}, u32[]{:S(2)}) collective-permute-start(bf16[256,640]{1,0:T(8,128)(2,1)S(1)} %get-tuple-element.50), channel_id=1, source_target_pairs={{4,1},{5,0},{6,3},{7,2},{12,9},{13,8},{14,11},{15,10},{20,17},{21,... | collective-permute-start | bytes 983048 | tf_op jit(solution)/shard_map/ppermute | solution.py:262
  16.1 2.2 %prepare.5 = (bf16[768,512]{1,0:T(8,128)(2,1)S(1)}, bf16[256,640]{1,0:T(8,128)(2,1)S(1)}) custom-call(s32[4,32]{1,0:T(4,128)S(1)} %bitcast.16, bf16[4096,4,128]{2,1,0:T(4,128)(2,1)} %bitcast.33), custom_call_target="tpu_custom_call" | custom-call | flops 18749999104 | tf_op jit(solution)/shard_map/prepare/pallas_call | solution.py:104
  18.3 2.2 %collective-permute-start.3 = (bf16[256,640]{1,0:T(8,128)(2,1)S(1)}, bf16[256,640]{1,0:T(8,128)(2,1)S(1)}, u32[]{:S(2)}, u32[]{:S(2)}) collective-permute-start(bf16[256,640]{1,0:T(8,128)(2,1)S(1)} %get-tuple-element.49), channel_id=1, source_target_pairs={{5,2},{6,1},{13,10},{14,9},{21,18},{22,17},{29,26},{30,25}} | collective-permute-start | bytes 983048 | tf_op jit(solution)/shard_map/ppermute | solution.py:262
  20.5 0.0 collective-permute-done.6.refs_3_
  20.5 1.3 %collective-permute-start.2 = (bf16[768,512]{1,0:T(8,128)(2,1)S(1)}, bf16[768,512]{1,0:T(8,128)(2,1)S(1)}, u32[]{:S(2)}, u32[]{:S(2)}) collective-permute-start(bf16[768,512]{1,0:T(8,128)(2,1)S(1)} %get-tuple-element.48.refs_1_.refs_2_), channel_id=1, source_target_pairs={{4,0},{5,1},{6,2},{7,3},{12,8},{13,9},{14,10},{15,11},{20,16},{21,... | collective-permute-start | bytes 2359304 | tf_op jit(solution)/shard_map/ppermute | solution.py:262
  21.8 0.0 collective-permute-done.4.refs_1_.refs_2_.refs_0_
  21.9 0.6 pair_step.12
  22.5 0.7 collective-permute-start.12
  23.2 0.7 collective-permute-start.11
  23.9 0.6 pair_step.13
  24.5 0.7 collective-permute-start.10
  25.2 0.6 pair_step.14
  25.9 0.7 collective-permute-start.9
  26.5 0.7 collective-permute-start.8
  27.2 0.6 pair_step.15
  27.9 0.7 collective-permute-start.17
  28.5 0.7 collective-permute-start.16
  29.2 0.6 pair_step.16
  29.9 0.7 collective-permute-start.15
  30.6 0.6 pair_step.17
  31.2 0.8 %collective-permute-start.14 = (bf16[512,128]{1,0:T(8,128)(2,1)S(1)}, bf16[512,128]{1,0:T(8,128)(2,1)S(1)}, u32[]{:S(2)}, u32[]{:S(2)}) collective-permute-start(bf16[512,128]{1,0:T(8,128)(2,1)S(1)} %get-tuple-element.67), channel_id=1, source_target_pairs={{17,10},{18,9}} | collective-permute-start | bytes 393224 | tf_op jit(solution)/shard_map/ppermute | solution.py:262
  32.1 0.7 collective-permute-start.13
  32.8 0.6 pair_step.18
  33.4 0.7 collective-permute-start.21
  34.1 0.7 collective-permute-start.22
  34.8 0.6 pair_step.19
  35.4 0.7 collective-permute-start.20
  36.1 0.6 pair_step.20
  36.8 0.7 collective-permute-start.18
  37.5 0.7 collective-permute-start.19
  38.2 0.6 pair_step.21
  38.8 0.6 pair_step.22
  39.4 0.0 copy-start.2
  39.4 0.6 pair_step.23
  40.1 34.6 %collective-permute-start.23 = (bf16[5120,128]{1,0:T(8,128)(2,1)S(1)}, bf16[5120,128]{1,0:T(8,128)(2,1)S(1)}, u32[]{:S(2)}, u32[]{:S(2)}) collective-permute-start(bf16[5120,128]{1,0:T(8,128)(2,1)S(1)} %get-tuple-element.88), channel_id=1, source_target_pairs={{0,4},{1,5},{2,6},{3,7},{4,0},{5,1},{6,2},{7,3},{8,12},{9,13},{10,... | collective-permute-start | bytes 3932168 | tf_op jit(solution)/shard_map/ppermute | solution.py:262
  74.7 2.7 %collective-permute-done.23.refs_3_ = bf16[5120,128]{1,0:T(8,128)(2,1)S(1)} collective-permute-done((bf16[5120,128]{1,0:T(8,128)(2,1)S(1)}, bf16[5120,128]{1,0:T(8,128)(2,1)S(1)}, u32[]{:S(2)}, u32[]{:S(2)}) %collective-permute-start.23) | collective-permute-done | bytes 1310752 | tf_op jit(solution)/shard_map/ppermute | solution.py:262
  77.3 5.0 %finish.1 = (bf16[4608,128]{1,0:T(8,128)(2,1)S(1)}, bf16[4096,128]{1,0:T(8,128)(2,1)}, bf16[4096,4,128]{2,1,0:T(4,128)(2,1)}) custom-call(s32[4,32]{1,0:T(4,128)S(1)} %bitcast.29, bf16[1792,512]{1,0:T(8,128)(2,1)S(1)} %get-tuple-element.47.refs_0_, bf16[1536,512]{1,0:T(8,128)(2,1)S(1)} %prepare.4.refs_1_.refs_0_, ...), custom_call_target="tpu_custom_call", output_to_operand_aliasing={{0}: (6, {})} | custom-call | flops 49999998976 | tf_op jit(solution)/shard_map/finish/pallas_call | solution.py:232
  (23 shorter events, 0.1 us)
Async XLA Ops:
  0.6 14.0 %collective-permute-start = (s32[4,32]{1,0:T(4,128)}, s32[4,32]{1,0:T(4,128)S(1)}, u32[]{:S(2)}, u32[]{:S(2)}) collective-permute-start(s32[4,32]{1,0:T(4,128)} %bitcast.13), channel_id=1, source_target_pairs={{4,0},{5,1},{6,2},{7,3},{12,8},{13,9},{14,10},{15,11},{20,16},{21,... | collective-permute-start | bytes 1544 | tf_op jit(solution)/shard_map/ppermute | solution.py:262
  4.2 14.1 %collective-permute-start.7 = (bf16[512,128]{1,0:T(8,128)(2,1)S(1)}, bf16[512,128]{1,0:T(8,128)(2,1)S(1)}, u32[]{:S(2)}, u32[]{:S(2)}) collective-permute-start(bf16[512,128]{1,0:T(8,128)(2,1)S(1)} %get-tuple-element.92), channel_id=1, source_target_pairs={{17,24},{18,25},{19,26},{21,28},{22,29},{23,30}} | collective-permute-start | bytes 393224 | tf_op jit(solution)/shard_map/ppermute | solution.py:262
  4.9 15.6 %collective-permute-start.6 = (bf16[512,128]{1,0:T(8,128)(2,1)S(1)}, bf16[512,128]{1,0:T(8,128)(2,1)S(1)}, u32[]{:S(2)}, u32[]{:S(2)}) collective-permute-start(bf16[512,128]{1,0:T(8,128)(2,1)S(1)} %get-tuple-element.93), channel_id=1, source_target_pairs={{16,25},{17,26},{18,27},{20,29},{21,30},{22,31}} | collective-permute-start | bytes 393224 | tf_op jit(solution)/shard_map/ppermute | solution.py:262
  5.6 0.7 copy-start.1
  9.1 12.7 %collective-permute-start.4 = (bf16[1792,512]{1,0:T(8,128)(2,1)S(1)}, bf16[1792,512]{1,0:T(8,128)(2,1)S(1)}, u32[]{:S(2)}, u32[]{:S(2)}) collective-permute-start(bf16[1792,512]{1,0:T(8,128)(2,1)S(1)} %get-tuple-element.47.refs_0_), channel_id=1, source_target_pairs={{4,0},{5,1},{6,2},{7,3},{12,8},{13,9},{14,10},{15,11},{20,16},{21,... | collective-permute-start | bytes 5505032 | tf_op jit(solution)/shard_map/ppermute | solution.py:262
  13.2 10.7 %collective-permute-start.1 = (bf16[1536,512]{1,0:T(8,128)(2,1)S(1)}, bf16[1536,512]{1,0:T(8,128)(2,1)S(1)}, u32[]{:S(2)}, u32[]{:S(2)}) collective-permute-start(bf16[1536,512]{1,0:T(8,128)(2,1)S(1)} %prepare.4.refs_1_.refs_0_), channel_id=1, source_target_pairs={{4,0},{5,1},{6,2},{7,3},{12,8},{13,9},{14,10},{15,11},{20,16},{21,... | collective-permute-start | bytes 4718600 | tf_op jit(solution)/shard_map/ppermute | solution.py:262
  14.6 7.2 %copy-start = (bf16[1,4096,128]{2,1,0:T(8,128)(2,1)S(1)}, bf16[1,4096,128]{2,1,0:T(8,128)(2,1)}, u32[]{:S(2)}) copy-start(bf16[1,4096,128]{2,1,0:T(8,128)(2,1)} %param.4) | copy-start | bytes 3145732
  14.6 7.2 %collective-permute-start.5 = (bf16[256,640]{1,0:T(8,128)(2,1)S(1)}, bf16[256,640]{1,0:T(8,128)(2,1)S(1)}, u32[]{:S(2)}, u32[]{:S(2)}) collective-permute-start(bf16[256,640]{1,0:T(8,128)(2,1)S(1)} %get-tuple-element.50), channel_id=1, source_target_pairs={{4,1},{5,0},{6,3},{7,2},{12,9},{13,8},{14,11},{15,10},{20,17},{21,... | collective-permute-start | bytes 983048 | tf_op jit(solution)/shard_map/ppermute | solution.py:262
  18.3 6.9 %collective-permute-start.3 = (bf16[256,640]{1,0:T(8,128)(2,1)S(1)}, bf16[256,640]{1,0:T(8,128)(2,1)S(1)}, u32[]{:S(2)}, u32[]{:S(2)}) collective-permute-start(bf16[256,640]{1,0:T(8,128)(2,1)S(1)} %get-tuple-element.49), channel_id=1, source_target_pairs={{5,2},{6,1},{13,10},{14,9},{21,18},{22,17},{29,26},{30,25}} | collective-permute-start | bytes 983048 | tf_op jit(solution)/shard_map/ppermute | solution.py:262
  20.5 4.7 %collective-permute-start.2 = (bf16[768,512]{1,0:T(8,128)(2,1)S(1)}, bf16[768,512]{1,0:T(8,128)(2,1)S(1)}, u32[]{:S(2)}, u32[]{:S(2)}) collective-permute-start(bf16[768,512]{1,0:T(8,128)(2,1)S(1)} %get-tuple-element.48.refs_1_.refs_2_), channel_id=1, source_target_pairs={{4,0},{5,1},{6,2},{7,3},{12,8},{13,9},{14,10},{15,11},{20,16},{21,... | collective-permute-start | bytes 2359304 | tf_op jit(solution)/shard_map/ppermute | solution.py:262
  22.5 4.7 %collective-permute-start.12 = (bf16[512,128]{1,0:T(8,128)(2,1)S(1)}, bf16[512,128]{1,0:T(8,128)(2,1)S(1)}, u32[]{:S(2)}, u32[]{:S(2)}) collective-permute-start(bf16[512,128]{1,0:T(8,128)(2,1)S(1)} %get-tuple-element.59), channel_id=1, source_target_pairs={{24,17},{25,16},{26,19},{27,18}} | collective-permute-start | bytes 393224 | tf_op jit(solution)/shard_map/ppermute | solution.py:262
  23.2 4.0 %collective-permute-start.11 = (bf16[1536,128]{1,0:T(8,128)(2,1)S(1)}, bf16[1536,128]{1,0:T(8,128)(2,1)S(1)}, u32[]{:S(2)}, u32[]{:S(2)}) collective-permute-start(bf16[1536,128]{1,0:T(8,128)(2,1)S(1)} %get-tuple-element.58), channel_id=1, source_target_pairs={{24,16},{25,17},{26,18},{27,19}} | collective-permute-start | bytes 1179656 | tf_op jit(solution)/shard_map/ppermute | solution.py:262
  24.5 4.7 %collective-permute-start.10 = (bf16[1536,128]{1,0:T(8,128)(2,1)S(1)}, bf16[1536,128]{1,0:T(8,128)(2,1)S(1)}, u32[]{:S(2)}, u32[]{:S(2)}) collective-permute-start(bf16[1536,128]{1,0:T(8,128)(2,1)S(1)} %get-tuple-element.57), channel_id=1, source_target_pairs={{24,16},{25,17},{26,18},{27,19}} | collective-permute-start | bytes 1179656 | tf_op jit(solution)/shard_map/ppermute | solution.py:262
  25.9 4.7 %collective-permute-start.9 = (bf16[512,128]{1,0:T(8,128)(2,1)S(1)}, bf16[512,128]{1,0:T(8,128)(2,1)S(1)}, u32[]{:S(2)}, u32[]{:S(2)}) collective-permute-start(bf16[512,128]{1,0:T(8,128)(2,1)S(1)} %get-tuple-element.56), channel_id=1, source_target_pairs={{25,18},{26,17}} | collective-permute-start | bytes 393224 | tf_op jit(solution)/shard_map/ppermute | solution.py:262
  26.5 4.0 %collective-permute-start.8 = (bf16[1024,128]{1,0:T(8,128)(2,1)S(1)}, bf16[1024,128]{1,0:T(8,128)(2,1)S(1)}, u32[]{:S(2)}, u32[]{:S(2)}) collective-permute-start(bf16[1024,128]{1,0:T(8,128)(2,1)S(1)} %get-tuple-element.55), channel_id=1, source_target_pairs={{24,16},{25,17},{26,18},{27,19}} | collective-permute-start | bytes 786440 | tf_op jit(solution)/shard_map/ppermute | solution.py:262
  27.9 4.9 %collective-permute-start.17 = (bf16[512,128]{1,0:T(8,128)(2,1)S(1)}, bf16[512,128]{1,0:T(8,128)(2,1)S(1)}, u32[]{:S(2)}, u32[]{:S(2)}) collective-permute-start(bf16[512,128]{1,0:T(8,128)(2,1)S(1)} %get-tuple-element.70), channel_id=1, source_target_pairs={{16,9},{17,8},{18,11},{19,10}} | collective-permute-start | bytes 393224 | tf_op jit(solution)/shard_map/ppermute | solution.py:262
  28.5 4.2 %collective-permute-start.16 = (bf16[1024,128]{1,0:T(8,128)(2,1)S(1)}, bf16[1024,128]{1,0:T(8,128)(2,1)S(1)}, u32[]{:S(2)}, u32[]{:S(2)}) collective-permute-start(bf16[1024,128]{1,0:T(8,128)(2,1)S(1)} %get-tuple-element.69), channel_id=1, source_target_pairs={{16,8},{17,9},{18,10},{19,11}} | collective-permute-start | bytes 786440 | tf_op jit(solution)/shard_map/ppermute | solution.py:262
  29.9 4.9 %collective-permute-start.15 = (bf16[1536,128]{1,0:T(8,128)(2,1)S(1)}, bf16[1536,128]{1,0:T(8,128)(2,1)S(1)}, u32[]{:S(2)}, u32[]{:S(2)}) collective-permute-start(bf16[1536,128]{1,0:T(8,128)(2,1)S(1)} %get-tuple-element.68), channel_id=1, source_target_pairs={{16,8},{17,9},{18,10},{19,11}} | collective-permute-start | bytes 1179656 | tf_op jit(solution)/shard_map/ppermute | solution.py:262
  31.2 4.9 %collective-permute-start.14 = (bf16[512,128]{1,0:T(8,128)(2,1)S(1)}, bf16[512,128]{1,0:T(8,128)(2,1)S(1)}, u32[]{:S(2)}, u32[]{:S(2)}) collective-permute-start(bf16[512,128]{1,0:T(8,128)(2,1)S(1)} %get-tuple-element.67), channel_id=1, source_target_pairs={{17,10},{18,9}} | collective-permute-start | bytes 393224 | tf_op jit(solution)/shard_map/ppermute | solution.py:262
  32.1 4.0 %collective-permute-start.13 = (bf16[1536,128]{1,0:T(8,128)(2,1)S(1)}, bf16[1536,128]{1,0:T(8,128)(2,1)S(1)}, u32[]{:S(2)}, u32[]{:S(2)}) collective-permute-start(bf16[1536,128]{1,0:T(8,128)(2,1)S(1)} %get-tuple-element.66), channel_id=1, source_target_pairs={{16,8},{17,9},{18,10},{19,11}} | collective-permute-start | bytes 1179656 | tf_op jit(solution)/shard_map/ppermute | solution.py:262
  33.4 4.7 %collective-permute-start.21 = (bf16[512,128]{1,0:T(8,128)(2,1)S(1)}, bf16[512,128]{1,0:T(8,128)(2,1)S(1)}, u32[]{:S(2)}, u32[]{:S(2)}) collective-permute-start(bf16[512,128]{1,0:T(8,128)(2,1)S(1)} %get-tuple-element.80), channel_id=1, source_target_pairs={{8,0},{9,1},{10,2},{11,3}} | collective-permute-start | bytes 393224 | tf_op jit(solution)/shard_map/ppermute | solution.py:262
  34.1 4.1 %collective-permute-start.22 = (bf16[512,128]{1,0:T(8,128)(2,1)S(1)}, bf16[512,128]{1,0:T(8,128)(2,1)S(1)}, u32[]{:S(2)}, u32[]{:S(2)}) collective-permute-start(bf16[512,128]{1,0:T(8,128)(2,1)S(1)} %get-tuple-element.81), channel_id=1, source_target_pairs={{8,1},{9,0},{10,3},{11,2}} | collective-permute-start | bytes 393224 | tf_op jit(solution)/shard_map/ppermute | solution.py:262
  35.4 3.4 %collective-permute-start.20 = (bf16[1536,128]{1,0:T(8,128)(2,1)S(1)}, bf16[1536,128]{1,0:T(8,128)(2,1)S(1)}, u32[]{:S(2)}, u32[]{:S(2)}) collective-permute-start(bf16[1536,128]{1,0:T(8,128)(2,1)S(1)} %get-tuple-element.79), channel_id=1, source_target_pairs={{8,0},{9,1},{10,2},{11,3}} | collective-permute-start | bytes 1179656 | tf_op jit(solution)/shard_map/ppermute | solution.py:262
  36.8 2.7 %collective-permute-start.18 = (bf16[2048,128]{1,0:T(8,128)(2,1)S(1)}, bf16[2048,128]{1,0:T(8,128)(2,1)S(1)}, u32[]{:S(2)}, u32[]{:S(2)}) collective-permute-start(bf16[2048,128]{1,0:T(8,128)(2,1)S(1)} %get-tuple-element.77), channel_id=1, source_target_pairs={{8,0},{9,1},{10,2},{11,3}} | collective-permute-start | bytes 1572872 | tf_op jit(solution)/shard_map/ppermute | solution.py:262
  37.5 2.0 %collective-permute-start.19 = (bf16[512,128]{1,0:T(8,128)(2,1)S(1)}, bf16[512,128]{1,0:T(8,128)(2,1)S(1)}, u32[]{:S(2)}, u32[]{:S(2)}) collective-permute-start(bf16[512,128]{1,0:T(8,128)(2,1)S(1)} %get-tuple-element.78), channel_id=1, source_target_pairs={{9,2},{10,1}} | collective-permute-start | bytes 393224 | tf_op jit(solution)/shard_map/ppermute | solution.py:262
  39.4 37.9 %copy-start.2 = (bf16[1,1,4096,128]{3,2,1,0:T(8,128)(2,1)S(1)}, bf16[1,1,4096,128]{3,2,1,0:T(8,128)(2,1)}, u32[]{:S(2)}) copy-start(bf16[1,1,4096,128]{3,2,1,0:T(8,128)(2,1)} %param.7) | copy-start | bytes 3145732
  40.1 37.2 %collective-permute-start.23 = (bf16[5120,128]{1,0:T(8,128)(2,1)S(1)}, bf16[5120,128]{1,0:T(8,128)(2,1)S(1)}, u32[]{:S(2)}, u32[]{:S(2)}) collective-permute-start(bf16[5120,128]{1,0:T(8,128)(2,1)S(1)} %get-tuple-element.88), channel_id=1, source_target_pairs={{0,4},{1,5},{2,6},{3,7},{4,0},{5,1},{6,2},{7,3},{8,12},{9,13},{10,... | collective-permute-start | bytes 3932168 | tf_op jit(solution)/shard_map/ppermute | solution.py:262

commit v3 on v2

v3 whole, which is shorter than its diff:
```python
import jax
import jax.numpy as jnp
from jax import lax
from jax.experimental import pallas as pl
from jax.experimental.pallas import tpu as pltpu
from jax.sharding import PartitionSpec as P

TILE = 128
REACH = 2
WIDE = 2 * REACH
BAND = 2 * REACH + 1
GROUP = 4
PREPARE, FIRST, STEP, FINISH = 1e10, 2e10, 1e10, 4e9
VMEM = pl.BlockSpec(memory_space=pltpu.VMEM)
SMEM = pl.BlockSpec(memory_space=pltpu.SMEM)
HBM = pl.BlockSpec(memory_space=pltpu.HBM)


def params():
    return pltpu.CompilerParams(vmem_limit_bytes=16 * 1024 * 1024)


def cost(flops):
    return pl.CostEstimate(flops=int(flops), bytes_accessed=0, transcendentals=0)


def rows_of(tile, count=1):
    start = tile * TILE
    if not isinstance(start, int):
        start = pl.multiple_of(start, TILE)
    return pl.ds(start, count * TILE)


def tile_rows(count, width):
    return jax.ShapeDtypeStruct((count * TILE, width), jnp.bfloat16)


def kind_here():
    ncol, col = lax.axis_size("col"), lax.axis_index("col")
    return 2 * (ncol // 2 - 1 - col // 2) + col % 2


def reversed_here():
    return lax.axis_index("sec") % 2 == 0


def partner(s):
    return s + 1 if s % 2 == 0 else s - 1


def other(s):
    return s - 1 if s % 2 == 0 else s + 1


def places(table, tiles):
    back = reversed_here()
    base = lax.axis_index("sec") * tiles
    sign, flip = jnp.where(back, -1, 1), jnp.where(back, tiles - 1, 0)
    origin = jnp.where(back, tiles - 1 + base, -base)
    return lambda j, p: sign * table[j, sign * p + flip] + origin


def stacked(state, place, p, shift, pairs):
    return jnp.concatenate([state[rows_of(place(j, p) + shift), :] for j in range(pairs)], axis=0)


def product(blocks, state):
    return jnp.dot(blocks, state, preferred_element_type=jnp.float32).astype(jnp.bfloat16)


def blocks_at(parts, cuts, p):
    k = max(k for k in range(len(cuts) - 1) if cuts[k] <= p)
    return parts[k][rows_of(p - cuts[k]), :]


def prepare(first, final, cuts, pairs, table, transfer, right):
    tiles, bond = cuts[-1], right.shape[1]
    chosen = range(first, final)
    groups = [(p, min(GROUP, cuts[k + 1] - p)) for k in chosen for p in range(cuts[k], cuts[k + 1], GROUP)]
    begin, end = cuts[first], cuts[final]
    head, tail = first == 0, end == tiles
    spans = [range(WIDE)] * head + [range(tiles - WIDE, tiles)] * tail

    def kernel(table, source, environment, *refs):
        parts, refs = refs[: len(chosen)], refs[len(chosen) :]
        edges, refs = refs[: len(spans)], refs[len(spans) :]
        landed, halo, arrived, halo_arrived, placed = refs[-5:]
        back = reversed_here()
        place = places(table, tiles)
        copies, halos, whole = [], [], []
        for g, (p, size) in enumerate(groups):
            start = jnp.where(back, tiles - p - size, p)
            copies.append(pltpu.make_async_copy(source.at[rows_of(start, size)], landed.at[rows_of(p - begin, size)], arrived.at[g]))
        for e, span in enumerate(spans):
            start = jnp.where(back, tiles - span[0] - WIDE, span[0])
            halos.append(pltpu.make_async_copy(environment.at[rows_of(start, WIDE)], halo.at[e], halo_arrived.at[e]))
        if tail:
            for p in range(tiles):
                at = jnp.where(back, tiles - 1 - p, p)
                whole.append(pltpu.make_async_copy(environment.at[rows_of(at)], refs[0].at[rows_of(WIDE + p)], placed.at[p]))
        for copy in copies + halos + whole:
            copy.start()
        for edge in edges:
            edge[...] = jnp.zeros_like(edge)
        for g, (p, size) in enumerate(groups):
            copies[g].wait()
            k = max(k for k in chosen if cuts[k] <= p)
            for i in range(size):
                at = p - begin + jnp.where(back, size - 1 - i, i)
                split = jnp.swapaxes(landed[rows_of(at)], 0, 1)
                for j in range(pairs):
                    parts[k - first][rows_of(p + i - cuts[k]), j * TILE : (j + 1) * TILE] = split[j]
                for edge, span in zip(edges, spans):
                    near = span[:REACH] if span[0] == 0 else span[REACH:]
                    if p + i in near:
                        for j in range(pairs):
                            edge[rows_of(near.index(p + i)), rows_of(REACH - place(j, p + i) + p + i)] = split[j]
        for e, edge in enumerate(edges):
            halos[e].wait()
            for m in range(WIDE):
                at = jnp.where(back, WIDE - 1 - m, m)
                edge[rows_of(REACH), m * bond : (m + 1) * bond] = halo[e, rows_of(at), :]
        for copy in whole:
            copy.wait()

    outs = [tile_rows(cuts[k + 1] - cuts[k], pairs * TILE) for k in chosen] + [tile_rows(REACH + 1, BAND * TILE)] * len(spans)
    if tail:
        outs.append(tile_rows(tiles + 2 * WIDE, bond))
    return pl.pallas_call(
        kernel,
        in_specs=[SMEM, HBM, HBM],
        out_specs=[VMEM] * len(outs),
        out_shape=outs,
        scratch_shapes=[
            pltpu.VMEM(((end - begin) * TILE, pairs, TILE), jnp.bfloat16),
            pltpu.VMEM((len(spans), WIDE * TILE, bond), jnp.bfloat16),
            pltpu.SemaphoreType.DMA((len(groups),)),
            pltpu.SemaphoreType.DMA((len(spans),)),
            pltpu.SemaphoreType.DMA((tiles,)),
        ],
        compiler_params=params(),
        cost_estimate=cost(PREPARE * (end - begin) / tiles),
        name="prepare",
    )(table, *(pltpu.with_memory_space_constraint(value, pltpu.HBM) for value in (transfer, right)))


def pair_step(step, k, tiles, pairs, cuts, inner, outer, tables, own, odd, edges, arrived, keeps, give=()):
    count = len(own)
    head, tail = k == 0, k == count - 1
    edges = edges[:1] * head + edges[1:] * tail
    bond = keeps[-1].shape[1]
    begin, end = inner[k], inner[k + 1]
    emit = outer is not None
    out = (outer[k], outer[k + 1]) if emit else None
    begin_odd, end_odd = 0 if head else begin - REACH, tiles if tail else end - REACH
    odd_parts = [i for i in range(count) if cuts[i] < end_odd and cuts[i + 1] > begin_odd]
    own_parts = [i for i in range(count) if emit and cuts[i] < out[1] and cuts[i + 1] > out[0]]
    fixed = [*(own[i] for i in own_parts), *(odd[i] for i in odd_parts), *edges]
    first = 2 + len(fixed) + len(arrived)

    def kernel(table, odd_table, *refs):
        own_refs = dict(zip(own_parts, refs))
        odd_refs = dict(zip(odd_parts, refs[len(own_parts) :]))
        edge_refs = refs[len(own_parts) + len(odd_parts) : len(fixed)]
        came = refs[len(fixed) : first - 2]
        kept, wide, *outs = refs[first - 2 + len(keeps) :]
        kind = kind_here()
        place, odd_place = places(table, tiles), places(odd_table, tiles)

        @pl.when(kind == 2 * step)
        def _():
            if step > 0:
                wide[rows_of(WIDE + begin, end - begin), :] = came[0][...]
            for m in range(WIDE):
                if head:
                    value = came[1][rows_of(m), :] if step > 0 else edge_refs[0][rows_of(REACH), m * bond : (m + 1) * bond]
                    wide[rows_of(WIDE - 1 - m), :] = value
                if tail:
                    value = came[-1][rows_of(m), :] if step > 0 else edge_refs[-1][rows_of(REACH), m * bond : (m + 1) * bond]
                    wide[rows_of(tiles + 2 * WIDE - 1 - m), :] = value
            for e in range(REACH):
                if head:
                    kept[rows_of(REACH - 1 - e), :] = product(edge_refs[0][rows_of(e), :], wide[rows_of(WIDE - 1 - e - REACH, BAND), :])
                if tail:
                    at = tiles + REACH - 1 - e
                    kept[rows_of(REACH + at), :] = product(edge_refs[-1][rows_of(e), :], wide[rows_of(WIDE + at - REACH, BAND), :])
            for p in range(begin_odd, end_odd):
                kept[rows_of(REACH + p), :] = product(blocks_at(odd_refs, cuts, p), stacked(wide, odd_place, p, WIDE, pairs))
            for p in range(*(out or (0, 0))):
                fresh = product(blocks_at(own_refs, cuts, p), stacked(kept, place, p, REACH, pairs))
                outs[0][rows_of(p - out[0]), :] = fresh
                if p < WIDE:
                    outs[1][rows_of(p), :] = fresh
                if p >= tiles - WIDE:
                    outs[-1][rows_of(p - (tiles - WIDE)), :] = fresh

        if give:

            @pl.when(kind % 2 == 0)
            def _():
                for (low, high), out in zip(give, outs[len(outs) - len(give) :]):
                    out[...] = wide[rows_of(WIDE + low, high - low), :]

    outs = [tile_rows(tiles + 2 * REACH, bond), tile_rows(tiles + 2 * WIDE, bond)]
    if emit:
        outs += [tile_rows(out[1] - out[0], bond)] + [tile_rows(WIDE, bond)] * (head + tail)
    outs += [tile_rows(high - low, bond) for low, high in give]
    return pl.pallas_call(
        kernel,
        in_specs=[SMEM] * 2 + [VMEM] * (first - 2 + len(keeps)),
        out_specs=[VMEM] * len(outs),
        out_shape=outs,
        input_output_aliases={first + i: 2 - len(keeps) + i for i in range(len(keeps))},
        compiler_params=params(),
        cost_estimate=cost(STEP * (end - begin) / tiles if step or k else FIRST),
        name="pair_step",
    )(*tables, *fixed, *arrived, *keeps)


def finish(begin, end, tiles, pairs, cuts, table, own, given, regions, left, state, done):
    bond = state.shape[1]
    parts = [k for k in range(len(own)) if cuts[k] < end and cuts[k + 1] > begin]
    groups = [(p, min(GROUP, end - p)) for p in range(begin, end, GROUP)]
    refs_in = [*(own[k] for k in parts), *given, left, state, *done]
    count, fixed = len(parts), len(parts) + len(given) + 2

    def kernel(table, *refs):
        own_refs = dict(zip(parts, refs))
        *taken, rows = refs[count : fixed - 1]
        kept, env, grad, staged_env, staged, sent = refs[len(refs_in) :]

        @pl.when(kind_here() % 2 == 1)
        def _():
            for (low, high), value in zip(regions, taken):
                kept[rows_of(REACH + low, high - low), :] = value[...]

        place = places(table, tiles)
        back = reversed_here()
        copies = []
        for g, (p, size) in enumerate(groups):
            start = jnp.where(back, tiles - p - size, p)
            for i in range(size):
                inside = jnp.where(back, size - 1 - i, i)
                sources = stacked(kept, place, p + i, REACH, pairs)
                staged_env[rows_of(p - begin + inside), :] = product(blocks_at(own_refs, cuts, p + i), sources)
                block = lax.dot_general(
                    rows[rows_of(start + inside), :], sources, (((1,), (1,)), ((), ())), preferred_element_type=jnp.float32
                ).astype(jnp.bfloat16)
                block = jnp.stack([block[:, j * TILE : (j + 1) * TILE] for j in range(pairs)], axis=0)
                staged[rows_of(p - begin + inside)] = jnp.swapaxes(block, 0, 1)
            here, there = rows_of(p - begin, size), rows_of(start, size)
            copies.append(pltpu.make_async_copy(staged_env.at[here], env.at[there], sent.at[0, g]))
            copies.append(pltpu.make_async_copy(staged.at[here], grad.at[there], sent.at[1, g]))
            for copy in copies[-2:]:
                copy.start()
        for copy in copies:
            copy.wait()

    env = tile_rows(tiles, bond)
    grad = jax.ShapeDtypeStruct((tiles * TILE, pairs, TILE), jnp.bfloat16)
    size = (end - begin) * TILE
    return pl.pallas_call(
        kernel,
        in_specs=[SMEM] + [VMEM] * fixed + [HBM] * len(done),
        out_specs=[VMEM, HBM, HBM],
        out_shape=[tile_rows(tiles + 2 * REACH, bond), env, grad],
        input_output_aliases={fixed + i: i for i in range(1 + len(done))},
        scratch_shapes=[
            pltpu.VMEM((size, bond), jnp.bfloat16),
            pltpu.VMEM((size, pairs, TILE), jnp.bfloat16),
            pltpu.SemaphoreType.DMA((2, len(groups))),
        ],
        compiler_params=params(),
        cost_estimate=cost(FINISH * (end - begin) / tiles),
        name="finish",
    )(table, *refs_in)


def limits(tiles, crossings):
    room = WIDE * crossings
    ends = [e for e in (3 * tiles // 8, 3 * tiles // 4) if room <= e <= tiles - WIDE]
    return ends or [tiles - WIDE]


def per_device(env_right, transfer, sources, env_left):
    ncol, nsec = lax.axis_size("col"), lax.axis_size("sec")
    layers = ncol // 2
    blocks = transfer[0, 0]
    length, pairs = blocks.shape[0], blocks.shape[1]
    tiles = length // TILE
    right, left = env_right[0], env_left[0, 0]

    def move(value, hops):
        both = [(a * nsec + s, b * nsec + to(s)) for a, b, to in hops for s in range(nsec) if 0 <= to(s) < nsec]
        return lax.ppermute(value, ("col", "sec"), both)

    def same(s):
        return s

    swap = [(c, c ^ 1, same) for c in range(ncol)]

    table = sources[0, 0].T

    ends = limits(tiles, layers - 1)
    count = len(ends) + 1
    cuts = [0] + [e + WIDE - REACH for e in ends] + [tiles]
    head, first_edge = prepare(0, 1, cuts, pairs, table, blocks, right)
    *rest, last_edge, wide = prepare(1, count, cuts, pairs, table, blocks, right)
    own = [head, *rest]
    odd_cols = [(2 * z + 1, 2 * z) for z in range(layers)]
    odd = [move(part, swap) for part in own]
    odd_table = move(table, swap)
    odd_edges = [move(first_edge, [(a, b, partner) for a, b in odd_cols]), move(last_edge, [(a, b, other) for a, b in odd_cols])]

    keeps = [wide]
    sent = None
    for step in range(layers):
        end = step == layers - 1
        inner = [0] + [e - WIDE * (step - 1) for e in ends] + [tiles]
        outer = None if end else [0] + [e - WIDE * step for e in ends] + [tiles]
        above, here = 2 * (layers - step), 2 * (layers - 1 - step)
        leaving = []
        for k in range(count):
            came = []
            if step > 0:
                came = [move(sent[k][0], [(above, here, same)])]
                if k == 0:
                    came.append(move(sent[k][1], [(above, here, partner)]))
                if k == count - 1:
                    came.append(move(sent[k][-1], [(above, here, other)]))
            give = []
            if end and k == count - 2:
                middle = inner[k + 1] // 2
                give = [(-REACH, middle), (middle, inner[k + 1])]
            if end and k == count - 1:
                give = [(inner[k], tiles + REACH)]
            result = pair_step(step, k, tiles, pairs, cuts, inner, outer, [table, odd_table], own, odd, odd_edges, came, keeps, give)
            keeps = result[:2]
            if give:
                given = [move(value, swap) for value in result[len(result) - len(give) :]]
                if k == count - 2:
                    half = max(0, inner[k + 1] - WIDE) // GROUP * GROUP
                    state, *done = finish(0, half, tiles, pairs, cuts, table, own, given, give, left, keeps[0], [])
                    keeps = [state, keeps[1]]
                else:
                    _, env, grad = finish(half, tiles, tiles, pairs, cuts, table, own, given, give, left, keeps[0], done)
            leaving.append(result[2:])
        sent = leaving

    return env[None, None], grad[None, None]


def solution(mesh):
    placed = (
        P(None, "sec", None),
        P("col", None, "sec", None, None),
        P("col", None, "sec", None),
        P("col", None, "sec", None),
    )
    return jax.shard_map(
        per_device,
        mesh=mesh,
        in_specs=placed,
        out_specs=(P("col", None, "sec", None), P("col", None, "sec", None, None)),
        check_vma=False,
    )
```

time: 83.1 us -> 71 us (0.85)
  starting transfers between devices: 56.6 us -> 42.9 us
  waiting for transfers between devices: 2.72 us -> 4.59 us
  local copies, waits for them, and re-layouts: 1.68 us -> 0.68 us
    ppermute x24, starting transfers between devices: 56.6 us -> 42.9 us  [move(): return lax.ppermute(value, ('col', 'sec'), both)]
    ppermute x24, waiting for transfers between devices: 2.72 us -> 4.59 us  [move(): return lax.ppermute(value, ('col', 'sec'), both)]
    slice x1 -> x0, local copies, waits for them, and re-layouts: 0.99 us -> none  [per_device(): right[:WIDE * TILE]]
  transfers between devices with their start and end apart: 24 -> 24, of which waited for: 1 -> 3; matrix products, arithmetic and copies ran while one was open for 1% -> 0% of each run, Pallas kernels for 18% -> 19%
where the time goes in v3:
time: 71 us; the launch traced here: 69.9 us
  starting transfers between devices  42.9 us (60%)
  Pallas kernels  20.5 us (29%)
  waiting for transfers between devices  4.59 us (6%)
  between operations  1.22 us (2%)
    ppermute x24, starting transfers between devices, move(): return lax.ppermute(value, ('col', 'sec'), both)  42.9 us
    pallas_call x12, Pallas kernels, pair_step(): pl.pallas_call(kernel, in_specs=[SMEM] * 2 + [VMEM] * (first - 2 + len(ke...  7.63 us
    pallas_call x2, Pallas kernels, prepare(): pl.pallas_call(kernel, in_specs=[SMEM, HBM, HBM], out_specs=[VMEM] * len(...  7.21 us
    pallas_call x2, Pallas kernels, finish(): pl.pallas_call(kernel, in_specs=[SMEM] + [VMEM] * fixed + [HBM] * len(don...  5.67 us
    ppermute x24, waiting for transfers between devices, move(): return lax.ppermute(value, ('col', 'sec'), both)  4.59 us
  transfers between devices with their start and end apart: 24, of which 3 were waited for; matrix products, arithmetic and copies ran while one was open for 0% of the time, Pallas kernels for 19%

profile of v3, /device:TPU:3, one launch (start us, length us, event | category | flops | bytes accessed | tf_op | source)
XLA Modules:
  0.0 69.9 jit_solution(1013160196033248791)
XLA Ops:
  0.6 0.7 copy-done.1
  1.3 3.2 %prepare.2 = (bf16[1792,512]{1,0:T(8,128)(2,1)S(1)}, bf16[384,640]{1,0:T(8,128)(2,1)S(1)}) custom-call(s32[4,32]{1,0:T(4,128)S(1)} %bitcast.10, bf16[4096,4,128]{2,1,0:T(4,128)(2,1)} %bitcast.29, bf16[4096,128]{1,0:T(8,128)(2,1)} %bitcast.31), custom_call_target="tpu_custom_call" | custom-call | flops 4375000064 | tf_op jit(solution)/shard_map/prepare/pallas_call | solution.py:129
  4.5 0.7 %collective-permute-start.4 = (bf16[1792,512]{1,0:T(8,128)(2,1)S(1)}, bf16[1792,512]{1,0:T(8,128)(2,1)S(1)}, u32[]{:S(2)}, u32[]{:S(2)}) collective-permute-start(bf16[1792,512]{1,0:T(8,128)(2,1)S(1)} %get-tuple-element.54.refs_0_), channel_id=1, source_target_pairs={{0,4},{1,5},{2,6},{3,7},{4,0},{5,1},{6,2},{7,3},{8,12},{9,13},{10,... | collective-permute-start | bytes 5505032 | tf_op jit(solution)/shard_map/ppermute | solution.py:295
  5.3 0.1 collective-permute-start
  5.3 1.3 %collective-permute-start.5 = (bf16[384,640]{1,0:T(8,128)(2,1)S(1)}, bf16[384,640]{1,0:T(8,128)(2,1)S(1)}, u32[]{:S(2)}, u32[]{:S(2)}) collective-permute-start(bf16[384,640]{1,0:T(8,128)(2,1)S(1)} %get-tuple-element.58), channel_id=1, source_target_pairs={{4,1},{5,0},{6,3},{7,2},{12,9},{13,8},{14,11},{15,10},{20,17},{21,... | collective-permute-start | bytes 1474568 | tf_op jit(solution)/shard_map/ppermute | solution.py:295
  6.7 4.0 %prepare.3 = (bf16[1536,512]{1,0:T(8,128)(2,1)S(1)}, bf16[768,512]{1,0:T(8,128)(2,1)S(1)}, bf16[384,640]{1,0:T(8,128)(2,1)S(1)}, bf16[5120,128]{1,0:T(8,128)(2,1)S(1)}) custom-call(s32[4,32]{1,0:T(4,128)S(1)} %bitcast.12, bf16[4096,4,128]{2,1,0:T(4,128)(2,1)} %bitcast.30, bf16[4096,128]{1,0:T(8,128)(2,1)} %bitcast.32), custom_call_target="tpu_custom_call" | custom-call | flops 5624999936 | tf_op jit(solution)/shard_map/prepare/pallas_call | solution.py:129
  10.7 3.4 %collective-permute-start.3 = (bf16[384,640]{1,0:T(8,128)(2,1)S(1)}, bf16[384,640]{1,0:T(8,128)(2,1)S(1)}, u32[]{:S(2)}, u32[]{:S(2)}) collective-permute-start(bf16[384,640]{1,0:T(8,128)(2,1)S(1)} %get-tuple-element.57), channel_id=1, source_target_pairs={{5,2},{6,1},{13,10},{14,9},{21,18},{22,17},{29,26},{30,25}} | collective-permute-start | bytes 1474568 | tf_op jit(solution)/shard_map/ppermute | solution.py:295
  14.1 0.1 collective-permute-start.2
  14.2 0.0 collective-permute-done.odd_table
  14.2 0.5 collective-permute-start.1
  14.7 0.6 pair_step.12
  15.3 0.7 collective-permute-start.10
  16.0 0.7 collective-permute-start.9
  16.7 2.0 %collective-permute-done.1.refs_2_.refs_3_.refs_0_ = bf16[1536,512]{1,0:T(8,128)(2,1)S(1)} collective-permute-done((bf16[1536,512]{1,0:T(8,128)(2,1)S(1)}, bf16[1536,512]{1,0:T(8,128)(2,1)S(1)}, u32[]{:S(2)}, u32[]{:S(2)}) %collective-permute-start.1) | collective-permute-done | bytes 1572896 | tf_op jit(solution)/shard_map/ppermute | solution.py:295
  18.7 0.6 pair_step.13
  19.3 0.7 collective-permute-start.8
  20.1 0.6 pair_step.14
  20.7 0.7 collective-permute-start.7
  21.4 0.7 collective-permute-start.6
  22.0 0.0 collective-permute-done.10.refs_4_
  22.1 0.6 pair_step.15
  22.7 0.7 collective-permute-start.15
  23.4 0.7 collective-permute-start.14
  24.1 0.0 collective-permute-done.8.refs_4_
  24.1 0.6 pair_step.16
  24.7 0.7 collective-permute-start.13
  25.4 0.6 pair_step.17
  26.0 0.7 collective-permute-start.12
  26.7 0.7 collective-permute-start.11
  27.4 0.8 %pair_step.18 = (bf16[4608,128]{1,0:T(8,128)(2,1)S(1)}, bf16[5120,128]{1,0:T(8,128)(2,1)S(1)}, bf16[512,128]{1,0:T(8,128)(2,1)S(1)}, bf16[512,128]{1,0:T(8,128)(2,1)S(1)}) custom-call(s32[4,32]{1,0:T(4,128)S(1)} %bitcast.19, s32[4,32]{1,0:T(4,128)S(1)} %collective-permute-done.odd_table, ...), custom_call_target="tpu_custom_call", output_to_operand_aliasing={{0}: (7, {}), {1}: (8, {})} | custom-call | flops 2500000000 | tf_op jit(solution)/shard_map/pair_step/pallas_call | solution.py:208
  28.2 0.7 collective-permute-start.19
  28.9 0.7 collective-permute-start.20
  29.6 0.6 pair_step.19
  30.2 0.7 collective-permute-start.18
  30.9 0.6 pair_step.20
  31.6 0.7 collective-permute-start.16
  32.3 0.6 pair_step.21
  32.9 0.0 copy-start
  33.0 0.6 pair_step.22
  33.6 20.6 %collective-permute-start.21 = (bf16[1280,128]{1,0:T(8,128)(2,1)S(1)}, bf16[1280,128]{1,0:T(8,128)(2,1)S(1)}, u32[]{:S(2)}, u32[]{:S(2)}) collective-permute-start(bf16[1280,128]{1,0:T(8,128)(2,1)S(1)} %get-tuple-element.95), channel_id=1, source_target_pairs={{0,4},{1,5},{2,6},{3,7},{4,0},{5,1},{6,2},{7,3},{8,12},{9,13},{10,... | collective-permute-start | bytes 983048 | tf_op jit(solution)/shard_map/ppermute | solution.py:295
  54.2 0.1 collective-permute-start.22
  54.3 0.7 collective-permute-start.17
  54.9 0.9 %collective-permute-done.22.refs_2_ = bf16[1024,128]{1,0:T(8,128)(2,1)S(1)} collective-permute-done((bf16[1024,128]{1,0:T(8,128)(2,1)S(1)}, bf16[1024,128]{1,0:T(8,128)(2,1)S(1)}, u32[]{:S(2)}, u32[]{:S(2)}) %collective-permute-start.22) | collective-permute-done | bytes 262176 | tf_op jit(solution)/shard_map/ppermute | solution.py:295
  55.8 2.5 %finish.2 = (bf16[4608,128]{1,0:T(8,128)(2,1)S(1)}, bf16[4096,128]{1,0:T(8,128)(2,1)}, bf16[4096,4,128]{2,1,0:T(4,128)(2,1)}) custom-call(s32[4,32]{1,0:T(4,128)S(1)} %bitcast.24, bf16[1792,512]{1,0:T(8,128)(2,1)S(1)} %get-tuple-element.54.refs_0_, bf16[1280,128]{1,0:T(8,128)(2,1)S(1)} %collective-permute-done.21.refs_1_, ...), custom_call_target="tpu_custom_call", output_to_operand_aliasing={{0}: (5, {})} | custom-call | flops 1500000000 | tf_op jit(solution)/shard_map/finish/pallas_call | solution.py:262
  58.4 0.6 pair_step.23
  59.0 5.9 %collective-permute-start.23 = (bf16[2304,128]{1,0:T(8,128)(2,1)S(1)}, bf16[2304,128]{1,0:T(8,128)(2,1)S(1)}, u32[]{:S(2)}, u32[]{:S(2)}) collective-permute-start(bf16[2304,128]{1,0:T(8,128)(2,1)S(1)} %get-tuple-element.100), channel_id=1, source_target_pairs={{0,4},{1,5},{2,6},{3,7},{4,0},{5,1},{6,2},{7,3},{8,12},{9,13},{10,... | collective-permute-start | bytes 1769480 | tf_op jit(solution)/shard_map/ppermute | solution.py:295
  65.0 1.6 %collective-permute-done.23.refs_3_ = bf16[2304,128]{1,0:T(8,128)(2,1)S(1)} collective-permute-done((bf16[2304,128]{1,0:T(8,128)(2,1)S(1)}, bf16[2304,128]{1,0:T(8,128)(2,1)S(1)}, u32[]{:S(2)}, u32[]{:S(2)}) %collective-permute-start.23) | collective-permute-done | bytes 589856 | tf_op jit(solution)/shard_map/ppermute | solution.py:295
  66.6 3.1 %finish.3 = (bf16[4608,128]{1,0:T(8,128)(2,1)S(1)}, bf16[4096,128]{1,0:T(8,128)(2,1)}, bf16[4096,4,128]{2,1,0:T(4,128)(2,1)}) custom-call(s32[4,32]{1,0:T(4,128)S(1)} %bitcast.26, bf16[1792,512]{1,0:T(8,128)(2,1)S(1)} %get-tuple-element.54.refs_0_, ...), custom_call_target="tpu_custom_call", output_to_operand_aliasing={{0}: (6, {}), {1}: (7, {}), {2}: (8, {})} | custom-call | flops 2500000000 | tf_op jit(solution)/shard_map/finish/pallas_call | solution.py:262
  (20 shorter events, 0.1 us)
Async XLA Ops:
  0.6 0.7 copy-start.1
  4.5 10.2 %collective-permute-start.4 = (bf16[1792,512]{1,0:T(8,128)(2,1)S(1)}, bf16[1792,512]{1,0:T(8,128)(2,1)S(1)}, u32[]{:S(2)}, u32[]{:S(2)}) collective-permute-start(bf16[1792,512]{1,0:T(8,128)(2,1)S(1)} %get-tuple-element.54.refs_0_), channel_id=1, source_target_pairs={{0,4},{1,5},{2,6},{3,7},{4,0},{5,1},{6,2},{7,3},{8,12},{9,13},{10,... | collective-permute-start | bytes 5505032 | tf_op jit(solution)/shard_map/ppermute | solution.py:295
  5.3 8.9 %collective-permute-start = (s32[4,32]{1,0:T(4,128)S(1)}, s32[4,32]{1,0:T(4,128)S(1)}, u32[]{:S(2)}, u32[]{:S(2)}) collective-permute-start(s32[4,32]{1,0:T(4,128)S(1)} %bitcast.11), channel_id=1, source_target_pairs={{0,4},{1,5},{2,6},{3,7},{4,0},{5,1},{6,2},{7,3},{8,12},{9,13},{10,... | collective-permute-start | bytes 1544 | tf_op jit(solution)/shard_map/ppermute | solution.py:295
  5.3 9.4 %collective-permute-start.5 = (bf16[384,640]{1,0:T(8,128)(2,1)S(1)}, bf16[384,640]{1,0:T(8,128)(2,1)S(1)}, u32[]{:S(2)}, u32[]{:S(2)}) collective-permute-start(bf16[384,640]{1,0:T(8,128)(2,1)S(1)} %get-tuple-element.58), channel_id=1, source_target_pairs={{4,1},{5,0},{6,3},{7,2},{12,9},{13,8},{14,11},{15,10},{20,17},{21,... | collective-permute-start | bytes 1474568 | tf_op jit(solution)/shard_map/ppermute | solution.py:295
  10.7 9.4 %collective-permute-start.3 = (bf16[384,640]{1,0:T(8,128)(2,1)S(1)}, bf16[384,640]{1,0:T(8,128)(2,1)S(1)}, u32[]{:S(2)}, u32[]{:S(2)}) collective-permute-start(bf16[384,640]{1,0:T(8,128)(2,1)S(1)} %get-tuple-element.57), channel_id=1, source_target_pairs={{5,2},{6,1},{13,10},{14,9},{21,18},{22,17},{29,26},{30,25}} | collective-permute-start | bytes 1474568 | tf_op jit(solution)/shard_map/ppermute | solution.py:295
  14.1 5.9 %collective-permute-start.2 = (bf16[768,512]{1,0:T(8,128)(2,1)S(1)}, bf16[768,512]{1,0:T(8,128)(2,1)S(1)}, u32[]{:S(2)}, u32[]{:S(2)}) collective-permute-start(bf16[768,512]{1,0:T(8,128)(2,1)S(1)} %get-tuple-element.56.refs_1_.refs_2_), channel_id=1, source_target_pairs={{0,4},{1,5},{2,6},{3,7},{4,0},{5,1},{6,2},{7,3},{8,12},{9,13},{10,... | collective-permute-start | bytes 2359304 | tf_op jit(solution)/shard_map/ppermute | solution.py:295
  14.2 4.5 %collective-permute-start.1 = (bf16[1536,512]{1,0:T(8,128)(2,1)S(1)}, bf16[1536,512]{1,0:T(8,128)(2,1)S(1)}, u32[]{:S(2)}, u32[]{:S(2)}) collective-permute-start(bf16[1536,512]{1,0:T(8,128)(2,1)S(1)} %get-tuple-element.55.refs_1_.refs_0_), channel_id=1, source_target_pairs={{0,4},{1,5},{2,6},{3,7},{4,0},{5,1},{6,2},{7,3},{8,12},{9,13},{10,... | collective-permute-start | bytes 4718600 | tf_op jit(solution)/shard_map/ppermute | solution.py:295
  15.3 6.7 %collective-permute-start.10 = (bf16[512,128]{1,0:T(8,128)(2,1)S(1)}, bf16[512,128]{1,0:T(8,128)(2,1)S(1)}, u32[]{:S(2)}, u32[]{:S(2)}) collective-permute-start(bf16[512,128]{1,0:T(8,128)(2,1)S(1)} %get-tuple-element.68), channel_id=1, source_target_pairs={{24,17},{25,16},{26,19},{27,18}} | collective-permute-start | bytes 393224 | tf_op jit(solution)/shard_map/ppermute | solution.py:295
  16.0 6.1 %collective-permute-start.9 = (bf16[1536,128]{1,0:T(8,128)(2,1)S(1)}, bf16[1536,128]{1,0:T(8,128)(2,1)S(1)}, u32[]{:S(2)}, u32[]{:S(2)}) collective-permute-start(bf16[1536,128]{1,0:T(8,128)(2,1)S(1)} %get-tuple-element.67), channel_id=1, source_target_pairs={{24,16},{25,17},{26,18},{27,19}} | collective-permute-start | bytes 1179656 | tf_op jit(solution)/shard_map/ppermute | solution.py:295
  19.3 4.7 %collective-permute-start.8 = (bf16[1536,128]{1,0:T(8,128)(2,1)S(1)}, bf16[1536,128]{1,0:T(8,128)(2,1)S(1)}, u32[]{:S(2)}, u32[]{:S(2)}) collective-permute-start(bf16[1536,128]{1,0:T(8,128)(2,1)S(1)} %get-tuple-element.66), channel_id=1, source_target_pairs={{24,16},{25,17},{26,18},{27,19}} | collective-permute-start | bytes 1179656 | tf_op jit(solution)/shard_map/ppermute | solution.py:295
  20.7 4.7 %collective-permute-start.7 = (bf16[512,128]{1,0:T(8,128)(2,1)S(1)}, bf16[512,128]{1,0:T(8,128)(2,1)S(1)}, u32[]{:S(2)}, u32[]{:S(2)}) collective-permute-start(bf16[512,128]{1,0:T(8,128)(2,1)S(1)} %get-tuple-element.65), channel_id=1, source_target_pairs={{25,18},{26,17}} | collective-permute-start | bytes 393224 | tf_op jit(solution)/shard_map/ppermute | solution.py:295
  21.4 4.0 %collective-permute-start.6 = (bf16[1024,128]{1,0:T(8,128)(2,1)S(1)}, bf16[1024,128]{1,0:T(8,128)(2,1)S(1)}, u32[]{:S(2)}, u32[]{:S(2)}) collective-permute-start(bf16[1024,128]{1,0:T(8,128)(2,1)S(1)} %get-tuple-element.64), channel_id=1, source_target_pairs={{24,16},{25,17},{26,18},{27,19}} | collective-permute-start | bytes 786440 | tf_op jit(solution)/shard_map/ppermute | solution.py:295
  22.7 4.7 %collective-permute-start.15 = (bf16[512,128]{1,0:T(8,128)(2,1)S(1)}, bf16[512,128]{1,0:T(8,128)(2,1)S(1)}, u32[]{:S(2)}, u32[]{:S(2)}) collective-permute-start(bf16[512,128]{1,0:T(8,128)(2,1)S(1)} %get-tuple-element.79), channel_id=1, source_target_pairs={{16,9},{17,8},{18,11},{19,10}} | collective-permute-start | bytes 393224 | tf_op jit(solution)/shard_map/ppermute | solution.py:295
  23.4 4.1 %collective-permute-start.14 = (bf16[1024,128]{1,0:T(8,128)(2,1)S(1)}, bf16[1024,128]{1,0:T(8,128)(2,1)S(1)}, u32[]{:S(2)}, u32[]{:S(2)}) collective-permute-start(bf16[1024,128]{1,0:T(8,128)(2,1)S(1)} %get-tuple-element.78), channel_id=1, source_target_pairs={{16,8},{17,9},{18,10},{19,11}} | collective-permute-start | bytes 786440 | tf_op jit(solution)/shard_map/ppermute | solution.py:295
  24.7 4.9 %collective-permute-start.13 = (bf16[1536,128]{1,0:T(8,128)(2,1)S(1)}, bf16[1536,128]{1,0:T(8,128)(2,1)S(1)}, u32[]{:S(2)}, u32[]{:S(2)}) collective-permute-start(bf16[1536,128]{1,0:T(8,128)(2,1)S(1)} %get-tuple-element.77), channel_id=1, source_target_pairs={{16,8},{17,9},{18,10},{19,11}} | collective-permute-start | bytes 1179656 | tf_op jit(solution)/shard_map/ppermute | solution.py:295
  26.0 4.9 %collective-permute-start.12 = (bf16[512,128]{1,0:T(8,128)(2,1)S(1)}, bf16[512,128]{1,0:T(8,128)(2,1)S(1)}, u32[]{:S(2)}, u32[]{:S(2)}) collective-permute-start(bf16[512,128]{1,0:T(8,128)(2,1)S(1)} %get-tuple-element.76), channel_id=1, source_target_pairs={{17,10},{18,9}} | collective-permute-start | bytes 393224 | tf_op jit(solution)/shard_map/ppermute | solution.py:295
  26.7 4.2 %collective-permute-start.11 = (bf16[1536,128]{1,0:T(8,128)(2,1)S(1)}, bf16[1536,128]{1,0:T(8,128)(2,1)S(1)}, u32[]{:S(2)}, u32[]{:S(2)}) collective-permute-start(bf16[1536,128]{1,0:T(8,128)(2,1)S(1)} %get-tuple-element.75), channel_id=1, source_target_pairs={{16,8},{17,9},{18,10},{19,11}} | collective-permute-start | bytes 1179656 | tf_op jit(solution)/shard_map/ppermute | solution.py:295
  28.2 4.0 %collective-permute-start.19 = (bf16[512,128]{1,0:T(8,128)(2,1)S(1)}, bf16[512,128]{1,0:T(8,128)(2,1)S(1)}, u32[]{:S(2)}, u32[]{:S(2)}) collective-permute-start(bf16[512,128]{1,0:T(8,128)(2,1)S(1)} %get-tuple-element.89), channel_id=1, source_target_pairs={{8,0},{9,1},{10,2},{11,3}} | collective-permute-start | bytes 393224 | tf_op jit(solution)/shard_map/ppermute | solution.py:295
  28.9 3.4 %collective-permute-start.20 = (bf16[512,128]{1,0:T(8,128)(2,1)S(1)}, bf16[512,128]{1,0:T(8,128)(2,1)S(1)}, u32[]{:S(2)}, u32[]{:S(2)}) collective-permute-start(bf16[512,128]{1,0:T(8,128)(2,1)S(1)} %get-tuple-element.90), channel_id=1, source_target_pairs={{8,1},{9,0},{10,3},{11,2}} | collective-permute-start | bytes 393224 | tf_op jit(solution)/shard_map/ppermute | solution.py:295
  30.2 2.7 %collective-permute-start.18 = (bf16[1536,128]{1,0:T(8,128)(2,1)S(1)}, bf16[1536,128]{1,0:T(8,128)(2,1)S(1)}, u32[]{:S(2)}, u32[]{:S(2)}) collective-permute-start(bf16[1536,128]{1,0:T(8,128)(2,1)S(1)} %get-tuple-element.88), channel_id=1, source_target_pairs={{8,0},{9,1},{10,2},{11,3}} | collective-permute-start | bytes 1179656 | tf_op jit(solution)/shard_map/ppermute | solution.py:295
  31.6 26.8 %collective-permute-start.16 = (bf16[2048,128]{1,0:T(8,128)(2,1)S(1)}, bf16[2048,128]{1,0:T(8,128)(2,1)S(1)}, u32[]{:S(2)}, u32[]{:S(2)}) collective-permute-start(bf16[2048,128]{1,0:T(8,128)(2,1)S(1)} %get-tuple-element.86), channel_id=1, source_target_pairs={{8,0},{9,1},{10,2},{11,3}} | collective-permute-start | bytes 1572872 | tf_op jit(solution)/shard_map/ppermute | solution.py:295
  32.9 22.9 %copy-start = (bf16[1,1,4096,128]{3,2,1,0:T(8,128)(2,1)S(1)}, bf16[1,1,4096,128]{3,2,1,0:T(8,128)(2,1)}, u32[]{:S(2)}) copy-start(bf16[1,1,4096,128]{3,2,1,0:T(8,128)(2,1)} %param.7) | copy-start | bytes 3145732
  33.6 22.2 %collective-permute-start.21 = (bf16[1280,128]{1,0:T(8,128)(2,1)S(1)}, bf16[1280,128]{1,0:T(8,128)(2,1)S(1)}, u32[]{:S(2)}, u32[]{:S(2)}) collective-permute-start(bf16[1280,128]{1,0:T(8,128)(2,1)S(1)} %get-tuple-element.95), channel_id=1, source_target_pairs={{0,4},{1,5},{2,6},{3,7},{4,0},{5,1},{6,2},{7,3},{8,12},{9,13},{10,... | collective-permute-start | bytes 983048 | tf_op jit(solution)/shard_map/ppermute | solution.py:295
  54.2 1.6 %collective-permute-start.22 = (bf16[1024,128]{1,0:T(8,128)(2,1)S(1)}, bf16[1024,128]{1,0:T(8,128)(2,1)S(1)}, u32[]{:S(2)}, u32[]{:S(2)}) collective-permute-start(bf16[1024,128]{1,0:T(8,128)(2,1)S(1)} %get-tuple-element.96), channel_id=1, source_target_pairs={{0,4},{1,5},{2,6},{3,7},{4,0},{5,1},{6,2},{7,3},{8,12},{9,13},{10,... | collective-permute-start | bytes 786440 | tf_op jit(solution)/shard_map/ppermute | solution.py:295
  54.3 4.1 %collective-permute-start.17 = (bf16[512,128]{1,0:T(8,128)(2,1)S(1)}, bf16[512,128]{1,0:T(8,128)(2,1)S(1)}, u32[]{:S(2)}, u32[]{:S(2)}) collective-permute-start(bf16[512,128]{1,0:T(8,128)(2,1)S(1)} %get-tuple-element.87), channel_id=1, source_target_pairs={{9,2},{10,1}} | collective-permute-start | bytes 393224 | tf_op jit(solution)/shard_map/ppermute | solution.py:295
  59.0 7.6 %collective-permute-start.23 = (bf16[2304,128]{1,0:T(8,128)(2,1)S(1)}, bf16[2304,128]{1,0:T(8,128)(2,1)S(1)}, u32[]{:S(2)}, u32[]{:S(2)}) collective-permute-start(bf16[2304,128]{1,0:T(8,128)(2,1)S(1)} %get-tuple-element.100), channel_id=1, source_target_pairs={{0,4},{1,5},{2,6},{3,7},{4,0},{5,1},{6,2},{7,3},{8,12},{9,13},{10,... | collective-permute-start | bytes 1769480 | tf_op jit(solution)/shard_map/ppermute | solution.py:295

commit v4 on v3

--- a/solution.py
+++ b/solution.py
@@ -10,7 +10,8 @@
 WIDE = 2 * REACH
 BAND = 2 * REACH + 1
 GROUP = 4
-PREPARE, FIRST, STEP, FINISH = 1e10, 2e10, 1e10, 4e9
+FILL, EDGE, MAIN = range(3)
+PREPARE, FIRST, SECOND, STEP, COLLECT, FINISH = 1e9, 2e10, 2e10, 1e10, 1e9, 4e9
 VMEM = pl.BlockSpec(memory_space=pltpu.VMEM)
 SMEM = pl.BlockSpec(memory_space=pltpu.SMEM)
 HBM = pl.BlockSpec(memory_space=pltpu.HBM)
@@ -73,35 +74,76 @@
     return parts[k][rows_of(p - cuts[k]), :]
 
 
-def prepare(first, final, cuts, pairs, table, transfer, right):
+def prepare_edges(pairs, tiles, table, transfer, right):
+    bond = right.shape[1]
+    starts = [0, tiles - WIDE]
+
+    def kernel(sources, source, environment, first, last, landed, halo, table, arrived, listed):
+        back = reversed_here()
+        place = places(table, tiles)
+        copies = []
+        for e, (near, begin) in enumerate(((0, 0), (tiles - REACH, starts[1]))):
+            start = jnp.where(back, tiles - REACH - near, near)
+            copies.append(pltpu.make_async_copy(source.at[rows_of(start, REACH)], landed.at[rows_of(e * REACH, REACH)], arrived.at[0, e]))
+            start = jnp.where(back, tiles - WIDE - begin, begin)
+            copies.append(pltpu.make_async_copy(environment.at[rows_of(start, WIDE)], halo.at[rows_of(e * WIDE, WIDE)], arrived.at[1, e]))
+        lists = pltpu.make_async_copy(sources, table, listed)
+        for copy in [lists, *copies]:
+            copy.start()
+        first[...] = jnp.zeros_like(first)
+        last[...] = jnp.zeros_like(last)
+        lists.wait()
+        for e, (edge, near) in enumerate(((first, 0), (last, tiles - REACH))):
+            copies[2 * e].wait()
+            for i in range(REACH):
+                p = near + i
+                split = jnp.swapaxes(landed[rows_of(e * REACH + jnp.where(back, REACH - 1 - i, i))], 0, 1)
+                for j in range(pairs):
+                    edge[rows_of(i), rows_of(REACH - place(j, p) + p)] = split[j]
+            copies[2 * e + 1].wait()
+            for m in range(WIDE):
+                at = e * WIDE + jnp.where(back, WIDE - 1 - m, m)
+                edge[rows_of(REACH), m * bond : (m + 1) * bond] = halo[rows_of(at), :]
+
+    return pl.pallas_call(
+        kernel,
+        in_specs=[HBM, HBM, HBM],
+        out_specs=[VMEM, VMEM],
+        out_shape=[tile_rows(REACH + 1, BAND * TILE)] * 2,
+        scratch_shapes=[
+            pltpu.VMEM((2 * REACH * TILE, pairs, TILE), jnp.bfloat16),
+            pltpu.VMEM((2 * WIDE * TILE, bond), jnp.bfloat16),
+            pltpu.SMEM(table.shape, jnp.int32),
+            pltpu.SemaphoreType.DMA((2, 2)),
+            pltpu.SemaphoreType.DMA,
+        ],
+        compiler_params=params(),
+        cost_estimate=cost(PREPARE / 8),
+        name="prepare_edges",
+    )(*(pltpu.with_memory_space_constraint(value, pltpu.HBM) for value in (table, transfer, right)))
+
+
+def prepare(first, final, cuts, pairs, transfer, right):
     tiles, bond = cuts[-1], right.shape[1]
     chosen = range(first, final)
     groups = [(p, min(GROUP, cuts[k + 1] - p)) for k in chosen for p in range(cuts[k], cuts[k + 1], GROUP)]
     begin, end = cuts[first], cuts[final]
-    head, tail = first == 0, end == tiles
-    spans = [range(WIDE)] * head + [range(tiles - WIDE, tiles)] * tail
-
-    def kernel(table, source, environment, *refs):
+    tail = end == tiles
+
+    def kernel(source, environment, *refs):
         parts, refs = refs[: len(chosen)], refs[len(chosen) :]
-        edges, refs = refs[: len(spans)], refs[len(spans) :]
-        landed, halo, arrived, halo_arrived, placed = refs[-5:]
+        landed, arrived, placed = refs[-3:]
         back = reversed_here()
-        place = places(table, tiles)
-        copies, halos, whole = [], [], []
+        copies, whole = [], []
         for g, (p, size) in enumerate(groups):
             start = jnp.where(back, tiles - p - size, p)
             copies.append(pltpu.make_async_copy(source.at[rows_of(start, size)], landed.at[rows_of(p - begin, size)], arrived.at[g]))
-        for e, span in enumerate(spans):
-            start = jnp.where(back, tiles - span[0] - WIDE, span[0])
-            halos.append(pltpu.make_async_copy(environment.at[rows_of(start, WIDE)], halo.at[e], halo_arrived.at[e]))
         if tail:
             for p in range(tiles):
                 at = jnp.where(back, tiles - 1 - p, p)
                 whole.append(pltpu.make_async_copy(environment.at[rows_of(at)], refs[0].at[rows_of(WIDE + p)], placed.at[p]))
-        for copy in copies + halos + whole:
+        for copy in copies + whole:
             copy.start()
-        for edge in edges:
-            edge[...] = jnp.zeros_like(edge)
         for g, (p, size) in enumerate(groups):
             copies[g].wait()
             k = max(k for k in chosen if cuts[k] <= p)
@@ -110,50 +152,39 @@
                 split = jnp.swapaxes(landed[rows_of(at)], 0, 1)
                 for j in range(pairs):
                     parts[k - first][rows_of(p + i - cuts[k]), j * TILE : (j + 1) * TILE] = split[j]
-                for edge, span in zip(edges, spans):
-                    near = span[:REACH] if span[0] == 0 else span[REACH:]
-                    if p + i in near:
-                        for j in range(pairs):
-                            edge[rows_of(near.index(p + i)), rows_of(REACH - place(j, p + i) + p + i)] = split[j]
-        for e, edge in enumerate(edges):
-            halos[e].wait()
-            for m in range(WIDE):
-                at = jnp.where(back, WIDE - 1 - m, m)
-                edge[rows_of(REACH), m * bond : (m + 1) * bond] = halo[e, rows_of(at), :]
         for copy in whole:
             copy.wait()
 
-    outs = [tile_rows(cuts[k + 1] - cuts[k], pairs * TILE) for k in chosen] + [tile_rows(REACH + 1, BAND * TILE)] * len(spans)
+    outs = [tile_rows(cuts[k + 1] - cuts[k], pairs * TILE) for k in chosen]
     if tail:
         outs.append(tile_rows(tiles + 2 * WIDE, bond))
     return pl.pallas_call(
         kernel,
-        in_specs=[SMEM, HBM, HBM],
+        in_specs=[HBM, HBM],
         out_specs=[VMEM] * len(outs),
         out_shape=outs,
         scratch_shapes=[
             pltpu.VMEM(((end - begin) * TILE, pairs, TILE), jnp.bfloat16),
-            pltpu.VMEM((len(spans), WIDE * TILE, bond), jnp.bfloat16),
             pltpu.SemaphoreType.DMA((len(groups),)),
-            pltpu.SemaphoreType.DMA((len(spans),)),
             pltpu.SemaphoreType.DMA((tiles,)),
         ],
         compiler_params=params(),
         cost_estimate=cost(PREPARE * (end - begin) / tiles),
         name="prepare",
-    )(table, *(pltpu.with_memory_space_constraint(value, pltpu.HBM) for value in (transfer, right)))
-
-
-def pair_step(step, k, tiles, pairs, cuts, inner, outer, tables, own, odd, edges, arrived, keeps, give=()):
+    )(*(pltpu.with_memory_space_constraint(value, pltpu.HBM) for value in (transfer, right)))
+
+
+def pair_step(step, k, tiles, pairs, cuts, inner, outer, tables, own, odd, edges, arrived, keeps, give=(), doing=(FILL, EDGE, MAIN), work=0):
     count = len(own)
     head, tail = k == 0, k == count - 1
-    edges = edges[:1] * head + edges[1:] * tail
+    edges = (edges[:1] * head + edges[1:] * tail) * (EDGE in doing or step == 0 and FILL in doing)
+    arrived = arrived * (FILL in doing)
     bond = keeps[-1].shape[1]
     begin, end = inner[k], inner[k + 1]
-    emit = outer is not None
+    emit = outer is not None and MAIN in doing
     out = (outer[k], outer[k + 1]) if emit else None
     begin_odd, end_odd = 0 if head else begin - REACH, tiles if tail else end - REACH
-    odd_parts = [i for i in range(count) if cuts[i] < end_odd and cuts[i + 1] > begin_odd]
+    odd_parts = [i for i in range(count) if MAIN in doing and cuts[i] < end_odd and cuts[i + 1] > begin_odd]
     own_parts = [i for i in range(count) if emit and cuts[i] < out[1] and cuts[i + 1] > out[0]]
     fixed = [*(own[i] for i in own_parts), *(odd[i] for i in odd_parts), *edges]
     first = 2 + len(fixed) + len(arrived)
@@ -169,22 +200,22 @@
 
         @pl.when(kind == 2 * step)
         def _():
-            if step > 0:
+            if step > 0 and FILL in doing:
                 wide[rows_of(WIDE + begin, end - begin), :] = came[0][...]
-            for m in range(WIDE):
+            for m in range(WIDE * (FILL in doing)):
                 if head:
                     value = came[1][rows_of(m), :] if step > 0 else edge_refs[0][rows_of(REACH), m * bond : (m + 1) * bond]
                     wide[rows_of(WIDE - 1 - m), :] = value
                 if tail:
                     value = came[-1][rows_of(m), :] if step > 0 else edge_refs[-1][rows_of(REACH), m * bond : (m + 1) * bond]
                     wide[rows_of(tiles + 2 * WIDE - 1 - m), :] = value
-            for e in range(REACH):
+            for e in range(REACH * (EDGE in doing)):
                 if head:
                     kept[rows_of(REACH - 1 - e), :] = product(edge_refs[0][rows_of(e), :], wide[rows_of(WIDE - 1 - e - REACH, BAND), :])
                 if tail:
                     at = tiles + REACH - 1 - e
                     kept[rows_of(REACH + at), :] = product(edge_refs[-1][rows_of(e), :], wide[rows_of(WIDE + at - REACH, BAND), :])
-            for p in range(begin_odd, end_odd):
+            for p in range(begin_odd, end_odd if MAIN in doing else begin_odd):
                 kept[rows_of(REACH + p), :] = product(blocks_at(odd_refs, cuts, p), stacked(wide, odd_place, p, WIDE, pairs))
             for p in range(*(out or (0, 0))):
                 fresh = product(blocks_at(own_refs, cuts, p), stacked(kept, place, p, REACH, pairs))
@@ -212,12 +243,12 @@
         out_shape=outs,
         input_output_aliases={first + i: 2 - len(keeps) + i for i in range(len(keeps))},
         compiler_params=params(),
-        cost_estimate=cost(STEP * (end - begin) / tiles if step or k else FIRST),
+        cost_estimate=cost(work or STEP * (end - begin) / tiles),
         name="pair_step",
     )(*tables, *fixed, *arrived, *keeps)
 
 
-def finish(begin, end, tiles, pairs, cuts, table, own, given, regions, left, state, done):
+def finish(begin, end, odd_column, tiles, pairs, cuts, table, own, given, regions, left, state, done):
     bond = state.shape[1]
     parts = [k for k in range(len(own)) if cuts[k] < end and cuts[k + 1] > begin]
     groups = [(p, min(GROUP, end - p)) for p in range(begin, end, GROUP)]
@@ -229,32 +260,36 @@
         *taken, rows = refs[count : fixed - 1]
         kept, env, grad, staged_env, staged, sent = refs[len(refs_in) :]
 
-        @pl.when(kind_here() % 2 == 1)
+        core = kind_here() % 2
+
+        @pl.when(core == 1)
         def _():
             for (low, high), value in zip(regions, taken):
                 kept[rows_of(REACH + low, high - low), :] = value[...]
 
-        place = places(table, tiles)
-        back = reversed_here()
-        copies = []
-        for g, (p, size) in enumerate(groups):
-            start = jnp.where(back, tiles - p - size, p)
-            for i in range(size):
-                inside = jnp.where(back, size - 1 - i, i)
-                sources = stacked(kept, place, p + i, REACH, pairs)
-                staged_env[rows_of(p - begin + inside), :] = product(blocks_at(own_refs, cuts, p + i), sources)
-                block = lax.dot_general(
-                    rows[rows_of(start + inside), :], sources, (((1,), (1,)), ((), ())), preferred_element_type=jnp.float32
-                ).astype(jnp.bfloat16)
-                block = jnp.stack([block[:, j * TILE : (j + 1) * TILE] for j in range(pairs)], axis=0)
-                staged[rows_of(p - begin + inside)] = jnp.swapaxes(block, 0, 1)
-            here, there = rows_of(p - begin, size), rows_of(start, size)
-            copies.append(pltpu.make_async_copy(staged_env.at[here], env.at[there], sent.at[0, g]))
-            copies.append(pltpu.make_async_copy(staged.at[here], grad.at[there], sent.at[1, g]))
-            for copy in copies[-2:]:
-                copy.start()
-        for copy in copies:
-            copy.wait()
+        @pl.when(core >= 0 if odd_column is None else core == odd_column)
+        def _():
+            place = places(table, tiles)
+            back = reversed_here()
+            copies = []
+            for g, (p, size) in enumerate(groups):
+                start = jnp.where(back, tiles - p - size, p)
+                for i in range(size):
+                    inside = jnp.where(back, size - 1 - i, i)
+                    sources = stacked(kept, place, p + i, REACH, pairs)
+                    staged_env[rows_of(p - begin + inside), :] = product(blocks_at(own_refs, cuts, p + i), sources)
+                    block = lax.dot_general(
+                        rows[rows_of(start + inside), :], sources, (((1,), (1,)), ((), ())), preferred_element_type=jnp.float32
+                    ).astype(jnp.bfloat16)
+                    block = jnp.stack([block[:, j * TILE : (j + 1) * TILE] for j in range(pairs)], axis=0)
+                    staged[rows_of(p - begin + inside)] = jnp.swapaxes(block, 0, 1)
+                here, there = rows_of(p - begin, size), rows_of(start, size)
+                copies.append(pltpu.make_async_copy(staged_env.at[here], env.at[there], sent.at[0, g]))
+                copies.append(pltpu.make_async_copy(staged.at[here], grad.at[there], sent.at[1, g]))
+                for copy in copies[-2:]:
+                    copy.start()
+            for copy in copies:
+                copy.wait()
 
     env = tile_rows(tiles, bond)
     grad = jax.ShapeDtypeStruct((tiles * TILE, pairs, TILE), jnp.bfloat16)
@@ -304,12 +339,14 @@
     ends = limits(tiles, layers - 1)
     count = len(ends) + 1
     cuts = [0] + [e + WIDE - REACH for e in ends] + [tiles]
-    head, first_edge = prepare(0, 1, cuts, pairs, table, blocks, right)
-    *rest, last_edge, wide = prepare(1, count, cuts, pairs, table, blocks, right)
+    first_edge, last_edge = prepare_edges(pairs, tiles, table, blocks, right)
+    first_edge, last_edge, blocks = lax.optimization_barrier((first_edge, last_edge, blocks))
+    (head,) = prepare(0, 1, cuts, pairs, blocks, right)
+    *rest, wide = prepare(1, count, cuts, pairs, blocks, right)
     own = [head, *rest]
     odd_cols = [(2 * z + 1, 2 * z) for z in range(layers)]
     odd = [move(part, swap) for part in own]
-    odd_table = move(table, swap)
+    odd_table = move(lax.optimization_barrier((table, head))[0], swap)
     odd_edges = [move(first_edge, [(a, b, partner) for a, b in odd_cols]), move(last_edge, [(a, b, other) for a, b in odd_cols])]
 
     keeps = [wide]
@@ -327,23 +364,37 @@
                 if k == 0:
                     came.append(move(sent[k][1], [(above, here, partner)]))
                 if k == count - 1:
-                    came.append(move(sent[k][-1], [(above, here, other)]))
+                    came.append(halo if end else move(sent[k][-1], [(above, here, other)]))
+                if end and k == count - 2:
+                    halo = move(sent[k + 1][-1], [(above, here, other)])
+                    came.append(halo)
             give = []
             if end and k == count - 2:
                 middle = inner[k + 1] // 2
                 give = [(-REACH, middle), (middle, inner[k + 1])]
             if end and k == count - 1:
                 give = [(inner[k], tiles + REACH)]
-            result = pair_step(step, k, tiles, pairs, cuts, inner, outer, [table, odd_table], own, odd, odd_edges, came, keeps, give)
-            keeps = result[:2]
+            arguments = [table, odd_table], own, odd, odd_edges, came
+            if step == 0 and k == 0:
+                keeps = pair_step(step, k, tiles, pairs, cuts, inner, None, *arguments, keeps, (), (FILL, EDGE), FIRST)
+                result = pair_step(step, k, tiles, pairs, cuts, inner, outer, *arguments, keeps, (), (MAIN,))
+            elif end and k == count - 1:
+                *keeps, gift = pair_step(step, k, tiles, pairs, cuts, inner, None, *arguments, keeps, give, (FILL,), COLLECT)
+                result = pair_step(step, k, tiles, pairs, cuts, inner, None, *arguments, keeps, (), (EDGE, MAIN))
+            else:
+                result = pair_step(step, k, tiles, pairs, cuts, inner, outer, *arguments, keeps, give, work=SECOND * (step == 0 and k == 1))
+            keeps = list(result[:2])
             if give:
-                given = [move(value, swap) for value in result[len(result) - len(give) :]]
+                gifts = [gift] if k == count - 1 else result[len(result) - len(give) :]
+                given = [move(value, swap) for value in gifts]
                 if k == count - 2:
-                    half = max(0, inner[k + 1] - WIDE) // GROUP * GROUP
-                    state, *done = finish(0, half, tiles, pairs, cuts, table, own, given, give, left, keeps[0], [])
-                    keeps = [state, keeps[1]]
+                    half = max(0, give[-1][1] - WIDE) // GROUP * GROUP
+                    done = []
+                    for odd_column in (0, 1):
+                        takes = (given, give) if odd_column else ([], [])
+                        keeps[0], *done = finish(0, half, odd_column, tiles, pairs, cuts, table, own, *takes, left, keeps[0], done)
                 else:
-                    _, env, grad = finish(half, tiles, tiles, pairs, cuts, table, own, given, give, left, keeps[0], done)
+                    _, env, grad = finish(half, tiles, None, tiles, pairs, cuts, table, own, given, give, left, keeps[0], done)
             leaving.append(result[2:])
         sent = leaving
 

time: 71 us -> 67.9 us (0.956)
  starting transfers between devices: 42.9 us -> 40.2 us
  Pallas kernels: 20.5 us -> 22.3 us
  waiting for transfers between devices: 4.59 us -> 3.7 us
    ppermute x24, starting transfers between devices: 42.9 us -> 40.2 us  [move(): return lax.ppermute(value, ('col', 'sec'), both)]
    pallas_call x12 -> x14, Pallas kernels: 7.63 us -> 8.69 us  [pair_step(): pl.pallas_call(kernel, in_specs=[SMEM] * 2 + [VMEM] * (first - 2 + len(ke...]
    ppermute x24, waiting for transfers between devices: 4.59 us -> 3.7 us  [move(): return lax.ppermute(value, ('col', 'sec'), both)]
    pallas_call x2 -> x3, Pallas kernels: 5.67 us -> 6.31 us  [finish(): pl.pallas_call(kernel, in_specs=[SMEM] + [VMEM] * fixed + [HBM] * len(don...]
    pallas_call x2 -> x3, Pallas kernels: 7.21 us -> 7.27 us  [the longest x2 5.91 us: prepare(): pl.pallas_call(kernel, in_specs=[HBM, HBM], out_specs=[VMEM] * len(outs),...]
  transfers between devices with their start and end apart: 24 -> 24, of which waited for: 3 -> 3; matrix products, arithmetic and copies ran while one was open for 0% -> 0% of each run, Pallas kernels for 19% -> 25%
where the time goes in v4:
time: 67.9 us; the launch traced here: 67.5 us
  starting transfers between devices  40.2 us (59%)
  Pallas kernels  22.3 us (33%)
  waiting for transfers between devices  3.7 us (5%)
  between operations  1.26 us (2%)
    ppermute x24, starting transfers between devices, move(): return lax.ppermute(value, ('col', 'sec'), both)  40.2 us
    pallas_call x14, Pallas kernels, pair_step(): pl.pallas_call(kernel, in_specs=[SMEM] * 2 + [VMEM] * (first - 2 + len(ke...  8.69 us
    pallas_call x3, Pallas kernels, finish(): pl.pallas_call(kernel, in_specs=[SMEM] + [VMEM] * fixed + [HBM] * len(don...  6.31 us
    pallas_call x2, Pallas kernels, prepare(): pl.pallas_call(kernel, in_specs=[HBM, HBM], out_specs=[VMEM] * len(outs),...  5.91 us
    ppermute x24, waiting for transfers between devices, move(): return lax.ppermute(value, ('col', 'sec'), both)  3.7 us
    pallas_call x1, Pallas kernels, prepare_edges(): pl.pallas_call(kernel, in_specs=[HBM, HBM, HBM], out_specs=[VMEM, VMEM],...  1.36 us
  transfers between devices with their start and end apart: 24, of which 3 were waited for; matrix products, arithmetic and copies ran while one was open for 0% of the time, Pallas kernels for 25%

profile of v4, /device:TPU:3, one launch (start us, length us, event | category | flops | bytes accessed | tf_op | source)
XLA Modules:
  0.0 67.5 jit_solution(2446906747708626627)
XLA Ops:
  0.6 1.4 %prepare_edges.1 = (bf16[384,640]{1,0:T(8,128)(2,1)S(1)}, bf16[384,640]{1,0:T(8,128)(2,1)S(1)}) custom-call(s32[4,32]{1,0:T(4,128)} %bitcast.11, bf16[4096,4,128]{2,1,0:T(4,128)(2,1)} %bitcast.30, bf16[4096,128]{1,0:T(8,128)(2,1)} %bitcast.34), custom_call_target="tpu_custom_call" | custom-call | flops 125000000 | tf_op jit(solution)/shard_map/prepare_edges/pallas_call | solution.py:108
  2.0 0.0 copy-start.1
  2.0 1.3 %collective-permute-start.5 = (bf16[384,640]{1,0:T(8,128)(2,1)S(1)}, bf16[384,640]{1,0:T(8,128)(2,1)S(1)}, u32[]{:S(2)}, u32[]{:S(2)}) collective-permute-start(bf16[384,640]{1,0:T(8,128)(2,1)S(1)} %get-tuple-element.71), channel_id=1, source_target_pairs={{4,1},{5,0},{6,3},{7,2},{12,9},{13,8},{14,11},{15,10},{20,17},{21,... | collective-permute-start | bytes 1474568 | tf_op jit(solution)/shard_map/ppermute | solution.py:330
  3.3 3.7 %collective-permute-start.3 = (bf16[384,640]{1,0:T(8,128)(2,1)S(1)}, bf16[384,640]{1,0:T(8,128)(2,1)S(1)}, u32[]{:S(2)}, u32[]{:S(2)}) collective-permute-start(bf16[384,640]{1,0:T(8,128)(2,1)S(1)} %get-tuple-element.70), channel_id=1, source_target_pairs={{5,2},{6,1},{13,10},{14,9},{21,18},{22,17},{29,26},{30,25}} | collective-permute-start | bytes 1474568 | tf_op jit(solution)/shard_map/ppermute | solution.py:330
  7.0 2.6 %prepare.2.refs_0_ = bf16[1792,512]{1,0:T(8,128)(2,1)S(1)} custom-call(bf16[4096,4,128]{2,1,0:T(4,128)(2,1)} %bitcast.31, bf16[4096,128]{1,0:T(8,128)(2,1)} %bitcast.35), custom_call_target="tpu_custom_call" | custom-call | flops 437500000 | tf_op jit(solution)/shard_map/prepare/pallas_call | solution.py:161
  9.6 0.1 collective-permute-start.4
  9.7 0.5 collective-permute-start
  10.2 3.3 %prepare.3 = (bf16[1536,512]{1,0:T(8,128)(2,1)S(1)}, bf16[768,512]{1,0:T(8,128)(2,1)S(1)}, bf16[5120,128]{1,0:T(8,128)(2,1)S(1)}) custom-call(bf16[4096,4,128]{2,1,0:T(4,128)(2,1)} %bitcast.32, bf16[4096,128]{1,0:T(8,128)(2,1)} %bitcast.36), custom_call_target="tpu_custom_call" | custom-call | flops 562499968 | tf_op jit(solution)/shard_map/prepare/pallas_call | solution.py:161
  13.5 0.2 collective-permute-start.2
  13.7 0.4 collective-permute-start.1
  14.1 0.6 pair_step.14
  14.7 0.6 pair_step.15
  15.4 0.7 collective-permute-start.10
  16.1 0.7 %collective-permute-start.9 = (bf16[1536,128]{1,0:T(8,128)(2,1)S(1)}, bf16[1536,128]{1,0:T(8,128)(2,1)S(1)}, u32[]{:S(2)}, u32[]{:S(2)}) collective-permute-start(bf16[1536,128]{1,0:T(8,128)(2,1)S(1)} %get-tuple-element.82), channel_id=1, source_target_pairs={{24,16},{25,17},{26,18},{27,19}} | collective-permute-start | bytes 1179656 | tf_op jit(solution)/shard_map/ppermute | solution.py:330
  16.7 1.4 %collective-permute-done.1.refs_2_.refs_3_.refs_0_ = bf16[1536,512]{1,0:T(8,128)(2,1)S(1)} collective-permute-done((bf16[1536,512]{1,0:T(8,128)(2,1)S(1)}, bf16[1536,512]{1,0:T(8,128)(2,1)S(1)}, u32[]{:S(2)}, u32[]{:S(2)}) %collective-permute-start.1) | collective-permute-done | bytes 1572896 | tf_op jit(solution)/shard_map/ppermute | solution.py:330
  18.1 0.6 pair_step.16
  18.8 0.7 %collective-permute-start.8 = (bf16[1536,128]{1,0:T(8,128)(2,1)S(1)}, bf16[1536,128]{1,0:T(8,128)(2,1)S(1)}, u32[]{:S(2)}, u32[]{:S(2)}) collective-permute-start(bf16[1536,128]{1,0:T(8,128)(2,1)S(1)} %get-tuple-element.81), channel_id=1, source_target_pairs={{24,16},{25,17},{26,18},{27,19}} | collective-permute-start | bytes 1179656 | tf_op jit(solution)/shard_map/ppermute | solution.py:330
  19.5 0.6 pair_step.17
  20.1 0.7 collective-permute-start.7
  20.8 0.7 %collective-permute-start.6 = (bf16[1024,128]{1,0:T(8,128)(2,1)S(1)}, bf16[1024,128]{1,0:T(8,128)(2,1)S(1)}, u32[]{:S(2)}, u32[]{:S(2)}) collective-permute-start(bf16[1024,128]{1,0:T(8,128)(2,1)S(1)} %get-tuple-element.79), channel_id=1, source_target_pairs={{24,16},{25,17},{26,18},{27,19}} | collective-permute-start | bytes 786440 | tf_op jit(solution)/shard_map/ppermute | solution.py:330
  21.5 0.6 pair_step.18
  22.1 0.7 collective-permute-start.15
  22.8 0.7 %collective-permute-start.14 = (bf16[1024,128]{1,0:T(8,128)(2,1)S(1)}, bf16[1024,128]{1,0:T(8,128)(2,1)S(1)}, u32[]{:S(2)}, u32[]{:S(2)}) collective-permute-start(bf16[1024,128]{1,0:T(8,128)(2,1)S(1)} %get-tuple-element.93), channel_id=1, source_target_pairs={{16,8},{17,9},{18,10},{19,11}} | collective-permute-start | bytes 786440 | tf_op jit(solution)/shard_map/ppermute | solution.py:330
  23.5 0.6 pair_step.19
  24.1 0.7 %collective-permute-start.13 = (bf16[1536,128]{1,0:T(8,128)(2,1)S(1)}, bf16[1536,128]{1,0:T(8,128)(2,1)S(1)}, u32[]{:S(2)}, u32[]{:S(2)}) collective-permute-start(bf16[1536,128]{1,0:T(8,128)(2,1)S(1)} %get-tuple-element.92), channel_id=1, source_target_pairs={{16,8},{17,9},{18,10},{19,11}} | collective-permute-start | bytes 1179656 | tf_op jit(solution)/shard_map/ppermute | solution.py:330
  24.8 0.6 pair_step.20
  25.5 0.7 collective-permute-start.12
  26.1 0.9 %collective-permute-start.11 = (bf16[1536,128]{1,0:T(8,128)(2,1)S(1)}, bf16[1536,128]{1,0:T(8,128)(2,1)S(1)}, u32[]{:S(2)}, u32[]{:S(2)}) collective-permute-start(bf16[1536,128]{1,0:T(8,128)(2,1)S(1)} %get-tuple-element.90), channel_id=1, source_target_pairs={{16,8},{17,9},{18,10},{19,11}} | collective-permute-start | bytes 1179656 | tf_op jit(solution)/shard_map/ppermute | solution.py:330
  27.0 0.6 pair_step.21
  27.7 0.7 collective-permute-start.19
  28.3 0.7 collective-permute-start.20
  29.0 0.6 pair_step.22
  29.6 0.7 %collective-permute-start.18 = (bf16[1536,128]{1,0:T(8,128)(2,1)S(1)}, bf16[1536,128]{1,0:T(8,128)(2,1)S(1)}, u32[]{:S(2)}, u32[]{:S(2)}) collective-permute-start(bf16[1536,128]{1,0:T(8,128)(2,1)S(1)} %get-tuple-element.103), channel_id=1, source_target_pairs={{8,0},{9,1},{10,2},{11,3}} | collective-permute-start | bytes 1179656 | tf_op jit(solution)/shard_map/ppermute | solution.py:330
  30.4 0.6 pair_step.23
  31.0 0.7 collective-permute-start.17
  31.7 0.7 %collective-permute-start.16 = (bf16[2048,128]{1,0:T(8,128)(2,1)S(1)}, bf16[2048,128]{1,0:T(8,128)(2,1)S(1)}, u32[]{:S(2)}, u32[]{:S(2)}) collective-permute-start(bf16[2048,128]{1,0:T(8,128)(2,1)S(1)} %get-tuple-element.101), channel_id=1, source_target_pairs={{8,0},{9,1},{10,2},{11,3}} | collective-permute-start | bytes 1572872 | tf_op jit(solution)/shard_map/ppermute | solution.py:330
  32.4 0.6 pair_step.24
  33.0 0.6 pair_step.25
  33.7 23.6 %collective-permute-start.21 = (bf16[1280,128]{1,0:T(8,128)(2,1)S(1)}, bf16[1280,128]{1,0:T(8,128)(2,1)S(1)}, u32[]{:S(2)}, u32[]{:S(2)}) collective-permute-start(bf16[1280,128]{1,0:T(8,128)(2,1)S(1)} %get-tuple-element.110), channel_id=1, source_target_pairs={{0,4},{1,5},{2,6},{3,7},{4,0},{5,1},{6,2},{7,3},{8,12},{9,13},{10,... | collective-permute-start | bytes 983048 | tf_op jit(solution)/shard_map/ppermute | solution.py:330
  57.3 0.1 collective-permute-start.22
  57.4 0.6 finish.3
  58.0 0.9 %collective-permute-done.22.refs_2_ = bf16[1024,128]{1,0:T(8,128)(2,1)S(1)} collective-permute-done((bf16[1024,128]{1,0:T(8,128)(2,1)S(1)}, bf16[1024,128]{1,0:T(8,128)(2,1)S(1)}, u32[]{:S(2)}, u32[]{:S(2)}) %collective-permute-start.22) | collective-permute-done | bytes 262176 | tf_op jit(solution)/shard_map/ppermute | solution.py:330
  58.9 2.5 %finish.4 = (bf16[4608,128]{1,0:T(8,128)(2,1)S(1)}, bf16[4096,128]{1,0:T(8,128)(2,1)}, bf16[4096,4,128]{2,1,0:T(4,128)(2,1)}) custom-call(s32[4,32]{1,0:T(4,128)S(1)} %bitcast.26, bf16[1792,512]{1,0:T(8,128)(2,1)S(1)} %prepare.2.refs_0_, ...), custom_call_target="tpu_custom_call", output_to_operand_aliasing={{0}: (5, {}), {1}: (6, {}), {2}: (7, {})} | custom-call | flops 1500000000 | tf_op jit(solution)/shard_map/finish/pallas_call | solution.py:297
  61.5 0.6 pair_step.26
  62.1 0.1 collective-permute-start.23
  62.2 0.6 pair_step.27
  62.8 1.4 %collective-permute-done.23.refs_3_ = bf16[2304,128]{1,0:T(8,128)(2,1)S(1)} collective-permute-done((bf16[2304,128]{1,0:T(8,128)(2,1)S(1)}, bf16[2304,128]{1,0:T(8,128)(2,1)S(1)}, u32[]{:S(2)}, u32[]{:S(2)}) %collective-permute-start.23) | collective-permute-done | bytes 589856 | tf_op jit(solution)/shard_map/ppermute | solution.py:330
  64.2 3.1 %finish.5 = (bf16[4608,128]{1,0:T(8,128)(2,1)S(1)}, bf16[4096,128]{1,0:T(8,128)(2,1)}, bf16[4096,4,128]{2,1,0:T(4,128)(2,1)}) custom-call(s32[4,32]{1,0:T(4,128)S(1)} %bitcast.29, bf16[1792,512]{1,0:T(8,128)(2,1)S(1)} %prepare.2.refs_0_, ...), custom_call_target="tpu_custom_call", output_to_operand_aliasing={{0}: (6, {}), {1}: (7, {}), {2}: (8, {})} | custom-call | flops 2500000000 | tf_op jit(solution)/shard_map/finish/pallas_call | solution.py:297
  (24 shorter events, 0.1 us)
Async XLA Ops:
  2.0 7.7 %copy-start.1 = (s32[1,1,32,4]{2,3,1,0:T(4,128)S(1)}, s32[1,1,32,4]{2,3,1,0:T(4,128)}, u32[]{:S(2)}) copy-start(s32[1,1,32,4]{2,3,1,0:T(4,128)} %param.6) | copy-start | bytes 1540
  2.0 12.1 %collective-permute-start.5 = (bf16[384,640]{1,0:T(8,128)(2,1)S(1)}, bf16[384,640]{1,0:T(8,128)(2,1)S(1)}, u32[]{:S(2)}, u32[]{:S(2)}) collective-permute-start(bf16[384,640]{1,0:T(8,128)(2,1)S(1)} %get-tuple-element.71), channel_id=1, source_target_pairs={{4,1},{5,0},{6,3},{7,2},{12,9},{13,8},{14,11},{15,10},{20,17},{21,... | collective-permute-start | bytes 1474568 | tf_op jit(solution)/shard_map/ppermute | solution.py:330
  3.3 16.1 %collective-permute-start.3 = (bf16[384,640]{1,0:T(8,128)(2,1)S(1)}, bf16[384,640]{1,0:T(8,128)(2,1)S(1)}, u32[]{:S(2)}, u32[]{:S(2)}) collective-permute-start(bf16[384,640]{1,0:T(8,128)(2,1)S(1)} %get-tuple-element.70), channel_id=1, source_target_pairs={{5,2},{6,1},{13,10},{14,9},{21,18},{22,17},{29,26},{30,25}} | collective-permute-start | bytes 1474568 | tf_op jit(solution)/shard_map/ppermute | solution.py:330
  9.6 5.1 %collective-permute-start.4 = (bf16[1792,512]{1,0:T(8,128)(2,1)S(1)}, bf16[1792,512]{1,0:T(8,128)(2,1)S(1)}, u32[]{:S(2)}, u32[]{:S(2)}) collective-permute-start(bf16[1792,512]{1,0:T(8,128)(2,1)S(1)} %prepare.2.refs_0_), channel_id=1, source_target_pairs={{0,4},{1,5},{2,6},{3,7},{4,0},{5,1},{6,2},{7,3},{8,12},{9,13},{10,... | collective-permute-start | bytes 5505032 | tf_op jit(solution)/shard_map/ppermute | solution.py:330
  9.7 4.0 %collective-permute-start = (s32[4,32]{1,0:T(4,128)S(1)}, s32[4,32]{1,0:T(4,128)S(1)}, u32[]{:S(2)}, u32[]{:S(2)}) collective-permute-start(s32[4,32]{1,0:T(4,128)S(1)} %bitcast.12), channel_id=1, source_target_pairs={{0,4},{1,5},{2,6},{3,7},{4,0},{5,1},{6,2},{7,3},{8,12},{9,13},{10,... | collective-permute-start | bytes 1544 | tf_op jit(solution)/shard_map/ppermute | solution.py:330
  13.5 5.9 %collective-permute-start.2 = (bf16[768,512]{1,0:T(8,128)(2,1)S(1)}, bf16[768,512]{1,0:T(8,128)(2,1)S(1)}, u32[]{:S(2)}, u32[]{:S(2)}) collective-permute-start(bf16[768,512]{1,0:T(8,128)(2,1)S(1)} %get-tuple-element.68.refs_1_.refs_2_), channel_id=1, source_target_pairs={{0,4},{1,5},{2,6},{3,7},{4,0},{5,1},{6,2},{7,3},{8,12},{9,13},{10,... | collective-permute-start | bytes 2359304 | tf_op jit(solution)/shard_map/ppermute | solution.py:330
  13.7 4.4 %collective-permute-start.1 = (bf16[1536,512]{1,0:T(8,128)(2,1)S(1)}, bf16[1536,512]{1,0:T(8,128)(2,1)S(1)}, u32[]{:S(2)}, u32[]{:S(2)}) collective-permute-start(bf16[1536,512]{1,0:T(8,128)(2,1)S(1)} %get-tuple-element.67.refs_1_.refs_0_), channel_id=1, source_target_pairs={{0,4},{1,5},{2,6},{3,7},{4,0},{5,1},{6,2},{7,3},{8,12},{9,13},{10,... | collective-permute-start | bytes 4718600 | tf_op jit(solution)/shard_map/ppermute | solution.py:330
  15.4 6.1 %collective-permute-start.10 = (bf16[512,128]{1,0:T(8,128)(2,1)S(1)}, bf16[512,128]{1,0:T(8,128)(2,1)S(1)}, u32[]{:S(2)}, u32[]{:S(2)}) collective-permute-start(bf16[512,128]{1,0:T(8,128)(2,1)S(1)} %get-tuple-element.83), channel_id=1, source_target_pairs={{24,17},{25,16},{26,19},{27,18}} | collective-permute-start | bytes 393224 | tf_op jit(solution)/shard_map/ppermute | solution.py:330
  16.1 5.4 %collective-permute-start.9 = (bf16[1536,128]{1,0:T(8,128)(2,1)S(1)}, bf16[1536,128]{1,0:T(8,128)(2,1)S(1)}, u32[]{:S(2)}, u32[]{:S(2)}) collective-permute-start(bf16[1536,128]{1,0:T(8,128)(2,1)S(1)} %get-tuple-element.82), channel_id=1, source_target_pairs={{24,16},{25,17},{26,18},{27,19}} | collective-permute-start | bytes 1179656 | tf_op jit(solution)/shard_map/ppermute | solution.py:330
  18.8 4.7 %collective-permute-start.8 = (bf16[1536,128]{1,0:T(8,128)(2,1)S(1)}, bf16[1536,128]{1,0:T(8,128)(2,1)S(1)}, u32[]{:S(2)}, u32[]{:S(2)}) collective-permute-start(bf16[1536,128]{1,0:T(8,128)(2,1)S(1)} %get-tuple-element.81), channel_id=1, source_target_pairs={{24,16},{25,17},{26,18},{27,19}} | collective-permute-start | bytes 1179656 | tf_op jit(solution)/shard_map/ppermute | solution.py:330
  20.1 4.7 %collective-permute-start.7 = (bf16[512,128]{1,0:T(8,128)(2,1)S(1)}, bf16[512,128]{1,0:T(8,128)(2,1)S(1)}, u32[]{:S(2)}, u32[]{:S(2)}) collective-permute-start(bf16[512,128]{1,0:T(8,128)(2,1)S(1)} %get-tuple-element.80), channel_id=1, source_target_pairs={{25,18},{26,17}} | collective-permute-start | bytes 393224 | tf_op jit(solution)/shard_map/ppermute | solution.py:330
  20.8 4.0 %collective-permute-start.6 = (bf16[1024,128]{1,0:T(8,128)(2,1)S(1)}, bf16[1024,128]{1,0:T(8,128)(2,1)S(1)}, u32[]{:S(2)}, u32[]{:S(2)}) collective-permute-start(bf16[1024,128]{1,0:T(8,128)(2,1)S(1)} %get-tuple-element.79), channel_id=1, source_target_pairs={{24,16},{25,17},{26,18},{27,19}} | collective-permute-start | bytes 786440 | tf_op jit(solution)/shard_map/ppermute | solution.py:330
  22.1 4.9 %collective-permute-start.15 = (bf16[512,128]{1,0:T(8,128)(2,1)S(1)}, bf16[512,128]{1,0:T(8,128)(2,1)S(1)}, u32[]{:S(2)}, u32[]{:S(2)}) collective-permute-start(bf16[512,128]{1,0:T(8,128)(2,1)S(1)} %get-tuple-element.94), channel_id=1, source_target_pairs={{16,9},{17,8},{18,11},{19,10}} | collective-permute-start | bytes 393224 | tf_op jit(solution)/shard_map/ppermute | solution.py:330
  22.8 4.2 %collective-permute-start.14 = (bf16[1024,128]{1,0:T(8,128)(2,1)S(1)}, bf16[1024,128]{1,0:T(8,128)(2,1)S(1)}, u32[]{:S(2)}, u32[]{:S(2)}) collective-permute-start(bf16[1024,128]{1,0:T(8,128)(2,1)S(1)} %get-tuple-element.93), channel_id=1, source_target_pairs={{16,8},{17,9},{18,10},{19,11}} | collective-permute-start | bytes 786440 | tf_op jit(solution)/shard_map/ppermute | solution.py:330
  24.1 4.9 %collective-permute-start.13 = (bf16[1536,128]{1,0:T(8,128)(2,1)S(1)}, bf16[1536,128]{1,0:T(8,128)(2,1)S(1)}, u32[]{:S(2)}, u32[]{:S(2)}) collective-permute-start(bf16[1536,128]{1,0:T(8,128)(2,1)S(1)} %get-tuple-element.92), channel_id=1, source_target_pairs={{16,8},{17,9},{18,10},{19,11}} | collective-permute-start | bytes 1179656 | tf_op jit(solution)/shard_map/ppermute | solution.py:330
  25.5 4.9 %collective-permute-start.12 = (bf16[512,128]{1,0:T(8,128)(2,1)S(1)}, bf16[512,128]{1,0:T(8,128)(2,1)S(1)}, u32[]{:S(2)}, u32[]{:S(2)}) collective-permute-start(bf16[512,128]{1,0:T(8,128)(2,1)S(1)} %get-tuple-element.91), channel_id=1, source_target_pairs={{17,10},{18,9}} | collective-permute-start | bytes 393224 | tf_op jit(solution)/shard_map/ppermute | solution.py:330
  26.1 4.2 %collective-permute-start.11 = (bf16[1536,128]{1,0:T(8,128)(2,1)S(1)}, bf16[1536,128]{1,0:T(8,128)(2,1)S(1)}, u32[]{:S(2)}, u32[]{:S(2)}) collective-permute-start(bf16[1536,128]{1,0:T(8,128)(2,1)S(1)} %get-tuple-element.90), channel_id=1, source_target_pairs={{16,8},{17,9},{18,10},{19,11}} | collective-permute-start | bytes 1179656 | tf_op jit(solution)/shard_map/ppermute | solution.py:330
  27.7 4.7 %collective-permute-start.19 = (bf16[512,128]{1,0:T(8,128)(2,1)S(1)}, bf16[512,128]{1,0:T(8,128)(2,1)S(1)}, u32[]{:S(2)}, u32[]{:S(2)}) collective-permute-start(bf16[512,128]{1,0:T(8,128)(2,1)S(1)} %get-tuple-element.104), channel_id=1, source_target_pairs={{8,0},{9,1},{10,2},{11,3}} | collective-permute-start | bytes 393224 | tf_op jit(solution)/shard_map/ppermute | solution.py:330
  28.3 4.1 %collective-permute-start.20 = (bf16[512,128]{1,0:T(8,128)(2,1)S(1)}, bf16[512,128]{1,0:T(8,128)(2,1)S(1)}, u32[]{:S(2)}, u32[]{:S(2)}) collective-permute-start(bf16[512,128]{1,0:T(8,128)(2,1)S(1)} %get-tuple-element.105), channel_id=1, source_target_pairs={{8,1},{9,0},{10,3},{11,2}} | collective-permute-start | bytes 393224 | tf_op jit(solution)/shard_map/ppermute | solution.py:330
  29.6 3.4 %collective-permute-start.18 = (bf16[1536,128]{1,0:T(8,128)(2,1)S(1)}, bf16[1536,128]{1,0:T(8,128)(2,1)S(1)}, u32[]{:S(2)}, u32[]{:S(2)}) collective-permute-start(bf16[1536,128]{1,0:T(8,128)(2,1)S(1)} %get-tuple-element.103), channel_id=1, source_target_pairs={{8,0},{9,1},{10,2},{11,3}} | collective-permute-start | bytes 1179656 | tf_op jit(solution)/shard_map/ppermute | solution.py:330
  31.0 2.0 %collective-permute-start.17 = (bf16[512,128]{1,0:T(8,128)(2,1)S(1)}, bf16[512,128]{1,0:T(8,128)(2,1)S(1)}, u32[]{:S(2)}, u32[]{:S(2)}) collective-permute-start(bf16[512,128]{1,0:T(8,128)(2,1)S(1)} %get-tuple-element.102), channel_id=1, source_target_pairs={{9,2},{10,1}} | collective-permute-start | bytes 393224 | tf_op jit(solution)/shard_map/ppermute | solution.py:330
  31.7 29.8 %collective-permute-start.16 = (bf16[2048,128]{1,0:T(8,128)(2,1)S(1)}, bf16[2048,128]{1,0:T(8,128)(2,1)S(1)}, u32[]{:S(2)}, u32[]{:S(2)}) collective-permute-start(bf16[2048,128]{1,0:T(8,128)(2,1)S(1)} %get-tuple-element.101), channel_id=1, source_target_pairs={{8,0},{9,1},{10,2},{11,3}} | collective-permute-start | bytes 1572872 | tf_op jit(solution)/shard_map/ppermute | solution.py:330
  33.0 24.3 %copy-start = (bf16[1,1,4096,128]{3,2,1,0:T(8,128)(2,1)S(1)}, bf16[1,1,4096,128]{3,2,1,0:T(8,128)(2,1)}, u32[]{:S(2)}) copy-start(bf16[1,1,4096,128]{3,2,1,0:T(8,128)(2,1)} %param.7) | copy-start | bytes 3145732
  33.7 25.2 %collective-permute-start.21 = (bf16[1280,128]{1,0:T(8,128)(2,1)S(1)}, bf16[1280,128]{1,0:T(8,128)(2,1)S(1)}, u32[]{:S(2)}, u32[]{:S(2)}) collective-permute-start(bf16[1280,128]{1,0:T(8,128)(2,1)S(1)} %get-tuple-element.110), channel_id=1, source_target_pairs={{0,4},{1,5},{2,6},{3,7},{4,0},{5,1},{6,2},{7,3},{8,12},{9,13},{10,... | collective-permute-start | bytes 983048 | tf_op jit(solution)/shard_map/ppermute | solution.py:330
  57.3 1.6 %collective-permute-start.22 = (bf16[1024,128]{1,0:T(8,128)(2,1)S(1)}, bf16[1024,128]{1,0:T(8,128)(2,1)S(1)}, u32[]{:S(2)}, u32[]{:S(2)}) collective-permute-start(bf16[1024,128]{1,0:T(8,128)(2,1)S(1)} %get-tuple-element.111), channel_id=1, source_target_pairs={{0,4},{1,5},{2,6},{3,7},{4,0},{5,1},{6,2},{7,3},{8,12},{9,13},{10,... | collective-permute-start | bytes 786440 | tf_op jit(solution)/shard_map/ppermute | solution.py:330
  62.1 2.1 %collective-permute-start.23 = (bf16[2304,128]{1,0:T(8,128)(2,1)S(1)}, bf16[2304,128]{1,0:T(8,128)(2,1)S(1)}, u32[]{:S(2)}, u32[]{:S(2)}) collective-permute-start(bf16[2304,128]{1,0:T(8,128)(2,1)S(1)} %get-tuple-element.118), channel_id=1, source_target_pairs={{0,4},{1,5},{2,6},{3,7},{4,0},{5,1},{6,2},{7,3},{8,12},{9,13},{10,... | collective-permute-start | bytes 1769480 | tf_op jit(solution)/shard_map/ppermute | solution.py:330

commit v5 on v4

--- a/solution.py
+++ b/solution.py
@@ -248,12 +248,12 @@
     )(*tables, *fixed, *arrived, *keeps)
 
 
-def finish(begin, end, odd_column, tiles, pairs, cuts, table, own, given, regions, left, state, done):
+def finish(begin, end, odd_column, tiles, pairs, cuts, table, own, given, regions, left, state, done, extra=()):
     bond = state.shape[1]
     parts = [k for k in range(len(own)) if cuts[k] < end and cuts[k + 1] > begin]
     groups = [(p, min(GROUP, end - p)) for p in range(begin, end, GROUP)]
-    refs_in = [*(own[k] for k in parts), *given, left, state, *done]
-    count, fixed = len(parts), len(parts) + len(given) + 2
+    refs_in = [*(own[k] for k in parts), *given, *extra, left, state, *done]
+    count, fixed = len(parts), len(parts) + len(given) + len(extra) + 2
 
     def kernel(table, *refs):
         own_refs = dict(zip(parts, refs))
@@ -306,7 +306,7 @@
             pltpu.SemaphoreType.DMA((2, len(groups))),
         ],
         compiler_params=params(),
-        cost_estimate=cost(FINISH * (end - begin) / tiles),
+        cost_estimate=cost(FINISH if odd_column == 0 else FINISH * (end - begin) / tiles),
         name="finish",
     )(table, *refs_in)
 
@@ -346,7 +346,8 @@
     own = [head, *rest]
     odd_cols = [(2 * z + 1, 2 * z) for z in range(layers)]
     odd = [move(part, swap) for part in own]
-    odd_table = move(lax.optimization_barrier((table, head))[0], swap)
+    listed, _ = lax.optimization_barrier((table, head))
+    odd_table = move(listed, swap)
     odd_edges = [move(first_edge, [(a, b, partner) for a, b in odd_cols]), move(last_edge, [(a, b, other) for a, b in odd_cols])]
 
     keeps = [wide]
@@ -367,7 +368,6 @@
                     came.append(halo if end else move(sent[k][-1], [(above, here, other)]))
                 if end and k == count - 2:
                     halo = move(sent[k + 1][-1], [(above, here, other)])
-                    came.append(halo)
             give = []
             if end and k == count - 2:
                 middle = inner[k + 1] // 2
@@ -392,7 +392,8 @@
                     done = []
                     for odd_column in (0, 1):
                         takes = (given, give) if odd_column else ([], [])
-                        keeps[0], *done = finish(0, half, odd_column, tiles, pairs, cuts, table, own, *takes, left, keeps[0], done)
+                        extra = [] if odd_column else [halo]
+                        keeps[0], *done = finish(0, half, odd_column, tiles, pairs, cuts, table, own, *takes, left, keeps[0], done, extra)
                 else:
                     _, env, grad = finish(half, tiles, None, tiles, pairs, cuts, table, own, given, give, left, keeps[0], done)
             leaving.append(result[2:])

time: 67.9 us -> 66.8 us (0.984)
  starting transfers between devices: 40.2 us -> 39.5 us
    ppermute x24, starting transfers between devices: 40.2 us -> 39.5 us  [move(): return lax.ppermute(value, ('col', 'sec'), both)]
  transfers between devices with their start and end apart: 24 -> 24, of which waited for: 3 -> 4; matrix products, arithmetic and copies ran while one was open for 0% -> 0% of each run, Pallas kernels for 25% -> 26%
where the time goes in v5:
time: 66.8 us; the launch traced here: 66.3 us
  starting transfers between devices  39.5 us (59%)
  Pallas kernels  22.3 us (33%)
  waiting for transfers between devices  3.34 us (5%)
  between operations  1.25 us (2%)
    ppermute x24, starting transfers between devices, move(): return lax.ppermute(value, ('col', 'sec'), both)  39.5 us
    pallas_call x14, Pallas kernels, pair_step(): pl.pallas_call(kernel, in_specs=[SMEM] * 2 + [VMEM] * (first - 2 + len(ke...  8.68 us
    pallas_call x3, Pallas kernels, finish(): pl.pallas_call(kernel, in_specs=[SMEM] + [VMEM] * fixed + [HBM] * len(don...  6.31 us
    pallas_call x2, Pallas kernels, prepare(): pl.pallas_call(kernel, in_specs=[HBM, HBM], out_specs=[VMEM] * len(outs),...  5.91 us
    ppermute x24, waiting for transfers between devices, move(): return lax.ppermute(value, ('col', 'sec'), both)  3.34 us
    pallas_call x1, Pallas kernels, prepare_edges(): pl.pallas_call(kernel, in_specs=[HBM, HBM, HBM], out_specs=[VMEM, VMEM],...  1.36 us
  transfers between devices with their start and end apart: 24, of which 4 were waited for; matrix products, arithmetic and copies ran while one was open for 0% of the time, Pallas kernels for 26%

profile of v5, /device:TPU:3, one launch (start us, length us, event | category | flops | bytes accessed | tf_op | source)
XLA Modules:
  0.0 66.3 jit_solution(11726059343038927485)
XLA Ops:
  0.6 1.4 %prepare_edges.1 = (bf16[384,640]{1,0:T(8,128)(2,1)S(1)}, bf16[384,640]{1,0:T(8,128)(2,1)S(1)}) custom-call(s32[4,32]{1,0:T(4,128)} %bitcast.11, bf16[4096,4,128]{2,1,0:T(4,128)(2,1)} %bitcast.30, bf16[4096,128]{1,0:T(8,128)(2,1)} %bitcast.34), custom_call_target="tpu_custom_call" | custom-call | flops 125000000 | tf_op jit(solution)/shard_map/prepare_edges/pallas_call | solution.py:108
  2.0 1.3 %collective-permute-start.5 = (bf16[384,640]{1,0:T(8,128)(2,1)S(1)}, bf16[384,640]{1,0:T(8,128)(2,1)S(1)}, u32[]{:S(2)}, u32[]{:S(2)}) collective-permute-start(bf16[384,640]{1,0:T(8,128)(2,1)S(1)} %get-tuple-element.71), channel_id=1, source_target_pairs={{4,1},{5,0},{6,3},{7,2},{12,9},{13,8},{14,11},{15,10},{20,17},{21,... | collective-permute-start | bytes 1474568 | tf_op jit(solution)/shard_map/ppermute | solution.py:330
  3.3 3.7 %collective-permute-start.3 = (bf16[384,640]{1,0:T(8,128)(2,1)S(1)}, bf16[384,640]{1,0:T(8,128)(2,1)S(1)}, u32[]{:S(2)}, u32[]{:S(2)}) collective-permute-start(bf16[384,640]{1,0:T(8,128)(2,1)S(1)} %get-tuple-element.70), channel_id=1, source_target_pairs={{5,2},{6,1},{13,10},{14,9},{21,18},{22,17},{29,26},{30,25}} | collective-permute-start | bytes 1474568 | tf_op jit(solution)/shard_map/ppermute | solution.py:330
  7.0 2.6 %prepare.2.refs_0_ = bf16[1792,512]{1,0:T(8,128)(2,1)S(1)} custom-call(bf16[4096,4,128]{2,1,0:T(4,128)(2,1)} %bitcast.31, bf16[4096,128]{1,0:T(8,128)(2,1)} %bitcast.35), custom_call_target="tpu_custom_call" | custom-call | flops 437500000 | tf_op jit(solution)/shard_map/prepare/pallas_call | solution.py:161
  9.6 0.1 collective-permute-start.4
  9.7 0.5 collective-permute-start
  10.2 3.3 %prepare.3 = (bf16[1536,512]{1,0:T(8,128)(2,1)S(1)}, bf16[768,512]{1,0:T(8,128)(2,1)S(1)}, bf16[5120,128]{1,0:T(8,128)(2,1)S(1)}) custom-call(bf16[4096,4,128]{2,1,0:T(4,128)(2,1)} %bitcast.32, bf16[4096,128]{1,0:T(8,128)(2,1)} %bitcast.36), custom_call_target="tpu_custom_call" | custom-call | flops 562499968 | tf_op jit(solution)/shard_map/prepare/pallas_call | solution.py:161
  13.5 0.2 collective-permute-start.2
  13.7 0.4 collective-permute-start.1
  14.1 0.6 pair_step.14
  14.7 0.6 pair_step.15
  15.4 0.7 %collective-permute-start.10 = (bf16[512,128]{1,0:T(8,128)(2,1)S(1)}, bf16[512,128]{1,0:T(8,128)(2,1)S(1)}, u32[]{:S(2)}, u32[]{:S(2)}) collective-permute-start(bf16[512,128]{1,0:T(8,128)(2,1)S(1)} %get-tuple-element.83), channel_id=1, source_target_pairs={{24,17},{25,16},{26,19},{27,18}} | collective-permute-start | bytes 393224 | tf_op jit(solution)/shard_map/ppermute | solution.py:330
  16.1 0.7 %collective-permute-start.9 = (bf16[1536,128]{1,0:T(8,128)(2,1)S(1)}, bf16[1536,128]{1,0:T(8,128)(2,1)S(1)}, u32[]{:S(2)}, u32[]{:S(2)}) collective-permute-start(bf16[1536,128]{1,0:T(8,128)(2,1)S(1)} %get-tuple-element.82), channel_id=1, source_target_pairs={{24,16},{25,17},{26,18},{27,19}} | collective-permute-start | bytes 1179656 | tf_op jit(solution)/shard_map/ppermute | solution.py:330
  16.7 1.4 %collective-permute-done.1.refs_2_.refs_3_.refs_0_ = bf16[1536,512]{1,0:T(8,128)(2,1)S(1)} collective-permute-done((bf16[1536,512]{1,0:T(8,128)(2,1)S(1)}, bf16[1536,512]{1,0:T(8,128)(2,1)S(1)}, u32[]{:S(2)}, u32[]{:S(2)}) %collective-permute-start.1) | collective-permute-done | bytes 1572896 | tf_op jit(solution)/shard_map/ppermute | solution.py:330
  18.1 0.6 pair_step.16
  18.8 0.7 %collective-permute-start.8 = (bf16[1536,128]{1,0:T(8,128)(2,1)S(1)}, bf16[1536,128]{1,0:T(8,128)(2,1)S(1)}, u32[]{:S(2)}, u32[]{:S(2)}) collective-permute-start(bf16[1536,128]{1,0:T(8,128)(2,1)S(1)} %get-tuple-element.81), channel_id=1, source_target_pairs={{24,16},{25,17},{26,18},{27,19}} | collective-permute-start | bytes 1179656 | tf_op jit(solution)/shard_map/ppermute | solution.py:330
  19.5 0.6 pair_step.17
  20.1 0.7 %collective-permute-start.7 = (bf16[512,128]{1,0:T(8,128)(2,1)S(1)}, bf16[512,128]{1,0:T(8,128)(2,1)S(1)}, u32[]{:S(2)}, u32[]{:S(2)}) collective-permute-start(bf16[512,128]{1,0:T(8,128)(2,1)S(1)} %get-tuple-element.80), channel_id=1, source_target_pairs={{25,18},{26,17}} | collective-permute-start | bytes 393224 | tf_op jit(solution)/shard_map/ppermute | solution.py:330
  20.8 0.7 %collective-permute-start.6 = (bf16[1024,128]{1,0:T(8,128)(2,1)S(1)}, bf16[1024,128]{1,0:T(8,128)(2,1)S(1)}, u32[]{:S(2)}, u32[]{:S(2)}) collective-permute-start(bf16[1024,128]{1,0:T(8,128)(2,1)S(1)} %get-tuple-element.79), channel_id=1, source_target_pairs={{24,16},{25,17},{26,18},{27,19}} | collective-permute-start | bytes 786440 | tf_op jit(solution)/shard_map/ppermute | solution.py:330
  21.5 0.6 pair_step.18
  22.1 0.7 %collective-permute-start.15 = (bf16[512,128]{1,0:T(8,128)(2,1)S(1)}, bf16[512,128]{1,0:T(8,128)(2,1)S(1)}, u32[]{:S(2)}, u32[]{:S(2)}) collective-permute-start(bf16[512,128]{1,0:T(8,128)(2,1)S(1)} %get-tuple-element.94), channel_id=1, source_target_pairs={{16,9},{17,8},{18,11},{19,10}} | collective-permute-start | bytes 393224 | tf_op jit(solution)/shard_map/ppermute | solution.py:330
  22.8 0.7 %collective-permute-start.14 = (bf16[1024,128]{1,0:T(8,128)(2,1)S(1)}, bf16[1024,128]{1,0:T(8,128)(2,1)S(1)}, u32[]{:S(2)}, u32[]{:S(2)}) collective-permute-start(bf16[1024,128]{1,0:T(8,128)(2,1)S(1)} %get-tuple-element.93), channel_id=1, source_target_pairs={{16,8},{17,9},{18,10},{19,11}} | collective-permute-start | bytes 786440 | tf_op jit(solution)/shard_map/ppermute | solution.py:330
  23.5 0.6 pair_step.19
  24.1 0.7 %collective-permute-start.13 = (bf16[1536,128]{1,0:T(8,128)(2,1)S(1)}, bf16[1536,128]{1,0:T(8,128)(2,1)S(1)}, u32[]{:S(2)}, u32[]{:S(2)}) collective-permute-start(bf16[1536,128]{1,0:T(8,128)(2,1)S(1)} %get-tuple-element.92), channel_id=1, source_target_pairs={{16,8},{17,9},{18,10},{19,11}} | collective-permute-start | bytes 1179656 | tf_op jit(solution)/shard_map/ppermute | solution.py:330
  24.8 0.6 pair_step.20
  25.5 0.7 %collective-permute-start.12 = (bf16[512,128]{1,0:T(8,128)(2,1)S(1)}, bf16[512,128]{1,0:T(8,128)(2,1)S(1)}, u32[]{:S(2)}, u32[]{:S(2)}) collective-permute-start(bf16[512,128]{1,0:T(8,128)(2,1)S(1)} %get-tuple-element.91), channel_id=1, source_target_pairs={{17,10},{18,9}} | collective-permute-start | bytes 393224 | tf_op jit(solution)/shard_map/ppermute | solution.py:330
  26.1 0.9 %collective-permute-start.11 = (bf16[1536,128]{1,0:T(8,128)(2,1)S(1)}, bf16[1536,128]{1,0:T(8,128)(2,1)S(1)}, u32[]{:S(2)}, u32[]{:S(2)}) collective-permute-start(bf16[1536,128]{1,0:T(8,128)(2,1)S(1)} %get-tuple-element.90), channel_id=1, source_target_pairs={{16,8},{17,9},{18,10},{19,11}} | collective-permute-start | bytes 1179656 | tf_op jit(solution)/shard_map/ppermute | solution.py:330
  27.0 0.6 pair_step.21
  27.7 0.7 %collective-permute-start.19 = (bf16[512,128]{1,0:T(8,128)(2,1)S(1)}, bf16[512,128]{1,0:T(8,128)(2,1)S(1)}, u32[]{:S(2)}, u32[]{:S(2)}) collective-permute-start(bf16[512,128]{1,0:T(8,128)(2,1)S(1)} %get-tuple-element.104), channel_id=1, source_target_pairs={{8,0},{9,1},{10,2},{11,3}} | collective-permute-start | bytes 393224 | tf_op jit(solution)/shard_map/ppermute | solution.py:330
  28.3 0.7 %collective-permute-start.20 = (bf16[512,128]{1,0:T(8,128)(2,1)S(1)}, bf16[512,128]{1,0:T(8,128)(2,1)S(1)}, u32[]{:S(2)}, u32[]{:S(2)}) collective-permute-start(bf16[512,128]{1,0:T(8,128)(2,1)S(1)} %get-tuple-element.105), channel_id=1, source_target_pairs={{8,1},{9,0},{10,3},{11,2}} | collective-permute-start | bytes 393224 | tf_op jit(solution)/shard_map/ppermute | solution.py:330
  29.0 0.6 pair_step.22
  29.6 0.7 %collective-permute-start.18 = (bf16[1536,128]{1,0:T(8,128)(2,1)S(1)}, bf16[1536,128]{1,0:T(8,128)(2,1)S(1)}, u32[]{:S(2)}, u32[]{:S(2)}) collective-permute-start(bf16[1536,128]{1,0:T(8,128)(2,1)S(1)} %get-tuple-element.103), channel_id=1, source_target_pairs={{8,0},{9,1},{10,2},{11,3}} | collective-permute-start | bytes 1179656 | tf_op jit(solution)/shard_map/ppermute | solution.py:330
  30.4 0.6 pair_step.23
  31.0 0.7 %collective-permute-start.17 = (bf16[512,128]{1,0:T(8,128)(2,1)S(1)}, bf16[512,128]{1,0:T(8,128)(2,1)S(1)}, u32[]{:S(2)}, u32[]{:S(2)}) collective-permute-start(bf16[512,128]{1,0:T(8,128)(2,1)S(1)} %get-tuple-element.102), channel_id=1, source_target_pairs={{9,2},{10,1}} | collective-permute-start | bytes 393224 | tf_op jit(solution)/shard_map/ppermute | solution.py:330
  31.7 0.7 %collective-permute-start.16 = (bf16[2048,128]{1,0:T(8,128)(2,1)S(1)}, bf16[2048,128]{1,0:T(8,128)(2,1)S(1)}, u32[]{:S(2)}, u32[]{:S(2)}) collective-permute-start(bf16[2048,128]{1,0:T(8,128)(2,1)S(1)} %get-tuple-element.101), channel_id=1, source_target_pairs={{8,0},{9,1},{10,2},{11,3}} | collective-permute-start | bytes 1572872 | tf_op jit(solution)/shard_map/ppermute | solution.py:330
  32.4 0.6 pair_step.24
  33.0 0.6 pair_step.25
  33.7 19.6 %collective-permute-start.22 = (bf16[1024,128]{1,0:T(8,128)(2,1)S(1)}, bf16[1024,128]{1,0:T(8,128)(2,1)S(1)}, u32[]{:S(2)}, u32[]{:S(2)}) collective-permute-start(bf16[1024,128]{1,0:T(8,128)(2,1)S(1)} %get-tuple-element.111), channel_id=1, source_target_pairs={{0,4},{1,5},{2,6},{3,7},{4,0},{5,1},{6,2},{7,3},{8,12},{9,13},{10,... | collective-permute-start | bytes 786440 | tf_op jit(solution)/shard_map/ppermute | solution.py:330
  53.2 0.1 collective-permute-start.21
  53.3 0.6 finish.3
  54.0 0.4 collective-permute-done.22.refs_2_
  54.4 0.5 collective-permute-done.21.refs_1_
  54.9 2.5 %finish.4 = (bf16[4608,128]{1,0:T(8,128)(2,1)S(1)}, bf16[4096,128]{1,0:T(8,128)(2,1)}, bf16[4096,4,128]{2,1,0:T(4,128)(2,1)}) custom-call(s32[4,32]{1,0:T(4,128)S(1)} %bitcast.26, bf16[1792,512]{1,0:T(8,128)(2,1)S(1)} %prepare.2.refs_0_, ...), custom_call_target="tpu_custom_call", output_to_operand_aliasing={{0}: (5, {}), {1}: (6, {}), {2}: (7, {})} | custom-call | flops 1500000000 | tf_op jit(solution)/shard_map/finish/pallas_call | solution.py:297
  57.4 0.6 pair_step.26
  58.1 3.4 %collective-permute-start.23 = (bf16[2304,128]{1,0:T(8,128)(2,1)S(1)}, bf16[2304,128]{1,0:T(8,128)(2,1)S(1)}, u32[]{:S(2)}, u32[]{:S(2)}) collective-permute-start(bf16[2304,128]{1,0:T(8,128)(2,1)S(1)} %get-tuple-element.118), channel_id=1, source_target_pairs={{0,4},{1,5},{2,6},{3,7},{4,0},{5,1},{6,2},{7,3},{8,12},{9,13},{10,... | collective-permute-start | bytes 1769480 | tf_op jit(solution)/shard_map/ppermute | solution.py:330
  61.4 0.6 pair_step.27
  62.0 1.0 %collective-permute-done.23.refs_3_ = bf16[2304,128]{1,0:T(8,128)(2,1)S(1)} collective-permute-done((bf16[2304,128]{1,0:T(8,128)(2,1)S(1)}, bf16[2304,128]{1,0:T(8,128)(2,1)S(1)}, u32[]{:S(2)}, u32[]{:S(2)}) %collective-permute-start.23) | collective-permute-done | bytes 589856 | tf_op jit(solution)/shard_map/ppermute | solution.py:330
  63.0 3.1 %finish.5 = (bf16[4608,128]{1,0:T(8,128)(2,1)S(1)}, bf16[4096,128]{1,0:T(8,128)(2,1)}, bf16[4096,4,128]{2,1,0:T(4,128)(2,1)}) custom-call(s32[4,32]{1,0:T(4,128)S(1)} %bitcast.29, bf16[1792,512]{1,0:T(8,128)(2,1)S(1)} %prepare.2.refs_0_, ...), custom_call_target="tpu_custom_call", output_to_operand_aliasing={{0}: (6, {}), {1}: (7, {}), {2}: (8, {})} | custom-call | flops 2500000000 | tf_op jit(solution)/shard_map/finish/pallas_call | solution.py:297
  (24 shorter events, 0.1 us)
Async XLA Ops:
  2.0 7.7 %copy-start.1 = (s32[1,1,32,4]{2,3,1,0:T(4,128)S(1)}, s32[1,1,32,4]{2,3,1,0:T(4,128)}, u32[]{:S(2)}) copy-start(s32[1,1,32,4]{2,3,1,0:T(4,128)} %param.6) | copy-start | bytes 1540
  2.0 12.1 %collective-permute-start.5 = (bf16[384,640]{1,0:T(8,128)(2,1)S(1)}, bf16[384,640]{1,0:T(8,128)(2,1)S(1)}, u32[]{:S(2)}, u32[]{:S(2)}) collective-permute-start(bf16[384,640]{1,0:T(8,128)(2,1)S(1)} %get-tuple-element.71), channel_id=1, source_target_pairs={{4,1},{5,0},{6,3},{7,2},{12,9},{13,8},{14,11},{15,10},{20,17},{21,... | collective-permute-start | bytes 1474568 | tf_op jit(solution)/shard_map/ppermute | solution.py:330
  3.3 16.1 %collective-permute-start.3 = (bf16[384,640]{1,0:T(8,128)(2,1)S(1)}, bf16[384,640]{1,0:T(8,128)(2,1)S(1)}, u32[]{:S(2)}, u32[]{:S(2)}) collective-permute-start(bf16[384,640]{1,0:T(8,128)(2,1)S(1)} %get-tuple-element.70), channel_id=1, source_target_pairs={{5,2},{6,1},{13,10},{14,9},{21,18},{22,17},{29,26},{30,25}} | collective-permute-start | bytes 1474568 | tf_op jit(solution)/shard_map/ppermute | solution.py:330
  9.6 5.1 %collective-permute-start.4 = (bf16[1792,512]{1,0:T(8,128)(2,1)S(1)}, bf16[1792,512]{1,0:T(8,128)(2,1)S(1)}, u32[]{:S(2)}, u32[]{:S(2)}) collective-permute-start(bf16[1792,512]{1,0:T(8,128)(2,1)S(1)} %prepare.2.refs_0_), channel_id=1, source_target_pairs={{0,4},{1,5},{2,6},{3,7},{4,0},{5,1},{6,2},{7,3},{8,12},{9,13},{10,... | collective-permute-start | bytes 5505032 | tf_op jit(solution)/shard_map/ppermute | solution.py:330
  9.7 4.0 %collective-permute-start = (s32[4,32]{1,0:T(4,128)S(1)}, s32[4,32]{1,0:T(4,128)S(1)}, u32[]{:S(2)}, u32[]{:S(2)}) collective-permute-start(s32[4,32]{1,0:T(4,128)S(1)} %bitcast.12), channel_id=1, source_target_pairs={{0,4},{1,5},{2,6},{3,7},{4,0},{5,1},{6,2},{7,3},{8,12},{9,13},{10,... | collective-permute-start | bytes 1544 | tf_op jit(solution)/shard_map/ppermute | solution.py:330
  13.5 5.9 %collective-permute-start.2 = (bf16[768,512]{1,0:T(8,128)(2,1)S(1)}, bf16[768,512]{1,0:T(8,128)(2,1)S(1)}, u32[]{:S(2)}, u32[]{:S(2)}) collective-permute-start(bf16[768,512]{1,0:T(8,128)(2,1)S(1)} %get-tuple-element.68.refs_1_.refs_2_), channel_id=1, source_target_pairs={{0,4},{1,5},{2,6},{3,7},{4,0},{5,1},{6,2},{7,3},{8,12},{9,13},{10,... | collective-permute-start | bytes 2359304 | tf_op jit(solution)/shard_map/ppermute | solution.py:330
  13.7 4.4 %collective-permute-start.1 = (bf16[1536,512]{1,0:T(8,128)(2,1)S(1)}, bf16[1536,512]{1,0:T(8,128)(2,1)S(1)}, u32[]{:S(2)}, u32[]{:S(2)}) collective-permute-start(bf16[1536,512]{1,0:T(8,128)(2,1)S(1)} %get-tuple-element.67.refs_1_.refs_0_), channel_id=1, source_target_pairs={{0,4},{1,5},{2,6},{3,7},{4,0},{5,1},{6,2},{7,3},{8,12},{9,13},{10,... | collective-permute-start | bytes 4718600 | tf_op jit(solution)/shard_map/ppermute | solution.py:330
  15.4 6.1 %collective-permute-start.10 = (bf16[512,128]{1,0:T(8,128)(2,1)S(1)}, bf16[512,128]{1,0:T(8,128)(2,1)S(1)}, u32[]{:S(2)}, u32[]{:S(2)}) collective-permute-start(bf16[512,128]{1,0:T(8,128)(2,1)S(1)} %get-tuple-element.83), channel_id=1, source_target_pairs={{24,17},{25,16},{26,19},{27,18}} | collective-permute-start | bytes 393224 | tf_op jit(solution)/shard_map/ppermute | solution.py:330
  16.1 5.4 %collective-permute-start.9 = (bf16[1536,128]{1,0:T(8,128)(2,1)S(1)}, bf16[1536,128]{1,0:T(8,128)(2,1)S(1)}, u32[]{:S(2)}, u32[]{:S(2)}) collective-permute-start(bf16[1536,128]{1,0:T(8,128)(2,1)S(1)} %get-tuple-element.82), channel_id=1, source_target_pairs={{24,16},{25,17},{26,18},{27,19}} | collective-permute-start | bytes 1179656 | tf_op jit(solution)/shard_map/ppermute | solution.py:330
  18.8 4.7 %collective-permute-start.8 = (bf16[1536,128]{1,0:T(8,128)(2,1)S(1)}, bf16[1536,128]{1,0:T(8,128)(2,1)S(1)}, u32[]{:S(2)}, u32[]{:S(2)}) collective-permute-start(bf16[1536,128]{1,0:T(8,128)(2,1)S(1)} %get-tuple-element.81), channel_id=1, source_target_pairs={{24,16},{25,17},{26,18},{27,19}} | collective-permute-start | bytes 1179656 | tf_op jit(solution)/shard_map/ppermute | solution.py:330
  20.1 4.7 %collective-permute-start.7 = (bf16[512,128]{1,0:T(8,128)(2,1)S(1)}, bf16[512,128]{1,0:T(8,128)(2,1)S(1)}, u32[]{:S(2)}, u32[]{:S(2)}) collective-permute-start(bf16[512,128]{1,0:T(8,128)(2,1)S(1)} %get-tuple-element.80), channel_id=1, source_target_pairs={{25,18},{26,17}} | collective-permute-start | bytes 393224 | tf_op jit(solution)/shard_map/ppermute | solution.py:330
  20.8 4.0 %collective-permute-start.6 = (bf16[1024,128]{1,0:T(8,128)(2,1)S(1)}, bf16[1024,128]{1,0:T(8,128)(2,1)S(1)}, u32[]{:S(2)}, u32[]{:S(2)}) collective-permute-start(bf16[1024,128]{1,0:T(8,128)(2,1)S(1)} %get-tuple-element.79), channel_id=1, source_target_pairs={{24,16},{25,17},{26,18},{27,19}} | collective-permute-start | bytes 786440 | tf_op jit(solution)/shard_map/ppermute | solution.py:330
  22.1 4.9 %collective-permute-start.15 = (bf16[512,128]{1,0:T(8,128)(2,1)S(1)}, bf16[512,128]{1,0:T(8,128)(2,1)S(1)}, u32[]{:S(2)}, u32[]{:S(2)}) collective-permute-start(bf16[512,128]{1,0:T(8,128)(2,1)S(1)} %get-tuple-element.94), channel_id=1, source_target_pairs={{16,9},{17,8},{18,11},{19,10}} | collective-permute-start | bytes 393224 | tf_op jit(solution)/shard_map/ppermute | solution.py:330
  22.8 4.2 %collective-permute-start.14 = (bf16[1024,128]{1,0:T(8,128)(2,1)S(1)}, bf16[1024,128]{1,0:T(8,128)(2,1)S(1)}, u32[]{:S(2)}, u32[]{:S(2)}) collective-permute-start(bf16[1024,128]{1,0:T(8,128)(2,1)S(1)} %get-tuple-element.93), channel_id=1, source_target_pairs={{16,8},{17,9},{18,10},{19,11}} | collective-permute-start | bytes 786440 | tf_op jit(solution)/shard_map/ppermute | solution.py:330
  24.1 4.9 %collective-permute-start.13 = (bf16[1536,128]{1,0:T(8,128)(2,1)S(1)}, bf16[1536,128]{1,0:T(8,128)(2,1)S(1)}, u32[]{:S(2)}, u32[]{:S(2)}) collective-permute-start(bf16[1536,128]{1,0:T(8,128)(2,1)S(1)} %get-tuple-element.92), channel_id=1, source_target_pairs={{16,8},{17,9},{18,10},{19,11}} | collective-permute-start | bytes 1179656 | tf_op jit(solution)/shard_map/ppermute | solution.py:330
  25.5 4.9 %collective-permute-start.12 = (bf16[512,128]{1,0:T(8,128)(2,1)S(1)}, bf16[512,128]{1,0:T(8,128)(2,1)S(1)}, u32[]{:S(2)}, u32[]{:S(2)}) collective-permute-start(bf16[512,128]{1,0:T(8,128)(2,1)S(1)} %get-tuple-element.91), channel_id=1, source_target_pairs={{17,10},{18,9}} | collective-permute-start | bytes 393224 | tf_op jit(solution)/shard_map/ppermute | solution.py:330
  26.1 4.2 %collective-permute-start.11 = (bf16[1536,128]{1,0:T(8,128)(2,1)S(1)}, bf16[1536,128]{1,0:T(8,128)(2,1)S(1)}, u32[]{:S(2)}, u32[]{:S(2)}) collective-permute-start(bf16[1536,128]{1,0:T(8,128)(2,1)S(1)} %get-tuple-element.90), channel_id=1, source_target_pairs={{16,8},{17,9},{18,10},{19,11}} | collective-permute-start | bytes 1179656 | tf_op jit(solution)/shard_map/ppermute | solution.py:330
  27.7 4.7 %collective-permute-start.19 = (bf16[512,128]{1,0:T(8,128)(2,1)S(1)}, bf16[512,128]{1,0:T(8,128)(2,1)S(1)}, u32[]{:S(2)}, u32[]{:S(2)}) collective-permute-start(bf16[512,128]{1,0:T(8,128)(2,1)S(1)} %get-tuple-element.104), channel_id=1, source_target_pairs={{8,0},{9,1},{10,2},{11,3}} | collective-permute-start | bytes 393224 | tf_op jit(solution)/shard_map/ppermute | solution.py:330
  28.3 4.1 %collective-permute-start.20 = (bf16[512,128]{1,0:T(8,128)(2,1)S(1)}, bf16[512,128]{1,0:T(8,128)(2,1)S(1)}, u32[]{:S(2)}, u32[]{:S(2)}) collective-permute-start(bf16[512,128]{1,0:T(8,128)(2,1)S(1)} %get-tuple-element.105), channel_id=1, source_target_pairs={{8,1},{9,0},{10,3},{11,2}} | collective-permute-start | bytes 393224 | tf_op jit(solution)/shard_map/ppermute | solution.py:330
  29.6 3.4 %collective-permute-start.18 = (bf16[1536,128]{1,0:T(8,128)(2,1)S(1)}, bf16[1536,128]{1,0:T(8,128)(2,1)S(1)}, u32[]{:S(2)}, u32[]{:S(2)}) collective-permute-start(bf16[1536,128]{1,0:T(8,128)(2,1)S(1)} %get-tuple-element.103), channel_id=1, source_target_pairs={{8,0},{9,1},{10,2},{11,3}} | collective-permute-start | bytes 1179656 | tf_op jit(solution)/shard_map/ppermute | solution.py:330
  31.0 22.3 %collective-permute-start.17 = (bf16[512,128]{1,0:T(8,128)(2,1)S(1)}, bf16[512,128]{1,0:T(8,128)(2,1)S(1)}, u32[]{:S(2)}, u32[]{:S(2)}) collective-permute-start(bf16[512,128]{1,0:T(8,128)(2,1)S(1)} %get-tuple-element.102), channel_id=1, source_target_pairs={{9,2},{10,1}} | collective-permute-start | bytes 393224 | tf_op jit(solution)/shard_map/ppermute | solution.py:330
  31.7 25.7 %collective-permute-start.16 = (bf16[2048,128]{1,0:T(8,128)(2,1)S(1)}, bf16[2048,128]{1,0:T(8,128)(2,1)S(1)}, u32[]{:S(2)}, u32[]{:S(2)}) collective-permute-start(bf16[2048,128]{1,0:T(8,128)(2,1)S(1)} %get-tuple-element.101), channel_id=1, source_target_pairs={{8,0},{9,1},{10,2},{11,3}} | collective-permute-start | bytes 1572872 | tf_op jit(solution)/shard_map/ppermute | solution.py:330
  33.0 20.3 %copy-start = (bf16[1,1,4096,128]{3,2,1,0:T(8,128)(2,1)S(1)}, bf16[1,1,4096,128]{3,2,1,0:T(8,128)(2,1)}, u32[]{:S(2)}) copy-start(bf16[1,1,4096,128]{3,2,1,0:T(8,128)(2,1)} %param.7) | copy-start | bytes 3145732
  33.7 20.7 %collective-permute-start.22 = (bf16[1024,128]{1,0:T(8,128)(2,1)S(1)}, bf16[1024,128]{1,0:T(8,128)(2,1)S(1)}, u32[]{:S(2)}, u32[]{:S(2)}) collective-permute-start(bf16[1024,128]{1,0:T(8,128)(2,1)S(1)} %get-tuple-element.111), channel_id=1, source_target_pairs={{0,4},{1,5},{2,6},{3,7},{4,0},{5,1},{6,2},{7,3},{8,12},{9,13},{10,... | collective-permute-start | bytes 786440 | tf_op jit(solution)/shard_map/ppermute | solution.py:330
  53.2 1.6 %collective-permute-start.21 = (bf16[1280,128]{1,0:T(8,128)(2,1)S(1)}, bf16[1280,128]{1,0:T(8,128)(2,1)S(1)}, u32[]{:S(2)}, u32[]{:S(2)}) collective-permute-start(bf16[1280,128]{1,0:T(8,128)(2,1)S(1)} %get-tuple-element.110), channel_id=1, source_target_pairs={{0,4},{1,5},{2,6},{3,7},{4,0},{5,1},{6,2},{7,3},{8,12},{9,13},{10,... | collective-permute-start | bytes 983048 | tf_op jit(solution)/shard_map/ppermute | solution.py:330
  58.1 5.0 %collective-permute-start.23 = (bf16[2304,128]{1,0:T(8,128)(2,1)S(1)}, bf16[2304,128]{1,0:T(8,128)(2,1)S(1)}, u32[]{:S(2)}, u32[]{:S(2)}) collective-permute-start(bf16[2304,128]{1,0:T(8,128)(2,1)S(1)} %get-tuple-element.118), channel_id=1, source_target_pairs={{0,4},{1,5},{2,6},{3,7},{4,0},{5,1},{6,2},{7,3},{8,12},{9,13},{10,... | collective-permute-start | bytes 1769480 | tf_op jit(solution)/shard_map/ppermute | solution.py:330

commit v6 on v5

--- a/solution.py
+++ b/solution.py
@@ -13,8 +13,8 @@
 FILL, EDGE, MAIN = range(3)
 PREPARE, FIRST, SECOND, STEP, COLLECT, FINISH = 1e9, 2e10, 2e10, 1e10, 1e9, 4e9
 VMEM = pl.BlockSpec(memory_space=pltpu.VMEM)
-SMEM = pl.BlockSpec(memory_space=pltpu.SMEM)
 HBM = pl.BlockSpec(memory_space=pltpu.HBM)
+ANY = pl.BlockSpec(memory_space=pl.ANY)
 
 
 def params():
@@ -128,7 +128,7 @@
     chosen = range(first, final)
     groups = [(p, min(GROUP, cuts[k + 1] - p)) for k in chosen for p in range(cuts[k], cuts[k + 1], GROUP)]
     begin, end = cuts[first], cuts[final]
-    tail = end == tiles
+    with_environment = first == 0
 
     def kernel(source, environment, *refs):
         parts, refs = refs[: len(chosen)], refs[len(chosen) :]
@@ -138,7 +138,7 @@
         for g, (p, size) in enumerate(groups):
             start = jnp.where(back, tiles - p - size, p)
             copies.append(pltpu.make_async_copy(source.at[rows_of(start, size)], landed.at[rows_of(p - begin, size)], arrived.at[g]))
-        if tail:
+        if with_environment:
             for p in range(tiles):
                 at = jnp.where(back, tiles - 1 - p, p)
                 whole.append(pltpu.make_async_copy(environment.at[rows_of(at)], refs[0].at[rows_of(WIDE + p)], placed.at[p]))
@@ -156,7 +156,7 @@
             copy.wait()
 
     outs = [tile_rows(cuts[k + 1] - cuts[k], pairs * TILE) for k in chosen]
-    if tail:
+    if with_environment:
         outs.append(tile_rows(tiles + 2 * WIDE, bond))
     return pl.pallas_call(
         kernel,
@@ -175,7 +175,7 @@
 
 
 def pair_step(step, k, tiles, pairs, cuts, inner, outer, tables, own, odd, edges, arrived, keeps, give=(), doing=(FILL, EDGE, MAIN), work=0):
-    count = len(own)
+    count = len(cuts) - 1
     head, tail = k == 0, k == count - 1
     edges = (edges[:1] * head + edges[1:] * tail) * (EDGE in doing or step == 0 and FILL in doing)
     arrived = arrived * (FILL in doing)
@@ -189,7 +189,8 @@
     fixed = [*(own[i] for i in own_parts), *(odd[i] for i in odd_parts), *edges]
     first = 2 + len(fixed) + len(arrived)
 
-    def kernel(table, odd_table, *refs):
+    def kernel(own_list, odd_list, *refs):
+        *refs, table, odd_table, listed = refs
         own_refs = dict(zip(own_parts, refs))
         odd_refs = dict(zip(odd_parts, refs[len(own_parts) :]))
         edge_refs = refs[len(own_parts) + len(odd_parts) : len(fixed)]
@@ -200,6 +201,11 @@
 
         @pl.when(kind == 2 * step)
         def _():
+            lists = []
+            if MAIN in doing:
+                lists = [pltpu.make_async_copy(own_list, table, listed.at[0]), pltpu.make_async_copy(odd_list, odd_table, listed.at[1])]
+            for copy in lists:
+                copy.start()
             if step > 0 and FILL in doing:
                 wide[rows_of(WIDE + begin, end - begin), :] = came[0][...]
             for m in range(WIDE * (FILL in doing)):
@@ -215,6 +221,8 @@
                 if tail:
                     at = tiles + REACH - 1 - e
                     kept[rows_of(REACH + at), :] = product(edge_refs[-1][rows_of(e), :], wide[rows_of(WIDE + at - REACH, BAND), :])
+            for copy in lists:
+                copy.wait()
             for p in range(begin_odd, end_odd if MAIN in doing else begin_odd):
                 kept[rows_of(REACH + p), :] = product(blocks_at(odd_refs, cuts, p), stacked(wide, odd_place, p, WIDE, pairs))
             for p in range(*(out or (0, 0))):
@@ -238,10 +246,11 @@
     outs += [tile_rows(high - low, bond) for low, high in give]
     return pl.pallas_call(
         kernel,
-        in_specs=[SMEM] * 2 + [VMEM] * (first - 2 + len(keeps)),
+        in_specs=[ANY] * 2 + [VMEM] * (first - 2 + len(keeps)),
         out_specs=[VMEM] * len(outs),
         out_shape=outs,
         input_output_aliases={first + i: 2 - len(keeps) + i for i in range(len(keeps))},
+        scratch_shapes=[pltpu.SMEM(tables[0].shape, jnp.int32)] * 2 + [pltpu.SemaphoreType.DMA((2,))],
         compiler_params=params(),
         cost_estimate=cost(work or STEP * (end - begin) / tiles),
         name="pair_step",
@@ -251,16 +260,18 @@
 def finish(begin, end, odd_column, tiles, pairs, cuts, table, own, given, regions, left, state, done, extra=()):
     bond = state.shape[1]
     parts = [k for k in range(len(own)) if cuts[k] < end and cuts[k + 1] > begin]
-    groups = [(p, min(GROUP, end - p)) for p in range(begin, end, GROUP)]
+    limit = max(begin, end - GROUP)
+    groups = [(p, min(GROUP, limit - p)) for p in range(begin, limit, GROUP)] + [(p, 1) for p in range(limit, end)]
     refs_in = [*(own[k] for k in parts), *given, *extra, left, state, *done]
     count, fixed = len(parts), len(parts) + len(given) + len(extra) + 2
 
-    def kernel(table, *refs):
+    def kernel(own_list, *refs):
         own_refs = dict(zip(parts, refs))
         *taken, rows = refs[count : fixed - 1]
-        kept, env, grad, staged_env, staged, sent = refs[len(refs_in) :]
+        kept, env, grad, staged_env, staged, sent, table, listed = refs[len(refs_in) :]
 
         core = kind_here() % 2
+        lists = pltpu.make_async_copy(own_list, table, listed)
 
         @pl.when(core == 1)
         def _():
@@ -269,6 +280,8 @@
 
         @pl.when(core >= 0 if odd_column is None else core == odd_column)
         def _():
+            lists.start()
+            lists.wait()
             place = places(table, tiles)
             back = reversed_here()
             copies = []
@@ -296,7 +309,7 @@
     size = (end - begin) * TILE
     return pl.pallas_call(
         kernel,
-        in_specs=[SMEM] + [VMEM] * fixed + [HBM] * len(done),
+        in_specs=[ANY] + [VMEM] * fixed + [HBM] * len(done),
         out_specs=[VMEM, HBM, HBM],
         out_shape=[tile_rows(tiles + 2 * REACH, bond), env, grad],
         input_output_aliases={fixed + i: i for i in range(1 + len(done))},
@@ -304,6 +317,8 @@
             pltpu.VMEM((size, bond), jnp.bfloat16),
             pltpu.VMEM((size, pairs, TILE), jnp.bfloat16),
             pltpu.SemaphoreType.DMA((2, len(groups))),
+            pltpu.SMEM(table.shape, jnp.int32),
+            pltpu.SemaphoreType.DMA,
         ],
         compiler_params=params(),
         cost_estimate=cost(FINISH if odd_column == 0 else FINISH * (end - begin) / tiles),
@@ -341,13 +356,14 @@
     cuts = [0] + [e + WIDE - REACH for e in ends] + [tiles]
     first_edge, last_edge = prepare_edges(pairs, tiles, table, blocks, right)
     first_edge, last_edge, blocks = lax.optimization_barrier((first_edge, last_edge, blocks))
-    (head,) = prepare(0, 1, cuts, pairs, blocks, right)
-    *rest, wide = prepare(1, count, cuts, pairs, blocks, right)
-    own = [head, *rest]
+    head, wide = prepare(0, 1, cuts, pairs, blocks, right)
+    middle = prepare(1, count - 1, cuts, pairs, blocks, right) if count > 2 else []
+    own = [head, *middle]
     odd_cols = [(2 * z + 1, 2 * z) for z in range(layers)]
     odd = [move(part, swap) for part in own]
     listed, _ = lax.optimization_barrier((table, head))
     odd_table = move(listed, swap)
+    last_edge, _ = lax.optimization_barrier((last_edge, own[-1]))
     odd_edges = [move(first_edge, [(a, b, partner) for a, b in odd_cols]), move(last_edge, [(a, b, other) for a, b in odd_cols])]
 
     keeps = [wide]
@@ -378,6 +394,8 @@
             if step == 0 and k == 0:
                 keeps = pair_step(step, k, tiles, pairs, cuts, inner, None, *arguments, keeps, (), (FILL, EDGE), FIRST)
                 result = pair_step(step, k, tiles, pairs, cuts, inner, outer, *arguments, keeps, (), (MAIN,))
+                own += prepare(count - 1, count, cuts, pairs, lax.optimization_barrier((blocks, result[2]))[0], right)
+                odd.append(move(own[-1], swap))
             elif end and k == count - 1:
                 *keeps, gift = pair_step(step, k, tiles, pairs, cuts, inner, None, *arguments, keeps, give, (FILL,), COLLECT)
                 result = pair_step(step, k, tiles, pairs, cuts, inner, None, *arguments, keeps, (), (EDGE, MAIN))

time: 66.8 us -> 65.7 us (0.984); the launches traced: 66.3 us -> 64.4 us
  Pallas kernels: 22.3 us -> 15.1 us
  starting transfers between devices: 39.5 us -> 43.5 us
  waiting for transfers between devices: 3.34 us -> 4.59 us
    pallas_call x17, Pallas kernels: 15 us -> 6.44 us  [the longest x3 5.68 us: finish(): pl.pallas_call(kernel, in_specs=[ANY] + [VMEM] * fixed + [HBM] * len(done...]
    ppermute x24, starting transfers between devices: 39.5 us -> 43.5 us  [move(): return lax.ppermute(value, ('col', 'sec'), both)]
    pallas_call x2 -> x3, Pallas kernels: 5.91 us -> 7.28 us  [prepare(): pl.pallas_call(kernel, in_specs=[HBM, HBM], out_specs=[VMEM] * len(outs),...]
    ppermute x24, waiting for transfers between devices: 3.34 us -> 4.59 us  [move(): return lax.ppermute(value, ('col', 'sec'), both)]
  transfers between devices with their start and end apart: 24 -> 24, of which waited for: 4 -> 4; matrix products, arithmetic and copies ran while one was open for 0% -> 0% of each run, Pallas kernels for 26% -> 16%
where the time goes in v6:
time: 65.7 us; the launch traced here: 64.4 us
  starting transfers between devices  43.5 us (66%)
  Pallas kernels  15.1 us (23%)
  waiting for transfers between devices  4.59 us (7%)
  between operations  1.25 us (2%)
    ppermute x24, starting transfers between devices, move(): return lax.ppermute(value, ('col', 'sec'), both)  43.5 us
    pallas_call x3, Pallas kernels, prepare(): pl.pallas_call(kernel, in_specs=[HBM, HBM], out_specs=[VMEM] * len(outs),...  7.28 us
    pallas_call x3, Pallas kernels, finish(): pl.pallas_call(kernel, in_specs=[ANY] + [VMEM] * fixed + [HBM] * len(done...  5.68 us
    ppermute x24, waiting for transfers between devices, move(): return lax.ppermute(value, ('col', 'sec'), both)  4.59 us
    pallas_call x1, Pallas kernels, prepare_edges(): pl.pallas_call(kernel, in_specs=[HBM, HBM, HBM], out_specs=[VMEM, VMEM],...  1.36 us
  transfers between devices with their start and end apart: 24, of which 4 were waited for; matrix products, arithmetic and copies ran while one was open for 0% of the time, Pallas kernels for 16%

profile of v6, /device:TPU:3, one launch (start us, length us, event | category | flops | bytes accessed | tf_op | source)
XLA Modules:
  0.0 64.4 jit_solution(13231180463877210613)
XLA Ops:
  0.6 1.4 %prepare_edges.1 = (bf16[384,640]{1,0:T(8,128)(2,1)S(1)}, bf16[384,640]{1,0:T(8,128)(2,1)S(1)}) custom-call(s32[4,32]{1,0:T(4,128)} %bitcast.11, bf16[4096,4,128]{2,1,0:T(4,128)(2,1)} %bitcast.30, bf16[4096,128]{1,0:T(8,128)(2,1)} %bitcast.35), custom_call_target="tpu_custom_call" | custom-call | flops 125000000 | tf_op jit(solution)/shard_map/prepare_edges/pallas_call | solution.py:108
  2.0 0.0 copy-start.1
  2.0 1.3 %collective-permute-start.2 = (bf16[384,640]{1,0:T(8,128)(2,1)S(1)}, bf16[384,640]{1,0:T(8,128)(2,1)S(1)}, u32[]{:S(2)}, u32[]{:S(2)}) collective-permute-start(bf16[384,640]{1,0:T(8,128)(2,1)S(1)} %get-tuple-element.70), channel_id=1, source_target_pairs={{4,1},{5,0},{6,3},{7,2},{12,9},{13,8},{14,11},{15,10},{20,17},{21,... | collective-permute-start | bytes 1474568 | tf_op jit(solution)/shard_map/ppermute | solution.py:345
  3.3 3.0 %prepare.3 = (bf16[1792,512]{1,0:T(8,128)(2,1)S(1)}, bf16[5120,128]{1,0:T(8,128)(2,1)S(1)}) custom-call(bf16[4096,4,128]{2,1,0:T(4,128)(2,1)} %bitcast.31, bf16[4096,128]{1,0:T(8,128)(2,1)} %bitcast.36), custom_call_target="tpu_custom_call" | custom-call | flops 437500000 | tf_op jit(solution)/shard_map/prepare/pallas_call | solution.py:161
  6.4 0.7 %collective-permute-start.1 = (bf16[1792,512]{1,0:T(8,128)(2,1)S(1)}, bf16[1792,512]{1,0:T(8,128)(2,1)S(1)}, u32[]{:S(2)}, u32[]{:S(2)}) collective-permute-start(bf16[1792,512]{1,0:T(8,128)(2,1)S(1)} %get-tuple-element.68.refs_0_), channel_id=1, source_target_pairs={{0,4},{1,5},{2,6},{3,7},{4,0},{5,1},{6,2},{7,3},{8,12},{9,13},{10,... | collective-permute-start | bytes 5505032 | tf_op jit(solution)/shard_map/ppermute | solution.py:345
  7.1 0.1 collective-permute-start
  7.2 2.4 %prepare.4.refs_1_.refs_0_ = bf16[1536,512]{1,0:T(8,128)(2,1)S(1)} custom-call(bf16[4096,4,128]{2,1,0:T(4,128)(2,1)} %bitcast.32, bf16[4096,128]{1,0:T(8,128)(2,1)} %bitcast.37), custom_call_target="tpu_custom_call" | custom-call | flops 375000000 | tf_op jit(solution)/shard_map/prepare/pallas_call | solution.py:161
  9.6 0.5 collective-permute-start.3
  10.1 5.3 %collective-permute-start.5 = (bf16[384,640]{1,0:T(8,128)(2,1)S(1)}, bf16[384,640]{1,0:T(8,128)(2,1)S(1)}, u32[]{:S(2)}, u32[]{:S(2)}) collective-permute-start(bf16[384,640]{1,0:T(8,128)(2,1)S(1)} %get-tuple-element.77), channel_id=1, source_target_pairs={{5,2},{6,1},{13,10},{14,9},{21,18},{22,17},{29,26},{30,25}} | collective-permute-start | bytes 1474568 | tf_op jit(solution)/shard_map/ppermute | solution.py:345
  15.4 0.0 collective-permute-done.1.refs_1_.refs_2_.refs_0_
  15.5 0.7 %collective-permute-start.9 = (bf16[1536,128]{1,0:T(8,128)(2,1)S(1)}, bf16[1536,128]{1,0:T(8,128)(2,1)S(1)}, u32[]{:S(2)}, u32[]{:S(2)}) collective-permute-start(bf16[1536,128]{1,0:T(8,128)(2,1)S(1)} %get-tuple-element.74), channel_id=1, source_target_pairs={{24,16},{25,17},{26,18},{27,19}} | collective-permute-start | bytes 1179656 | tf_op jit(solution)/shard_map/ppermute | solution.py:345
  16.2 0.7 %collective-permute-start.10 = (bf16[512,128]{1,0:T(8,128)(2,1)S(1)}, bf16[512,128]{1,0:T(8,128)(2,1)S(1)}, u32[]{:S(2)}, u32[]{:S(2)}) collective-permute-start(bf16[512,128]{1,0:T(8,128)(2,1)S(1)} %get-tuple-element.85), channel_id=1, source_target_pairs={{24,17},{25,16},{26,19},{27,18}} | collective-permute-start | bytes 393224 | tf_op jit(solution)/shard_map/ppermute | solution.py:345
  16.8 1.9 %prepare.5.refs_1_.refs_2_ = bf16[768,512]{1,0:T(8,128)(2,1)S(1)} custom-call(bf16[4096,4,128]{2,1,0:T(4,128)(2,1)} %bitcast.33, bf16[4096,128]{1,0:T(8,128)(2,1)} %bitcast.38), custom_call_target="tpu_custom_call" | custom-call | flops 187500000 | tf_op jit(solution)/shard_map/prepare/pallas_call | solution.py:161
  18.7 0.1 collective-permute-start.4
  18.8 0.0 collective-permute-done.3.refs_2_.refs_3_.refs_0_
  18.9 0.7 %collective-permute-start.8 = (bf16[1536,128]{1,0:T(8,128)(2,1)S(1)}, bf16[1536,128]{1,0:T(8,128)(2,1)S(1)}, u32[]{:S(2)}, u32[]{:S(2)}) collective-permute-start(bf16[1536,128]{1,0:T(8,128)(2,1)S(1)} %get-tuple-element.84), channel_id=1, source_target_pairs={{24,16},{25,17},{26,18},{27,19}} | collective-permute-start | bytes 1179656 | tf_op jit(solution)/shard_map/ppermute | solution.py:345
  19.5 1.5 %collective-permute-done.5.refs_3_.refs_4_.refs_2_ = bf16[384,640]{1,0:T(8,128)(2,1)S(1)} collective-permute-done((bf16[384,640]{1,0:T(8,128)(2,1)S(1)}, bf16[384,640]{1,0:T(8,128)(2,1)S(1)}, u32[]{:S(2)}, u32[]{:S(2)}) %collective-permute-start.5) | collective-permute-done | bytes 491552 | tf_op jit(solution)/shard_map/ppermute | solution.py:345
  21.1 0.0 collective-permute-done.4.refs_2_.refs_3_.refs_1_
  21.1 0.7 %collective-permute-start.7 = (bf16[512,128]{1,0:T(8,128)(2,1)S(1)}, bf16[512,128]{1,0:T(8,128)(2,1)S(1)}, u32[]{:S(2)}, u32[]{:S(2)}) collective-permute-start(bf16[512,128]{1,0:T(8,128)(2,1)S(1)} %get-tuple-element.83), channel_id=1, source_target_pairs={{25,18},{26,17}} | collective-permute-start | bytes 393224 | tf_op jit(solution)/shard_map/ppermute | solution.py:345
  21.8 0.7 %collective-permute-start.6 = (bf16[1024,128]{1,0:T(8,128)(2,1)S(1)}, bf16[1024,128]{1,0:T(8,128)(2,1)S(1)}, u32[]{:S(2)}, u32[]{:S(2)}) collective-permute-start(bf16[1024,128]{1,0:T(8,128)(2,1)S(1)} %get-tuple-element.82), channel_id=1, source_target_pairs={{24,16},{25,17},{26,18},{27,19}} | collective-permute-start | bytes 786440 | tf_op jit(solution)/shard_map/ppermute | solution.py:345
  22.5 0.0 collective-permute-done.9.refs_3_
  22.5 0.7 %collective-permute-start.15 = (bf16[512,128]{1,0:T(8,128)(2,1)S(1)}, bf16[512,128]{1,0:T(8,128)(2,1)S(1)}, u32[]{:S(2)}, u32[]{:S(2)}) collective-permute-start(bf16[512,128]{1,0:T(8,128)(2,1)S(1)} %get-tuple-element.96), channel_id=1, source_target_pairs={{16,9},{17,8},{18,11},{19,10}} | collective-permute-start | bytes 393224 | tf_op jit(solution)/shard_map/ppermute | solution.py:345
  23.2 0.7 %collective-permute-start.14 = (bf16[1024,128]{1,0:T(8,128)(2,1)S(1)}, bf16[1024,128]{1,0:T(8,128)(2,1)S(1)}, u32[]{:S(2)}, u32[]{:S(2)}) collective-permute-start(bf16[1024,128]{1,0:T(8,128)(2,1)S(1)} %get-tuple-element.95), channel_id=1, source_target_pairs={{16,8},{17,9},{18,10},{19,11}} | collective-permute-start | bytes 786440 | tf_op jit(solution)/shard_map/ppermute | solution.py:345
  23.9 0.0 collective-permute-done.8.refs_4_
  24.0 0.7 %collective-permute-start.13 = (bf16[1536,128]{1,0:T(8,128)(2,1)S(1)}, bf16[1536,128]{1,0:T(8,128)(2,1)S(1)}, u32[]{:S(2)}, u32[]{:S(2)}) collective-permute-start(bf16[1536,128]{1,0:T(8,128)(2,1)S(1)} %get-tuple-element.94), channel_id=1, source_target_pairs={{16,8},{17,9},{18,10},{19,11}} | collective-permute-start | bytes 1179656 | tf_op jit(solution)/shard_map/ppermute | solution.py:345
  24.6 0.0 collective-permute-done.7.refs_6_
  24.7 0.0 collective-permute-done.6.refs_5_
  24.7 0.2 pair_step.20
  24.9 0.7 %collective-permute-start.12 = (bf16[512,128]{1,0:T(8,128)(2,1)S(1)}, bf16[512,128]{1,0:T(8,128)(2,1)S(1)}, u32[]{:S(2)}, u32[]{:S(2)}) collective-permute-start(bf16[512,128]{1,0:T(8,128)(2,1)S(1)} %get-tuple-element.93), channel_id=1, source_target_pairs={{17,10},{18,9}} | collective-permute-start | bytes 393224 | tf_op jit(solution)/shard_map/ppermute | solution.py:345
  25.6 0.7 %collective-permute-start.11 = (bf16[1536,128]{1,0:T(8,128)(2,1)S(1)}, bf16[1536,128]{1,0:T(8,128)(2,1)S(1)}, u32[]{:S(2)}, u32[]{:S(2)}) collective-permute-start(bf16[1536,128]{1,0:T(8,128)(2,1)S(1)} %get-tuple-element.92), channel_id=1, source_target_pairs={{16,8},{17,9},{18,10},{19,11}} | collective-permute-start | bytes 1179656 | tf_op jit(solution)/shard_map/ppermute | solution.py:345
  26.3 0.0 collective-permute-done.15.refs_4_
  26.3 0.7 %collective-permute-start.19 = (bf16[512,128]{1,0:T(8,128)(2,1)S(1)}, bf16[512,128]{1,0:T(8,128)(2,1)S(1)}, u32[]{:S(2)}, u32[]{:S(2)}) collective-permute-start(bf16[512,128]{1,0:T(8,128)(2,1)S(1)} %get-tuple-element.106), channel_id=1, source_target_pairs={{8,0},{9,1},{10,2},{11,3}} | collective-permute-start | bytes 393224 | tf_op jit(solution)/shard_map/ppermute | solution.py:345
  27.0 0.7 %collective-permute-start.20 = (bf16[512,128]{1,0:T(8,128)(2,1)S(1)}, bf16[512,128]{1,0:T(8,128)(2,1)S(1)}, u32[]{:S(2)}, u32[]{:S(2)}) collective-permute-start(bf16[512,128]{1,0:T(8,128)(2,1)S(1)} %get-tuple-element.107), channel_id=1, source_target_pairs={{8,1},{9,0},{10,3},{11,2}} | collective-permute-start | bytes 393224 | tf_op jit(solution)/shard_map/ppermute | solution.py:345
  27.8 0.7 %collective-permute-start.18 = (bf16[1536,128]{1,0:T(8,128)(2,1)S(1)}, bf16[1536,128]{1,0:T(8,128)(2,1)S(1)}, u32[]{:S(2)}, u32[]{:S(2)}) collective-permute-start(bf16[1536,128]{1,0:T(8,128)(2,1)S(1)} %get-tuple-element.105), channel_id=1, source_target_pairs={{8,0},{9,1},{10,2},{11,3}} | collective-permute-start | bytes 1179656 | tf_op jit(solution)/shard_map/ppermute | solution.py:345
  28.5 0.7 %collective-permute-start.17 = (bf16[512,128]{1,0:T(8,128)(2,1)S(1)}, bf16[512,128]{1,0:T(8,128)(2,1)S(1)}, u32[]{:S(2)}, u32[]{:S(2)}) collective-permute-start(bf16[512,128]{1,0:T(8,128)(2,1)S(1)} %get-tuple-element.104), channel_id=1, source_target_pairs={{9,2},{10,1}} | collective-permute-start | bytes 393224 | tf_op jit(solution)/shard_map/ppermute | solution.py:345
  29.2 0.7 %collective-permute-start.16 = (bf16[2048,128]{1,0:T(8,128)(2,1)S(1)}, bf16[2048,128]{1,0:T(8,128)(2,1)S(1)}, u32[]{:S(2)}, u32[]{:S(2)}) collective-permute-start(bf16[2048,128]{1,0:T(8,128)(2,1)S(1)} %get-tuple-element.103), channel_id=1, source_target_pairs={{8,0},{9,1},{10,2},{11,3}} | collective-permute-start | bytes 1572872 | tf_op jit(solution)/shard_map/ppermute | solution.py:345
  30.0 0.0 copy-start
  30.0 0.1 pair_step.25
  30.1 21.9 %collective-permute-start.22 = (bf16[1024,128]{1,0:T(8,128)(2,1)S(1)}, bf16[1024,128]{1,0:T(8,128)(2,1)S(1)}, u32[]{:S(2)}, u32[]{:S(2)}) collective-permute-start(bf16[1024,128]{1,0:T(8,128)(2,1)S(1)} %get-tuple-element.113), channel_id=1, source_target_pairs={{0,4},{1,5},{2,6},{3,7},{4,0},{5,1},{6,2},{7,3},{8,12},{9,13},{10,... | collective-permute-start | bytes 786440 | tf_op jit(solution)/shard_map/ppermute | solution.py:345
  52.0 0.1 collective-permute-start.21
  52.1 0.1 finish.3
  52.2 1.0 %collective-permute-done.22.refs_2_ = bf16[1024,128]{1,0:T(8,128)(2,1)S(1)} collective-permute-done((bf16[1024,128]{1,0:T(8,128)(2,1)S(1)}, bf16[1024,128]{1,0:T(8,128)(2,1)S(1)}, u32[]{:S(2)}, u32[]{:S(2)}) %collective-permute-start.22) | collective-permute-done | bytes 262176 | tf_op jit(solution)/shard_map/ppermute | solution.py:345
  53.2 0.5 collective-permute-done.21.refs_1_
  53.6 2.5 %finish.4 = (bf16[4608,128]{1,0:T(8,128)(2,1)S(1)}, bf16[4096,128]{1,0:T(8,128)(2,1)}, bf16[4096,4,128]{2,1,0:T(4,128)(2,1)}) custom-call(s32[4,32]{1,0:T(4,128)S(1)} %bitcast.26, bf16[1792,512]{1,0:T(8,128)(2,1)S(1)} %get-tuple-element.68.refs_0_, ...), custom_call_target="tpu_custom_call", output_to_operand_aliasing={{0}: (5, {}), {1}: (6, {}), {2}: (7, {})} | custom-call | flops 1500000000 | tf_op jit(solution)/shard_map/finish/pallas_call | solution.py:310
  56.1 0.1 pair_step.26
  56.2 3.3 %collective-permute-start.23 = (bf16[2304,128]{1,0:T(8,128)(2,1)S(1)}, bf16[2304,128]{1,0:T(8,128)(2,1)S(1)}, u32[]{:S(2)}, u32[]{:S(2)}) collective-permute-start(bf16[2304,128]{1,0:T(8,128)(2,1)S(1)} %get-tuple-element.120), channel_id=1, source_target_pairs={{0,4},{1,5},{2,6},{3,7},{4,0},{5,1},{6,2},{7,3},{8,12},{9,13},{10,... | collective-permute-start | bytes 1769480 | tf_op jit(solution)/shard_map/ppermute | solution.py:345
  59.5 1.6 %collective-permute-done.23.refs_3_ = bf16[2304,128]{1,0:T(8,128)(2,1)S(1)} collective-permute-done((bf16[2304,128]{1,0:T(8,128)(2,1)S(1)}, bf16[2304,128]{1,0:T(8,128)(2,1)S(1)}, u32[]{:S(2)}, u32[]{:S(2)}) %collective-permute-start.23) | collective-permute-done | bytes 589856 | tf_op jit(solution)/shard_map/ppermute | solution.py:345
  61.1 3.1 %finish.5 = (bf16[4608,128]{1,0:T(8,128)(2,1)S(1)}, bf16[4096,128]{1,0:T(8,128)(2,1)}, bf16[4096,4,128]{2,1,0:T(4,128)(2,1)}) custom-call(s32[4,32]{1,0:T(4,128)S(1)} %bitcast.29, bf16[1792,512]{1,0:T(8,128)(2,1)S(1)} %get-tuple-element.68.refs_0_, ...), custom_call_target="tpu_custom_call", output_to_operand_aliasing={{0}: (6, {}), {1}: (7, {}), {2}: (8, {})} | custom-call | flops 2500000000 | tf_op jit(solution)/shard_map/finish/pallas_call | solution.py:310
  (25 shorter events, 0.5 us)
Async XLA Ops:
  2.0 5.1 %copy-start.1 = (s32[1,1,32,4]{2,3,1,0:T(4,128)S(1)}, s32[1,1,32,4]{2,3,1,0:T(4,128)}, u32[]{:S(2)}) copy-start(s32[1,1,32,4]{2,3,1,0:T(4,128)} %param.6) | copy-start | bytes 1540
  2.0 13.3 %collective-permute-start.2 = (bf16[384,640]{1,0:T(8,128)(2,1)S(1)}, bf16[384,640]{1,0:T(8,128)(2,1)S(1)}, u32[]{:S(2)}, u32[]{:S(2)}) collective-permute-start(bf16[384,640]{1,0:T(8,128)(2,1)S(1)} %get-tuple-element.70), channel_id=1, source_target_pairs={{4,1},{5,0},{6,3},{7,2},{12,9},{13,8},{14,11},{15,10},{20,17},{21,... | collective-permute-start | bytes 1474568 | tf_op jit(solution)/shard_map/ppermute | solution.py:345
  6.4 9.0 %collective-permute-start.1 = (bf16[1792,512]{1,0:T(8,128)(2,1)S(1)}, bf16[1792,512]{1,0:T(8,128)(2,1)S(1)}, u32[]{:S(2)}, u32[]{:S(2)}) collective-permute-start(bf16[1792,512]{1,0:T(8,128)(2,1)S(1)} %get-tuple-element.68.refs_0_), channel_id=1, source_target_pairs={{0,4},{1,5},{2,6},{3,7},{4,0},{5,1},{6,2},{7,3},{8,12},{9,13},{10,... | collective-permute-start | bytes 5505032 | tf_op jit(solution)/shard_map/ppermute | solution.py:345
  7.1 8.2 %collective-permute-start = (s32[4,32]{1,0:T(4,128)S(1)}, s32[4,32]{1,0:T(4,128)S(1)}, u32[]{:S(2)}, u32[]{:S(2)}) collective-permute-start(s32[4,32]{1,0:T(4,128)S(1)} %bitcast.12), channel_id=1, source_target_pairs={{0,4},{1,5},{2,6},{3,7},{4,0},{5,1},{6,2},{7,3},{8,12},{9,13},{10,... | collective-permute-start | bytes 1544 | tf_op jit(solution)/shard_map/ppermute | solution.py:345
  9.6 9.2 %collective-permute-start.3 = (bf16[1536,512]{1,0:T(8,128)(2,1)S(1)}, bf16[1536,512]{1,0:T(8,128)(2,1)S(1)}, u32[]{:S(2)}, u32[]{:S(2)}) collective-permute-start(bf16[1536,512]{1,0:T(8,128)(2,1)S(1)} %prepare.4.refs_1_.refs_0_), channel_id=1, source_target_pairs={{0,4},{1,5},{2,6},{3,7},{4,0},{5,1},{6,2},{7,3},{8,12},{9,13},{10,... | collective-permute-start | bytes 4718600 | tf_op jit(solution)/shard_map/ppermute | solution.py:345
  10.1 11.0 %collective-permute-start.5 = (bf16[384,640]{1,0:T(8,128)(2,1)S(1)}, bf16[384,640]{1,0:T(8,128)(2,1)S(1)}, u32[]{:S(2)}, u32[]{:S(2)}) collective-permute-start(bf16[384,640]{1,0:T(8,128)(2,1)S(1)} %get-tuple-element.77), channel_id=1, source_target_pairs={{5,2},{6,1},{13,10},{14,9},{21,18},{22,17},{29,26},{30,25}} | collective-permute-start | bytes 1474568 | tf_op jit(solution)/shard_map/ppermute | solution.py:345
  15.5 7.0 %collective-permute-start.9 = (bf16[1536,128]{1,0:T(8,128)(2,1)S(1)}, bf16[1536,128]{1,0:T(8,128)(2,1)S(1)}, u32[]{:S(2)}, u32[]{:S(2)}) collective-permute-start(bf16[1536,128]{1,0:T(8,128)(2,1)S(1)} %get-tuple-element.74), channel_id=1, source_target_pairs={{24,16},{25,17},{26,18},{27,19}} | collective-permute-start | bytes 1179656 | tf_op jit(solution)/shard_map/ppermute | solution.py:345
  16.2 6.3 %collective-permute-start.10 = (bf16[512,128]{1,0:T(8,128)(2,1)S(1)}, bf16[512,128]{1,0:T(8,128)(2,1)S(1)}, u32[]{:S(2)}, u32[]{:S(2)}) collective-permute-start(bf16[512,128]{1,0:T(8,128)(2,1)S(1)} %get-tuple-element.85), channel_id=1, source_target_pairs={{24,17},{25,16},{26,19},{27,18}} | collective-permute-start | bytes 393224 | tf_op jit(solution)/shard_map/ppermute | solution.py:345
  18.7 2.4 %collective-permute-start.4 = (bf16[768,512]{1,0:T(8,128)(2,1)S(1)}, bf16[768,512]{1,0:T(8,128)(2,1)S(1)}, u32[]{:S(2)}, u32[]{:S(2)}) collective-permute-start(bf16[768,512]{1,0:T(8,128)(2,1)S(1)} %prepare.5.refs_1_.refs_2_), channel_id=1, source_target_pairs={{0,4},{1,5},{2,6},{3,7},{4,0},{5,1},{6,2},{7,3},{8,12},{9,13},{10,... | collective-permute-start | bytes 2359304 | tf_op jit(solution)/shard_map/ppermute | solution.py:345
  18.9 5.0 %collective-permute-start.8 = (bf16[1536,128]{1,0:T(8,128)(2,1)S(1)}, bf16[1536,128]{1,0:T(8,128)(2,1)S(1)}, u32[]{:S(2)}, u32[]{:S(2)}) collective-permute-start(bf16[1536,128]{1,0:T(8,128)(2,1)S(1)} %get-tuple-element.84), channel_id=1, source_target_pairs={{24,16},{25,17},{26,18},{27,19}} | collective-permute-start | bytes 1179656 | tf_op jit(solution)/shard_map/ppermute | solution.py:345
  21.1 3.6 %collective-permute-start.7 = (bf16[512,128]{1,0:T(8,128)(2,1)S(1)}, bf16[512,128]{1,0:T(8,128)(2,1)S(1)}, u32[]{:S(2)}, u32[]{:S(2)}) collective-permute-start(bf16[512,128]{1,0:T(8,128)(2,1)S(1)} %get-tuple-element.83), channel_id=1, source_target_pairs={{25,18},{26,17}} | collective-permute-start | bytes 393224 | tf_op jit(solution)/shard_map/ppermute | solution.py:345
  21.8 2.9 %collective-permute-start.6 = (bf16[1024,128]{1,0:T(8,128)(2,1)S(1)}, bf16[1024,128]{1,0:T(8,128)(2,1)S(1)}, u32[]{:S(2)}, u32[]{:S(2)}) collective-permute-start(bf16[1024,128]{1,0:T(8,128)(2,1)S(1)} %get-tuple-element.82), channel_id=1, source_target_pairs={{24,16},{25,17},{26,18},{27,19}} | collective-permute-start | bytes 786440 | tf_op jit(solution)/shard_map/ppermute | solution.py:345
  22.5 3.7 %collective-permute-start.15 = (bf16[512,128]{1,0:T(8,128)(2,1)S(1)}, bf16[512,128]{1,0:T(8,128)(2,1)S(1)}, u32[]{:S(2)}, u32[]{:S(2)}) collective-permute-start(bf16[512,128]{1,0:T(8,128)(2,1)S(1)} %get-tuple-element.96), channel_id=1, source_target_pairs={{16,9},{17,8},{18,11},{19,10}} | collective-permute-start | bytes 393224 | tf_op jit(solution)/shard_map/ppermute | solution.py:345
  23.2 3.1 %collective-permute-start.14 = (bf16[1024,128]{1,0:T(8,128)(2,1)S(1)}, bf16[1024,128]{1,0:T(8,128)(2,1)S(1)}, u32[]{:S(2)}, u32[]{:S(2)}) collective-permute-start(bf16[1024,128]{1,0:T(8,128)(2,1)S(1)} %get-tuple-element.95), channel_id=1, source_target_pairs={{16,8},{17,9},{18,10},{19,11}} | collective-permute-start | bytes 786440 | tf_op jit(solution)/shard_map/ppermute | solution.py:345
  24.0 3.7 %collective-permute-start.13 = (bf16[1536,128]{1,0:T(8,128)(2,1)S(1)}, bf16[1536,128]{1,0:T(8,128)(2,1)S(1)}, u32[]{:S(2)}, u32[]{:S(2)}) collective-permute-start(bf16[1536,128]{1,0:T(8,128)(2,1)S(1)} %get-tuple-element.94), channel_id=1, source_target_pairs={{16,8},{17,9},{18,10},{19,11}} | collective-permute-start | bytes 1179656 | tf_op jit(solution)/shard_map/ppermute | solution.py:345
  24.9 3.6 %collective-permute-start.12 = (bf16[512,128]{1,0:T(8,128)(2,1)S(1)}, bf16[512,128]{1,0:T(8,128)(2,1)S(1)}, u32[]{:S(2)}, u32[]{:S(2)}) collective-permute-start(bf16[512,128]{1,0:T(8,128)(2,1)S(1)} %get-tuple-element.93), channel_id=1, source_target_pairs={{17,10},{18,9}} | collective-permute-start | bytes 393224 | tf_op jit(solution)/shard_map/ppermute | solution.py:345
  25.6 2.9 %collective-permute-start.11 = (bf16[1536,128]{1,0:T(8,128)(2,1)S(1)}, bf16[1536,128]{1,0:T(8,128)(2,1)S(1)}, u32[]{:S(2)}, u32[]{:S(2)}) collective-permute-start(bf16[1536,128]{1,0:T(8,128)(2,1)S(1)} %get-tuple-element.92), channel_id=1, source_target_pairs={{16,8},{17,9},{18,10},{19,11}} | collective-permute-start | bytes 1179656 | tf_op jit(solution)/shard_map/ppermute | solution.py:345
  26.3 3.6 %collective-permute-start.19 = (bf16[512,128]{1,0:T(8,128)(2,1)S(1)}, bf16[512,128]{1,0:T(8,128)(2,1)S(1)}, u32[]{:S(2)}, u32[]{:S(2)}) collective-permute-start(bf16[512,128]{1,0:T(8,128)(2,1)S(1)} %get-tuple-element.106), channel_id=1, source_target_pairs={{8,0},{9,1},{10,2},{11,3}} | collective-permute-start | bytes 393224 | tf_op jit(solution)/shard_map/ppermute | solution.py:345
  27.0 2.9 %collective-permute-start.20 = (bf16[512,128]{1,0:T(8,128)(2,1)S(1)}, bf16[512,128]{1,0:T(8,128)(2,1)S(1)}, u32[]{:S(2)}, u32[]{:S(2)}) collective-permute-start(bf16[512,128]{1,0:T(8,128)(2,1)S(1)} %get-tuple-element.107), channel_id=1, source_target_pairs={{8,1},{9,0},{10,3},{11,2}} | collective-permute-start | bytes 393224 | tf_op jit(solution)/shard_map/ppermute | solution.py:345
  27.8 2.2 %collective-permute-start.18 = (bf16[1536,128]{1,0:T(8,128)(2,1)S(1)}, bf16[1536,128]{1,0:T(8,128)(2,1)S(1)}, u32[]{:S(2)}, u32[]{:S(2)}) collective-permute-start(bf16[1536,128]{1,0:T(8,128)(2,1)S(1)} %get-tuple-element.105), channel_id=1, source_target_pairs={{8,0},{9,1},{10,2},{11,3}} | collective-permute-start | bytes 1179656 | tf_op jit(solution)/shard_map/ppermute | solution.py:345
  28.5 23.5 %collective-permute-start.17 = (bf16[512,128]{1,0:T(8,128)(2,1)S(1)}, bf16[512,128]{1,0:T(8,128)(2,1)S(1)}, u32[]{:S(2)}, u32[]{:S(2)}) collective-permute-start(bf16[512,128]{1,0:T(8,128)(2,1)S(1)} %get-tuple-element.104), channel_id=1, source_target_pairs={{9,2},{10,1}} | collective-permute-start | bytes 393224 | tf_op jit(solution)/shard_map/ppermute | solution.py:345
  29.2 26.9 %collective-permute-start.16 = (bf16[2048,128]{1,0:T(8,128)(2,1)S(1)}, bf16[2048,128]{1,0:T(8,128)(2,1)S(1)}, u32[]{:S(2)}, u32[]{:S(2)}) collective-permute-start(bf16[2048,128]{1,0:T(8,128)(2,1)S(1)} %get-tuple-element.103), channel_id=1, source_target_pairs={{8,0},{9,1},{10,2},{11,3}} | collective-permute-start | bytes 1572872 | tf_op jit(solution)/shard_map/ppermute | solution.py:345
  30.0 22.1 %copy-start = (bf16[1,1,4096,128]{3,2,1,0:T(8,128)(2,1)S(1)}, bf16[1,1,4096,128]{3,2,1,0:T(8,128)(2,1)}, u32[]{:S(2)}) copy-start(bf16[1,1,4096,128]{3,2,1,0:T(8,128)(2,1)} %param.7) | copy-start | bytes 3145732
  30.1 23.1 %collective-permute-start.22 = (bf16[1024,128]{1,0:T(8,128)(2,1)S(1)}, bf16[1024,128]{1,0:T(8,128)(2,1)S(1)}, u32[]{:S(2)}, u32[]{:S(2)}) collective-permute-start(bf16[1024,128]{1,0:T(8,128)(2,1)S(1)} %get-tuple-element.113), channel_id=1, source_target_pairs={{0,4},{1,5},{2,6},{3,7},{4,0},{5,1},{6,2},{7,3},{8,12},{9,13},{10,... | collective-permute-start | bytes 786440 | tf_op jit(solution)/shard_map/ppermute | solution.py:345
  52.0 1.6 %collective-permute-start.21 = (bf16[1280,128]{1,0:T(8,128)(2,1)S(1)}, bf16[1280,128]{1,0:T(8,128)(2,1)S(1)}, u32[]{:S(2)}, u32[]{:S(2)}) collective-permute-start(bf16[1280,128]{1,0:T(8,128)(2,1)S(1)} %get-tuple-element.112), channel_id=1, source_target_pairs={{0,4},{1,5},{2,6},{3,7},{4,0},{5,1},{6,2},{7,3},{8,12},{9,13},{10,... | collective-permute-start | bytes 983048 | tf_op jit(solution)/shard_map/ppermute | solution.py:345
  56.2 5.0 %collective-permute-start.23 = (bf16[2304,128]{1,0:T(8,128)(2,1)S(1)}, bf16[2304,128]{1,0:T(8,128)(2,1)S(1)}, u32[]{:S(2)}, u32[]{:S(2)}) collective-permute-start(bf16[2304,128]{1,0:T(8,128)(2,1)S(1)} %get-tuple-element.120), channel_id=1, source_target_pairs={{0,4},{1,5},{2,6},{3,7},{4,0},{5,1},{6,2},{7,3},{8,12},{9,13},{10,... | collective-permute-start | bytes 1769480 | tf_op jit(solution)/shard_map/ppermute | solution.py:345

commit v7 on v6

--- a/solution.py
+++ b/solution.py
@@ -328,7 +328,7 @@
 
 def limits(tiles, crossings):
     room = WIDE * crossings
-    ends = [e for e in (3 * tiles // 8, 3 * tiles // 4) if room <= e <= tiles - WIDE]
+    ends = [e for e in (13 * tiles // 32, 25 * tiles // 32) if room <= e <= tiles - WIDE]
     return ends or [tiles - WIDE]
 
 

time: 65.7 us -> 64.9 us (0.988)
  starting transfers between devices: 43.5 us -> 42.7 us
    ppermute x24, starting transfers between devices: 43.5 us -> 42.7 us  [move(): return lax.ppermute(value, ('col', 'sec'), both)]
  transfers between devices with their start and end apart: 24 -> 24, of which waited for: 4 -> 4; matrix products, arithmetic and copies ran while one was open for 0% -> 0% of each run, Pallas kernels for 16% -> 17%
where the time goes in v7:
time: 64.9 us; the launch traced here: 63.7 us
  starting transfers between devices  42.7 us (66%)
  Pallas kernels  15.1 us (23%)
  waiting for transfers between devices  4.67 us (7%)
  between operations  1.25 us (2%)
    ppermute x24, starting transfers between devices, move(): return lax.ppermute(value, ('col', 'sec'), both)  42.7 us
    pallas_call x3, Pallas kernels, prepare(): pl.pallas_call(kernel, in_specs=[HBM, HBM], out_specs=[VMEM] * len(outs),...  7.28 us
    pallas_call x3, Pallas kernels, finish(): pl.pallas_call(kernel, in_specs=[ANY] + [VMEM] * fixed + [HBM] * len(done...  5.69 us
    ppermute x24, waiting for transfers between devices, move(): return lax.ppermute(value, ('col', 'sec'), both)  4.67 us
    pallas_call x1, Pallas kernels, prepare_edges(): pl.pallas_call(kernel, in_specs=[HBM, HBM, HBM], out_specs=[VMEM, VMEM],...  1.36 us
  transfers between devices with their start and end apart: 24, of which 4 were waited for; matrix products, arithmetic and copies ran while one was open for 0% of the time, Pallas kernels for 17%

profile of v7, /device:TPU:3, one launch (start us, length us, event | category | flops | bytes accessed | tf_op | source)
XLA Modules:
  0.0 63.7 jit_solution(13278840677358059125)
XLA Ops:
  0.6 1.4 %prepare_edges.1 = (bf16[384,640]{1,0:T(8,128)(2,1)S(1)}, bf16[384,640]{1,0:T(8,128)(2,1)S(1)}) custom-call(s32[4,32]{1,0:T(4,128)} %bitcast.11, bf16[4096,4,128]{2,1,0:T(4,128)(2,1)} %bitcast.30, bf16[4096,128]{1,0:T(8,128)(2,1)} %bitcast.35), custom_call_target="tpu_custom_call" | custom-call | flops 125000000 | tf_op jit(solution)/shard_map/prepare_edges/pallas_call | solution.py:108
  2.0 0.0 copy-start.1
  2.0 1.3 %collective-permute-start.2 = (bf16[384,640]{1,0:T(8,128)(2,1)S(1)}, bf16[384,640]{1,0:T(8,128)(2,1)S(1)}, u32[]{:S(2)}, u32[]{:S(2)}) collective-permute-start(bf16[384,640]{1,0:T(8,128)(2,1)S(1)} %get-tuple-element.70), channel_id=1, source_target_pairs={{4,1},{5,0},{6,3},{7,2},{12,9},{13,8},{14,11},{15,10},{20,17},{21,... | collective-permute-start | bytes 1474568 | tf_op jit(solution)/shard_map/ppermute | solution.py:345
  3.3 3.1 %prepare.3 = (bf16[1920,512]{1,0:T(8,128)(2,1)S(1)}, bf16[5120,128]{1,0:T(8,128)(2,1)S(1)}) custom-call(bf16[4096,4,128]{2,1,0:T(4,128)(2,1)} %bitcast.31, bf16[4096,128]{1,0:T(8,128)(2,1)} %bitcast.36), custom_call_target="tpu_custom_call" | custom-call | flops 468750016 | tf_op jit(solution)/shard_map/prepare/pallas_call | solution.py:161
  6.5 0.7 %collective-permute-start.1 = (bf16[1920,512]{1,0:T(8,128)(2,1)S(1)}, bf16[1920,512]{1,0:T(8,128)(2,1)S(1)}, u32[]{:S(2)}, u32[]{:S(2)}) collective-permute-start(bf16[1920,512]{1,0:T(8,128)(2,1)S(1)} %get-tuple-element.68.refs_0_), channel_id=1, source_target_pairs={{0,4},{1,5},{2,6},{3,7},{4,0},{5,1},{6,2},{7,3},{8,12},{9,13},{10,... | collective-permute-start | bytes 5898248 | tf_op jit(solution)/shard_map/ppermute | solution.py:345
  7.2 0.1 collective-permute-start
  7.3 2.4 %prepare.4.refs_1_.refs_0_ = bf16[1536,512]{1,0:T(8,128)(2,1)S(1)} custom-call(bf16[4096,4,128]{2,1,0:T(4,128)(2,1)} %bitcast.32, bf16[4096,128]{1,0:T(8,128)(2,1)} %bitcast.37), custom_call_target="tpu_custom_call" | custom-call | flops 375000000 | tf_op jit(solution)/shard_map/prepare/pallas_call | solution.py:161
  9.7 0.5 collective-permute-start.3
  10.1 5.3 %collective-permute-start.5 = (bf16[384,640]{1,0:T(8,128)(2,1)S(1)}, bf16[384,640]{1,0:T(8,128)(2,1)S(1)}, u32[]{:S(2)}, u32[]{:S(2)}) collective-permute-start(bf16[384,640]{1,0:T(8,128)(2,1)S(1)} %get-tuple-element.77), channel_id=1, source_target_pairs={{5,2},{6,1},{13,10},{14,9},{21,18},{22,17},{29,26},{30,25}} | collective-permute-start | bytes 1474568 | tf_op jit(solution)/shard_map/ppermute | solution.py:345
  15.4 0.0 collective-permute-done.2.refs_0_.refs_2_.refs_1_
  15.5 0.0 collective-permute-done.1.refs_1_.refs_2_.refs_0_
  15.6 0.7 %collective-permute-start.9 = (bf16[1664,128]{1,0:T(8,128)(2,1)S(1)}, bf16[1664,128]{1,0:T(8,128)(2,1)S(1)}, u32[]{:S(2)}, u32[]{:S(2)}) collective-permute-start(bf16[1664,128]{1,0:T(8,128)(2,1)S(1)} %get-tuple-element.74), channel_id=1, source_target_pairs={{24,16},{25,17},{26,18},{27,19}} | collective-permute-start | bytes 1277960 | tf_op jit(solution)/shard_map/ppermute | solution.py:345
  16.2 0.7 %collective-permute-start.10 = (bf16[512,128]{1,0:T(8,128)(2,1)S(1)}, bf16[512,128]{1,0:T(8,128)(2,1)S(1)}, u32[]{:S(2)}, u32[]{:S(2)}) collective-permute-start(bf16[512,128]{1,0:T(8,128)(2,1)S(1)} %get-tuple-element.85), channel_id=1, source_target_pairs={{24,17},{25,16},{26,19},{27,18}} | collective-permute-start | bytes 393224 | tf_op jit(solution)/shard_map/ppermute | solution.py:345
  16.9 1.8 %prepare.5.refs_1_.refs_2_ = bf16[640,512]{1,0:T(8,128)(2,1)S(1)} custom-call(bf16[4096,4,128]{2,1,0:T(4,128)(2,1)} %bitcast.33, bf16[4096,128]{1,0:T(8,128)(2,1)} %bitcast.38), custom_call_target="tpu_custom_call" | custom-call | flops 156250000 | tf_op jit(solution)/shard_map/prepare/pallas_call | solution.py:161
  18.7 0.1 collective-permute-start.4
  18.9 0.7 %collective-permute-start.8 = (bf16[1536,128]{1,0:T(8,128)(2,1)S(1)}, bf16[1536,128]{1,0:T(8,128)(2,1)S(1)}, u32[]{:S(2)}, u32[]{:S(2)}) collective-permute-start(bf16[1536,128]{1,0:T(8,128)(2,1)S(1)} %get-tuple-element.84), channel_id=1, source_target_pairs={{24,16},{25,17},{26,18},{27,19}} | collective-permute-start | bytes 1179656 | tf_op jit(solution)/shard_map/ppermute | solution.py:345
  19.6 1.6 %collective-permute-done.5.refs_3_.refs_4_.refs_2_ = bf16[384,640]{1,0:T(8,128)(2,1)S(1)} collective-permute-done((bf16[384,640]{1,0:T(8,128)(2,1)S(1)}, bf16[384,640]{1,0:T(8,128)(2,1)S(1)}, u32[]{:S(2)}, u32[]{:S(2)}) %collective-permute-start.5) | collective-permute-done | bytes 491552 | tf_op jit(solution)/shard_map/ppermute | solution.py:345
  21.2 0.7 %collective-permute-start.7 = (bf16[512,128]{1,0:T(8,128)(2,1)S(1)}, bf16[512,128]{1,0:T(8,128)(2,1)S(1)}, u32[]{:S(2)}, u32[]{:S(2)}) collective-permute-start(bf16[512,128]{1,0:T(8,128)(2,1)S(1)} %get-tuple-element.83), channel_id=1, source_target_pairs={{25,18},{26,17}} | collective-permute-start | bytes 393224 | tf_op jit(solution)/shard_map/ppermute | solution.py:345
  21.9 0.7 %collective-permute-start.6 = (bf16[896,128]{1,0:T(8,128)(2,1)S(1)}, bf16[896,128]{1,0:T(8,128)(2,1)S(1)}, u32[]{:S(2)}, u32[]{:S(2)}) collective-permute-start(bf16[896,128]{1,0:T(8,128)(2,1)S(1)} %get-tuple-element.82), channel_id=1, source_target_pairs={{24,16},{25,17},{26,18},{27,19}} | collective-permute-start | bytes 688136 | tf_op jit(solution)/shard_map/ppermute | solution.py:345
  22.5 0.0 collective-permute-done.9.refs_3_
  22.6 0.7 %collective-permute-start.15 = (bf16[512,128]{1,0:T(8,128)(2,1)S(1)}, bf16[512,128]{1,0:T(8,128)(2,1)S(1)}, u32[]{:S(2)}, u32[]{:S(2)}) collective-permute-start(bf16[512,128]{1,0:T(8,128)(2,1)S(1)} %get-tuple-element.96), channel_id=1, source_target_pairs={{16,9},{17,8},{18,11},{19,10}} | collective-permute-start | bytes 393224 | tf_op jit(solution)/shard_map/ppermute | solution.py:345
  23.3 0.7 %collective-permute-start.14 = (bf16[1152,128]{1,0:T(8,128)(2,1)S(1)}, bf16[1152,128]{1,0:T(8,128)(2,1)S(1)}, u32[]{:S(2)}, u32[]{:S(2)}) collective-permute-start(bf16[1152,128]{1,0:T(8,128)(2,1)S(1)} %get-tuple-element.95), channel_id=1, source_target_pairs={{16,8},{17,9},{18,10},{19,11}} | collective-permute-start | bytes 884744 | tf_op jit(solution)/shard_map/ppermute | solution.py:345
  24.0 0.7 %collective-permute-start.13 = (bf16[1536,128]{1,0:T(8,128)(2,1)S(1)}, bf16[1536,128]{1,0:T(8,128)(2,1)S(1)}, u32[]{:S(2)}, u32[]{:S(2)}) collective-permute-start(bf16[1536,128]{1,0:T(8,128)(2,1)S(1)} %get-tuple-element.94), channel_id=1, source_target_pairs={{16,8},{17,9},{18,10},{19,11}} | collective-permute-start | bytes 1179656 | tf_op jit(solution)/shard_map/ppermute | solution.py:345
  24.7 0.0 collective-permute-done.7.refs_6_
  24.8 0.2 pair_step.20
  25.0 0.7 %collective-permute-start.12 = (bf16[512,128]{1,0:T(8,128)(2,1)S(1)}, bf16[512,128]{1,0:T(8,128)(2,1)S(1)}, u32[]{:S(2)}, u32[]{:S(2)}) collective-permute-start(bf16[512,128]{1,0:T(8,128)(2,1)S(1)} %get-tuple-element.93), channel_id=1, source_target_pairs={{17,10},{18,9}} | collective-permute-start | bytes 393224 | tf_op jit(solution)/shard_map/ppermute | solution.py:345
  25.7 0.7 %collective-permute-start.11 = (bf16[1408,128]{1,0:T(8,128)(2,1)S(1)}, bf16[1408,128]{1,0:T(8,128)(2,1)S(1)}, u32[]{:S(2)}, u32[]{:S(2)}) collective-permute-start(bf16[1408,128]{1,0:T(8,128)(2,1)S(1)} %get-tuple-element.92), channel_id=1, source_target_pairs={{16,8},{17,9},{18,10},{19,11}} | collective-permute-start | bytes 1081352 | tf_op jit(solution)/shard_map/ppermute | solution.py:345
  26.4 0.0 collective-permute-done.15.refs_4_
  26.4 0.7 %collective-permute-start.20 = (bf16[512,128]{1,0:T(8,128)(2,1)S(1)}, bf16[512,128]{1,0:T(8,128)(2,1)S(1)}, u32[]{:S(2)}, u32[]{:S(2)}) collective-permute-start(bf16[512,128]{1,0:T(8,128)(2,1)S(1)} %get-tuple-element.107), channel_id=1, source_target_pairs={{8,1},{9,0},{10,3},{11,2}} | collective-permute-start | bytes 393224 | tf_op jit(solution)/shard_map/ppermute | solution.py:345
  27.1 0.7 %collective-permute-start.19 = (bf16[640,128]{1,0:T(8,128)(2,1)S(1)}, bf16[640,128]{1,0:T(8,128)(2,1)S(1)}, u32[]{:S(2)}, u32[]{:S(2)}) collective-permute-start(bf16[640,128]{1,0:T(8,128)(2,1)S(1)} %get-tuple-element.106), channel_id=1, source_target_pairs={{8,0},{9,1},{10,2},{11,3}} | collective-permute-start | bytes 491528 | tf_op jit(solution)/shard_map/ppermute | solution.py:345
  27.8 0.0 collective-permute-done.13.refs_4_
  27.8 0.7 %collective-permute-start.18 = (bf16[1536,128]{1,0:T(8,128)(2,1)S(1)}, bf16[1536,128]{1,0:T(8,128)(2,1)S(1)}, u32[]{:S(2)}, u32[]{:S(2)}) collective-permute-start(bf16[1536,128]{1,0:T(8,128)(2,1)S(1)} %get-tuple-element.105), channel_id=1, source_target_pairs={{8,0},{9,1},{10,2},{11,3}} | collective-permute-start | bytes 1179656 | tf_op jit(solution)/shard_map/ppermute | solution.py:345
  28.5 0.0 collective-permute-done.11.refs_5_
  28.6 0.7 %collective-permute-start.17 = (bf16[512,128]{1,0:T(8,128)(2,1)S(1)}, bf16[512,128]{1,0:T(8,128)(2,1)S(1)}, u32[]{:S(2)}, u32[]{:S(2)}) collective-permute-start(bf16[512,128]{1,0:T(8,128)(2,1)S(1)} %get-tuple-element.104), channel_id=1, source_target_pairs={{9,2},{10,1}} | collective-permute-start | bytes 393224 | tf_op jit(solution)/shard_map/ppermute | solution.py:345
  29.3 0.7 %collective-permute-start.16 = (bf16[1920,128]{1,0:T(8,128)(2,1)S(1)}, bf16[1920,128]{1,0:T(8,128)(2,1)S(1)}, u32[]{:S(2)}, u32[]{:S(2)}) collective-permute-start(bf16[1920,128]{1,0:T(8,128)(2,1)S(1)} %get-tuple-element.103), channel_id=1, source_target_pairs={{8,0},{9,1},{10,2},{11,3}} | collective-permute-start | bytes 1474568 | tf_op jit(solution)/shard_map/ppermute | solution.py:345
  30.0 0.0 collective-permute-done.20.refs_3_
  30.1 0.0 copy-start
  30.1 0.1 pair_step.25
  30.1 22.0 %collective-permute-start.22 = (bf16[1152,128]{1,0:T(8,128)(2,1)S(1)}, bf16[1152,128]{1,0:T(8,128)(2,1)S(1)}, u32[]{:S(2)}, u32[]{:S(2)}) collective-permute-start(bf16[1152,128]{1,0:T(8,128)(2,1)S(1)} %get-tuple-element.113), channel_id=1, source_target_pairs={{0,4},{1,5},{2,6},{3,7},{4,0},{5,1},{6,2},{7,3},{8,12},{9,13},{10,... | collective-permute-start | bytes 884744 | tf_op jit(solution)/shard_map/ppermute | solution.py:345
  52.1 0.1 collective-permute-start.21
  52.2 0.1 finish.3
  52.3 1.0 %collective-permute-done.22.refs_2_ = bf16[1152,128]{1,0:T(8,128)(2,1)S(1)} collective-permute-done((bf16[1152,128]{1,0:T(8,128)(2,1)S(1)}, bf16[1152,128]{1,0:T(8,128)(2,1)S(1)}, u32[]{:S(2)}, u32[]{:S(2)}) %collective-permute-start.22) | collective-permute-done | bytes 294944 | tf_op jit(solution)/shard_map/ppermute | solution.py:345
  53.3 0.5 collective-permute-done.21.refs_1_
  53.8 2.5 %finish.4 = (bf16[4608,128]{1,0:T(8,128)(2,1)S(1)}, bf16[4096,128]{1,0:T(8,128)(2,1)}, bf16[4096,4,128]{2,1,0:T(4,128)(2,1)}) custom-call(s32[4,32]{1,0:T(4,128)S(1)} %bitcast.26, bf16[1920,512]{1,0:T(8,128)(2,1)S(1)} %get-tuple-element.68.refs_0_, ...), custom_call_target="tpu_custom_call", output_to_operand_aliasing={{0}: (5, {}), {1}: (6, {}), {2}: (7, {})} | custom-call | flops 1500000000 | tf_op jit(solution)/shard_map/finish/pallas_call | solution.py:310
  56.3 0.1 pair_step.26
  56.3 2.5 %collective-permute-start.23 = (bf16[2176,128]{1,0:T(8,128)(2,1)S(1)}, bf16[2176,128]{1,0:T(8,128)(2,1)S(1)}, u32[]{:S(2)}, u32[]{:S(2)}) collective-permute-start(bf16[2176,128]{1,0:T(8,128)(2,1)S(1)} %get-tuple-element.120), channel_id=1, source_target_pairs={{0,4},{1,5},{2,6},{3,7},{4,0},{5,1},{6,2},{7,3},{8,12},{9,13},{10,... | collective-permute-start | bytes 1671176 | tf_op jit(solution)/shard_map/ppermute | solution.py:345
  58.9 1.6 %collective-permute-done.23.refs_3_ = bf16[2176,128]{1,0:T(8,128)(2,1)S(1)} collective-permute-done((bf16[2176,128]{1,0:T(8,128)(2,1)S(1)}, bf16[2176,128]{1,0:T(8,128)(2,1)S(1)}, u32[]{:S(2)}, u32[]{:S(2)}) %collective-permute-start.23) | collective-permute-done | bytes 557088 | tf_op jit(solution)/shard_map/ppermute | solution.py:345
  60.4 3.1 %finish.5 = (bf16[4608,128]{1,0:T(8,128)(2,1)S(1)}, bf16[4096,128]{1,0:T(8,128)(2,1)}, bf16[4096,4,128]{2,1,0:T(4,128)(2,1)}) custom-call(s32[4,32]{1,0:T(4,128)S(1)} %bitcast.29, bf16[1920,512]{1,0:T(8,128)(2,1)S(1)} %get-tuple-element.68.refs_0_, ...), custom_call_target="tpu_custom_call", output_to_operand_aliasing={{0}: (6, {}), {1}: (7, {}), {2}: (8, {})} | custom-call | flops 2500000000 | tf_op jit(solution)/shard_map/finish/pallas_call | solution.py:310
  (25 shorter events, 0.5 us)
Async XLA Ops:
  2.0 5.2 %copy-start.1 = (s32[1,1,32,4]{2,3,1,0:T(4,128)S(1)}, s32[1,1,32,4]{2,3,1,0:T(4,128)}, u32[]{:S(2)}) copy-start(s32[1,1,32,4]{2,3,1,0:T(4,128)} %param.6) | copy-start | bytes 1540
  2.0 13.4 %collective-permute-start.2 = (bf16[384,640]{1,0:T(8,128)(2,1)S(1)}, bf16[384,640]{1,0:T(8,128)(2,1)S(1)}, u32[]{:S(2)}, u32[]{:S(2)}) collective-permute-start(bf16[384,640]{1,0:T(8,128)(2,1)S(1)} %get-tuple-element.70), channel_id=1, source_target_pairs={{4,1},{5,0},{6,3},{7,2},{12,9},{13,8},{14,11},{15,10},{20,17},{21,... | collective-permute-start | bytes 1474568 | tf_op jit(solution)/shard_map/ppermute | solution.py:345
  6.5 9.0 %collective-permute-start.1 = (bf16[1920,512]{1,0:T(8,128)(2,1)S(1)}, bf16[1920,512]{1,0:T(8,128)(2,1)S(1)}, u32[]{:S(2)}, u32[]{:S(2)}) collective-permute-start(bf16[1920,512]{1,0:T(8,128)(2,1)S(1)} %get-tuple-element.68.refs_0_), channel_id=1, source_target_pairs={{0,4},{1,5},{2,6},{3,7},{4,0},{5,1},{6,2},{7,3},{8,12},{9,13},{10,... | collective-permute-start | bytes 5898248 | tf_op jit(solution)/shard_map/ppermute | solution.py:345
  7.2 8.2 %collective-permute-start = (s32[4,32]{1,0:T(4,128)S(1)}, s32[4,32]{1,0:T(4,128)S(1)}, u32[]{:S(2)}, u32[]{:S(2)}) collective-permute-start(s32[4,32]{1,0:T(4,128)S(1)} %bitcast.12), channel_id=1, source_target_pairs={{0,4},{1,5},{2,6},{3,7},{4,0},{5,1},{6,2},{7,3},{8,12},{9,13},{10,... | collective-permute-start | bytes 1544 | tf_op jit(solution)/shard_map/ppermute | solution.py:345
  9.7 9.1 %collective-permute-start.3 = (bf16[1536,512]{1,0:T(8,128)(2,1)S(1)}, bf16[1536,512]{1,0:T(8,128)(2,1)S(1)}, u32[]{:S(2)}, u32[]{:S(2)}) collective-permute-start(bf16[1536,512]{1,0:T(8,128)(2,1)S(1)} %prepare.4.refs_1_.refs_0_), channel_id=1, source_target_pairs={{0,4},{1,5},{2,6},{3,7},{4,0},{5,1},{6,2},{7,3},{8,12},{9,13},{10,... | collective-permute-start | bytes 4718600 | tf_op jit(solution)/shard_map/ppermute | solution.py:345
  10.1 11.0 %collective-permute-start.5 = (bf16[384,640]{1,0:T(8,128)(2,1)S(1)}, bf16[384,640]{1,0:T(8,128)(2,1)S(1)}, u32[]{:S(2)}, u32[]{:S(2)}) collective-permute-start(bf16[384,640]{1,0:T(8,128)(2,1)S(1)} %get-tuple-element.77), channel_id=1, source_target_pairs={{5,2},{6,1},{13,10},{14,9},{21,18},{22,17},{29,26},{30,25}} | collective-permute-start | bytes 1474568 | tf_op jit(solution)/shard_map/ppermute | solution.py:345
  15.6 7.0 %collective-permute-start.9 = (bf16[1664,128]{1,0:T(8,128)(2,1)S(1)}, bf16[1664,128]{1,0:T(8,128)(2,1)S(1)}, u32[]{:S(2)}, u32[]{:S(2)}) collective-permute-start(bf16[1664,128]{1,0:T(8,128)(2,1)S(1)} %get-tuple-element.74), channel_id=1, source_target_pairs={{24,16},{25,17},{26,18},{27,19}} | collective-permute-start | bytes 1277960 | tf_op jit(solution)/shard_map/ppermute | solution.py:345
  16.2 6.3 %collective-permute-start.10 = (bf16[512,128]{1,0:T(8,128)(2,1)S(1)}, bf16[512,128]{1,0:T(8,128)(2,1)S(1)}, u32[]{:S(2)}, u32[]{:S(2)}) collective-permute-start(bf16[512,128]{1,0:T(8,128)(2,1)S(1)} %get-tuple-element.85), channel_id=1, source_target_pairs={{24,17},{25,16},{26,19},{27,18}} | collective-permute-start | bytes 393224 | tf_op jit(solution)/shard_map/ppermute | solution.py:345
  18.7 2.4 %collective-permute-start.4 = (bf16[640,512]{1,0:T(8,128)(2,1)S(1)}, bf16[640,512]{1,0:T(8,128)(2,1)S(1)}, u32[]{:S(2)}, u32[]{:S(2)}) collective-permute-start(bf16[640,512]{1,0:T(8,128)(2,1)S(1)} %prepare.5.refs_1_.refs_2_), channel_id=1, source_target_pairs={{0,4},{1,5},{2,6},{3,7},{4,0},{5,1},{6,2},{7,3},{8,12},{9,13},{10,... | collective-permute-start | bytes 1966088 | tf_op jit(solution)/shard_map/ppermute | solution.py:345
  18.9 5.1 %collective-permute-start.8 = (bf16[1536,128]{1,0:T(8,128)(2,1)S(1)}, bf16[1536,128]{1,0:T(8,128)(2,1)S(1)}, u32[]{:S(2)}, u32[]{:S(2)}) collective-permute-start(bf16[1536,128]{1,0:T(8,128)(2,1)S(1)} %get-tuple-element.84), channel_id=1, source_target_pairs={{24,16},{25,17},{26,18},{27,19}} | collective-permute-start | bytes 1179656 | tf_op jit(solution)/shard_map/ppermute | solution.py:345
  21.2 3.6 %collective-permute-start.7 = (bf16[512,128]{1,0:T(8,128)(2,1)S(1)}, bf16[512,128]{1,0:T(8,128)(2,1)S(1)}, u32[]{:S(2)}, u32[]{:S(2)}) collective-permute-start(bf16[512,128]{1,0:T(8,128)(2,1)S(1)} %get-tuple-element.83), channel_id=1, source_target_pairs={{25,18},{26,17}} | collective-permute-start | bytes 393224 | tf_op jit(solution)/shard_map/ppermute | solution.py:345
  21.9 2.9 %collective-permute-start.6 = (bf16[896,128]{1,0:T(8,128)(2,1)S(1)}, bf16[896,128]{1,0:T(8,128)(2,1)S(1)}, u32[]{:S(2)}, u32[]{:S(2)}) collective-permute-start(bf16[896,128]{1,0:T(8,128)(2,1)S(1)} %get-tuple-element.82), channel_id=1, source_target_pairs={{24,16},{25,17},{26,18},{27,19}} | collective-permute-start | bytes 688136 | tf_op jit(solution)/shard_map/ppermute | solution.py:345
  22.6 3.7 %collective-permute-start.15 = (bf16[512,128]{1,0:T(8,128)(2,1)S(1)}, bf16[512,128]{1,0:T(8,128)(2,1)S(1)}, u32[]{:S(2)}, u32[]{:S(2)}) collective-permute-start(bf16[512,128]{1,0:T(8,128)(2,1)S(1)} %get-tuple-element.96), channel_id=1, source_target_pairs={{16,9},{17,8},{18,11},{19,10}} | collective-permute-start | bytes 393224 | tf_op jit(solution)/shard_map/ppermute | solution.py:345
  23.3 3.1 %collective-permute-start.14 = (bf16[1152,128]{1,0:T(8,128)(2,1)S(1)}, bf16[1152,128]{1,0:T(8,128)(2,1)S(1)}, u32[]{:S(2)}, u32[]{:S(2)}) collective-permute-start(bf16[1152,128]{1,0:T(8,128)(2,1)S(1)} %get-tuple-element.95), channel_id=1, source_target_pairs={{16,8},{17,9},{18,10},{19,11}} | collective-permute-start | bytes 884744 | tf_op jit(solution)/shard_map/ppermute | solution.py:345
  24.0 3.7 %collective-permute-start.13 = (bf16[1536,128]{1,0:T(8,128)(2,1)S(1)}, bf16[1536,128]{1,0:T(8,128)(2,1)S(1)}, u32[]{:S(2)}, u32[]{:S(2)}) collective-permute-start(bf16[1536,128]{1,0:T(8,128)(2,1)S(1)} %get-tuple-element.94), channel_id=1, source_target_pairs={{16,8},{17,9},{18,10},{19,11}} | collective-permute-start | bytes 1179656 | tf_op jit(solution)/shard_map/ppermute | solution.py:345
  25.0 3.6 %collective-permute-start.12 = (bf16[512,128]{1,0:T(8,128)(2,1)S(1)}, bf16[512,128]{1,0:T(8,128)(2,1)S(1)}, u32[]{:S(2)}, u32[]{:S(2)}) collective-permute-start(bf16[512,128]{1,0:T(8,128)(2,1)S(1)} %get-tuple-element.93), channel_id=1, source_target_pairs={{17,10},{18,9}} | collective-permute-start | bytes 393224 | tf_op jit(solution)/shard_map/ppermute | solution.py:345
  25.7 2.9 %collective-permute-start.11 = (bf16[1408,128]{1,0:T(8,128)(2,1)S(1)}, bf16[1408,128]{1,0:T(8,128)(2,1)S(1)}, u32[]{:S(2)}, u32[]{:S(2)}) collective-permute-start(bf16[1408,128]{1,0:T(8,128)(2,1)S(1)} %get-tuple-element.92), channel_id=1, source_target_pairs={{16,8},{17,9},{18,10},{19,11}} | collective-permute-start | bytes 1081352 | tf_op jit(solution)/shard_map/ppermute | solution.py:345
  26.4 3.6 %collective-permute-start.20 = (bf16[512,128]{1,0:T(8,128)(2,1)S(1)}, bf16[512,128]{1,0:T(8,128)(2,1)S(1)}, u32[]{:S(2)}, u32[]{:S(2)}) collective-permute-start(bf16[512,128]{1,0:T(8,128)(2,1)S(1)} %get-tuple-element.107), channel_id=1, source_target_pairs={{8,1},{9,0},{10,3},{11,2}} | collective-permute-start | bytes 393224 | tf_op jit(solution)/shard_map/ppermute | solution.py:345
  27.1 2.9 %collective-permute-start.19 = (bf16[640,128]{1,0:T(8,128)(2,1)S(1)}, bf16[640,128]{1,0:T(8,128)(2,1)S(1)}, u32[]{:S(2)}, u32[]{:S(2)}) collective-permute-start(bf16[640,128]{1,0:T(8,128)(2,1)S(1)} %get-tuple-element.106), channel_id=1, source_target_pairs={{8,0},{9,1},{10,2},{11,3}} | collective-permute-start | bytes 491528 | tf_op jit(solution)/shard_map/ppermute | solution.py:345
  27.8 2.2 %collective-permute-start.18 = (bf16[1536,128]{1,0:T(8,128)(2,1)S(1)}, bf16[1536,128]{1,0:T(8,128)(2,1)S(1)}, u32[]{:S(2)}, u32[]{:S(2)}) collective-permute-start(bf16[1536,128]{1,0:T(8,128)(2,1)S(1)} %get-tuple-element.105), channel_id=1, source_target_pairs={{8,0},{9,1},{10,2},{11,3}} | collective-permute-start | bytes 1179656 | tf_op jit(solution)/shard_map/ppermute | solution.py:345
  28.6 23.6 %collective-permute-start.17 = (bf16[512,128]{1,0:T(8,128)(2,1)S(1)}, bf16[512,128]{1,0:T(8,128)(2,1)S(1)}, u32[]{:S(2)}, u32[]{:S(2)}) collective-permute-start(bf16[512,128]{1,0:T(8,128)(2,1)S(1)} %get-tuple-element.104), channel_id=1, source_target_pairs={{9,2},{10,1}} | collective-permute-start | bytes 393224 | tf_op jit(solution)/shard_map/ppermute | solution.py:345
  29.3 27.0 %collective-permute-start.16 = (bf16[1920,128]{1,0:T(8,128)(2,1)S(1)}, bf16[1920,128]{1,0:T(8,128)(2,1)S(1)}, u32[]{:S(2)}, u32[]{:S(2)}) collective-permute-start(bf16[1920,128]{1,0:T(8,128)(2,1)S(1)} %get-tuple-element.103), channel_id=1, source_target_pairs={{8,0},{9,1},{10,2},{11,3}} | collective-permute-start | bytes 1474568 | tf_op jit(solution)/shard_map/ppermute | solution.py:345
  30.1 22.1 %copy-start = (bf16[1,1,4096,128]{3,2,1,0:T(8,128)(2,1)S(1)}, bf16[1,1,4096,128]{3,2,1,0:T(8,128)(2,1)}, u32[]{:S(2)}) copy-start(bf16[1,1,4096,128]{3,2,1,0:T(8,128)(2,1)} %param.7) | copy-start | bytes 3145732
  30.1 23.2 %collective-permute-start.22 = (bf16[1152,128]{1,0:T(8,128)(2,1)S(1)}, bf16[1152,128]{1,0:T(8,128)(2,1)S(1)}, u32[]{:S(2)}, u32[]{:S(2)}) collective-permute-start(bf16[1152,128]{1,0:T(8,128)(2,1)S(1)} %get-tuple-element.113), channel_id=1, source_target_pairs={{0,4},{1,5},{2,6},{3,7},{4,0},{5,1},{6,2},{7,3},{8,12},{9,13},{10,... | collective-permute-start | bytes 884744 | tf_op jit(solution)/shard_map/ppermute | solution.py:345
  52.1 1.7 %collective-permute-start.21 = (bf16[1280,128]{1,0:T(8,128)(2,1)S(1)}, bf16[1280,128]{1,0:T(8,128)(2,1)S(1)}, u32[]{:S(2)}, u32[]{:S(2)}) collective-permute-start(bf16[1280,128]{1,0:T(8,128)(2,1)S(1)} %get-tuple-element.112), channel_id=1, source_target_pairs={{0,4},{1,5},{2,6},{3,7},{4,0},{5,1},{6,2},{7,3},{8,12},{9,13},{10,... | collective-permute-start | bytes 983048 | tf_op jit(solution)/shard_map/ppermute | solution.py:345
  56.3 4.1 %collective-permute-start.23 = (bf16[2176,128]{1,0:T(8,128)(2,1)S(1)}, bf16[2176,128]{1,0:T(8,128)(2,1)S(1)}, u32[]{:S(2)}, u32[]{:S(2)}) collective-permute-start(bf16[2176,128]{1,0:T(8,128)(2,1)S(1)} %get-tuple-element.120), channel_id=1, source_target_pairs={{0,4},{1,5},{2,6},{3,7},{4,0},{5,1},{6,2},{7,3},{8,12},{9,13},{10,... | collective-permute-start | bytes 1671176 | tf_op jit(solution)/shard_map/ppermute | solution.py:345

commit v8 on v7

--- a/solution.py
+++ b/solution.py
@@ -406,14 +406,19 @@
                 gifts = [gift] if k == count - 1 else result[len(result) - len(give) :]
                 given = [move(value, swap) for value in gifts]
                 if k == count - 2:
-                    half = max(0, give[-1][1] - WIDE) // GROUP * GROUP
+                    halves = max(0, give[-1][1] - WIDE), max(0, give[-1][1] - REACH)
                     done = []
                     for odd_column in (0, 1):
                         takes = (given, give) if odd_column else ([], [])
                         extra = [] if odd_column else [halo]
-                        keeps[0], *done = finish(0, half, odd_column, tiles, pairs, cuts, table, own, *takes, left, keeps[0], done, extra)
+                        keeps[0], *done = finish(0, halves[odd_column], odd_column, tiles, pairs, cuts, table, own, *takes, left, keeps[0], done, extra)
                 else:
-                    _, env, grad = finish(half, tiles, None, tiles, pairs, cuts, table, own, given, give, left, keeps[0], done)
+                    state = keeps[0]
+                    for odd_column in (0, 1):
+                        takes = (given, give) if odd_column else ([], [])
+                        begin = halves[odd_column]
+                        state, *done = finish(begin, tiles, odd_column, tiles, pairs, cuts, table, own, *takes, left, state, done)
+                    env, grad = done
             leaving.append(result[2:])
         sent = leaving
 

time: 64.9 us -> 64.7 us (level)
    pallas_call x3 -> x4, Pallas kernels: 5.69 us -> 5.8 us  [finish(): pl.pallas_call(kernel, in_specs=[ANY] + [VMEM] * fixed + [HBM] * len(done...]
where the time goes in v8:
time: 64.7 us; the launch traced here: 63.4 us
  starting transfers between devices  42.5 us (66%)
  Pallas kernels  15.2 us (23%)
  waiting for transfers between devices  4.46 us (7%)
  between operations  1.26 us (2%)
    ppermute x24, starting transfers between devices, move(): return lax.ppermute(value, ('col', 'sec'), both)  42.5 us
    pallas_call x3, Pallas kernels, prepare(): pl.pallas_call(kernel, in_specs=[HBM, HBM], out_specs=[VMEM] * len(outs),...  7.28 us
    pallas_call x4, Pallas kernels, finish(): pl.pallas_call(kernel, in_specs=[ANY] + [VMEM] * fixed + [HBM] * len(done...  5.8 us
    ppermute x24, waiting for transfers between devices, move(): return lax.ppermute(value, ('col', 'sec'), both)  4.46 us
    pallas_call x1, Pallas kernels, prepare_edges(): pl.pallas_call(kernel, in_specs=[HBM, HBM, HBM], out_specs=[VMEM, VMEM],...  1.36 us
  transfers between devices with their start and end apart: 24, of which 4 were waited for; matrix products, arithmetic and copies ran while one was open for 0% of the time, Pallas kernels for 17%

profile of v8, /device:TPU:3, one launch (start us, length us, event | category | flops | bytes accessed | tf_op | source)
XLA Modules:
  0.0 63.4 jit_solution(437357007949552580)
XLA Ops:
  0.6 1.4 %prepare_edges.1 = (bf16[384,640]{1,0:T(8,128)(2,1)S(1)}, bf16[384,640]{1,0:T(8,128)(2,1)S(1)}) custom-call(s32[4,32]{1,0:T(4,128)} %bitcast.12, bf16[4096,4,128]{2,1,0:T(4,128)(2,1)} %bitcast.32, bf16[4096,128]{1,0:T(8,128)(2,1)} %bitcast.37), custom_call_target="tpu_custom_call" | custom-call | flops 125000000 | tf_op jit(solution)/shard_map/prepare_edges/pallas_call | solution.py:108
  2.0 0.0 copy-start.1
  2.0 1.3 %collective-permute-start.2 = (bf16[384,640]{1,0:T(8,128)(2,1)S(1)}, bf16[384,640]{1,0:T(8,128)(2,1)S(1)}, u32[]{:S(2)}, u32[]{:S(2)}) collective-permute-start(bf16[384,640]{1,0:T(8,128)(2,1)S(1)} %get-tuple-element.73), channel_id=1, source_target_pairs={{4,1},{5,0},{6,3},{7,2},{12,9},{13,8},{14,11},{15,10},{20,17},{21,... | collective-permute-start | bytes 1474568 | tf_op jit(solution)/shard_map/ppermute | solution.py:345
  3.3 3.1 %prepare.4 = (bf16[1920,512]{1,0:T(8,128)(2,1)S(1)}, bf16[5120,128]{1,0:T(8,128)(2,1)S(1)}) custom-call(bf16[4096,4,128]{2,1,0:T(4,128)(2,1)} %bitcast.33, bf16[4096,128]{1,0:T(8,128)(2,1)} %bitcast.38), custom_call_target="tpu_custom_call" | custom-call | flops 468750016 | tf_op jit(solution)/shard_map/prepare/pallas_call | solution.py:161
  6.5 0.7 %collective-permute-start.1 = (bf16[1920,512]{1,0:T(8,128)(2,1)S(1)}, bf16[1920,512]{1,0:T(8,128)(2,1)S(1)}, u32[]{:S(2)}, u32[]{:S(2)}) collective-permute-start(bf16[1920,512]{1,0:T(8,128)(2,1)S(1)} %get-tuple-element.71.refs_0_), channel_id=1, source_target_pairs={{0,4},{1,5},{2,6},{3,7},{4,0},{5,1},{6,2},{7,3},{8,12},{9,13},{10,... | collective-permute-start | bytes 5898248 | tf_op jit(solution)/shard_map/ppermute | solution.py:345
  7.2 0.1 collective-permute-start
  7.3 2.4 %prepare.3.refs_1_.refs_0_ = bf16[1536,512]{1,0:T(8,128)(2,1)S(1)} custom-call(bf16[4096,4,128]{2,1,0:T(4,128)(2,1)} %bitcast.34, bf16[4096,128]{1,0:T(8,128)(2,1)} %bitcast.39), custom_call_target="tpu_custom_call" | custom-call | flops 375000000 | tf_op jit(solution)/shard_map/prepare/pallas_call | solution.py:161
  9.7 0.5 collective-permute-start.3
  10.1 5.3 %collective-permute-start.5 = (bf16[384,640]{1,0:T(8,128)(2,1)S(1)}, bf16[384,640]{1,0:T(8,128)(2,1)S(1)}, u32[]{:S(2)}, u32[]{:S(2)}) collective-permute-start(bf16[384,640]{1,0:T(8,128)(2,1)S(1)} %get-tuple-element.80), channel_id=1, source_target_pairs={{5,2},{6,1},{13,10},{14,9},{21,18},{22,17},{29,26},{30,25}} | collective-permute-start | bytes 1474568 | tf_op jit(solution)/shard_map/ppermute | solution.py:345
  15.4 0.0 collective-permute-done.odd_list
  15.5 0.0 collective-permute-done.1.refs_1_.refs_2_.refs_0_
  15.6 0.7 %collective-permute-start.9 = (bf16[1664,128]{1,0:T(8,128)(2,1)S(1)}, bf16[1664,128]{1,0:T(8,128)(2,1)S(1)}, u32[]{:S(2)}, u32[]{:S(2)}) collective-permute-start(bf16[1664,128]{1,0:T(8,128)(2,1)S(1)} %get-tuple-element.77), channel_id=1, source_target_pairs={{24,16},{25,17},{26,18},{27,19}} | collective-permute-start | bytes 1277960 | tf_op jit(solution)/shard_map/ppermute | solution.py:345
  16.2 0.7 %collective-permute-start.10 = (bf16[512,128]{1,0:T(8,128)(2,1)S(1)}, bf16[512,128]{1,0:T(8,128)(2,1)S(1)}, u32[]{:S(2)}, u32[]{:S(2)}) collective-permute-start(bf16[512,128]{1,0:T(8,128)(2,1)S(1)} %get-tuple-element.88), channel_id=1, source_target_pairs={{24,17},{25,16},{26,19},{27,18}} | collective-permute-start | bytes 393224 | tf_op jit(solution)/shard_map/ppermute | solution.py:345
  16.9 1.8 %prepare.5.refs_1_.refs_2_ = bf16[640,512]{1,0:T(8,128)(2,1)S(1)} custom-call(bf16[4096,4,128]{2,1,0:T(4,128)(2,1)} %bitcast.35, bf16[4096,128]{1,0:T(8,128)(2,1)} %bitcast.40), custom_call_target="tpu_custom_call" | custom-call | flops 156250000 | tf_op jit(solution)/shard_map/prepare/pallas_call | solution.py:161
  18.7 0.1 collective-permute-start.4
  18.8 0.0 collective-permute-done.3.refs_2_.refs_3_.refs_0_
  18.9 0.7 %collective-permute-start.8 = (bf16[1536,128]{1,0:T(8,128)(2,1)S(1)}, bf16[1536,128]{1,0:T(8,128)(2,1)S(1)}, u32[]{:S(2)}, u32[]{:S(2)}) collective-permute-start(bf16[1536,128]{1,0:T(8,128)(2,1)S(1)} %get-tuple-element.87), channel_id=1, source_target_pairs={{24,16},{25,17},{26,18},{27,19}} | collective-permute-start | bytes 1179656 | tf_op jit(solution)/shard_map/ppermute | solution.py:345
  19.6 1.6 %collective-permute-done.5.refs_3_.refs_4_.refs_2_ = bf16[384,640]{1,0:T(8,128)(2,1)S(1)} collective-permute-done((bf16[384,640]{1,0:T(8,128)(2,1)S(1)}, bf16[384,640]{1,0:T(8,128)(2,1)S(1)}, u32[]{:S(2)}, u32[]{:S(2)}) %collective-permute-start.5) | collective-permute-done | bytes 491552 | tf_op jit(solution)/shard_map/ppermute | solution.py:345
  21.1 0.0 collective-permute-done.4.refs_2_.refs_3_.refs_1_
  21.2 0.7 %collective-permute-start.7 = (bf16[512,128]{1,0:T(8,128)(2,1)S(1)}, bf16[512,128]{1,0:T(8,128)(2,1)S(1)}, u32[]{:S(2)}, u32[]{:S(2)}) collective-permute-start(bf16[512,128]{1,0:T(8,128)(2,1)S(1)} %get-tuple-element.86), channel_id=1, source_target_pairs={{25,18},{26,17}} | collective-permute-start | bytes 393224 | tf_op jit(solution)/shard_map/ppermute | solution.py:345
  21.9 0.7 %collective-permute-start.6 = (bf16[896,128]{1,0:T(8,128)(2,1)S(1)}, bf16[896,128]{1,0:T(8,128)(2,1)S(1)}, u32[]{:S(2)}, u32[]{:S(2)}) collective-permute-start(bf16[896,128]{1,0:T(8,128)(2,1)S(1)} %get-tuple-element.85), channel_id=1, source_target_pairs={{24,16},{25,17},{26,18},{27,19}} | collective-permute-start | bytes 688136 | tf_op jit(solution)/shard_map/ppermute | solution.py:345
  22.5 0.0 collective-permute-done.10.refs_4_
  22.6 0.7 %collective-permute-start.15 = (bf16[512,128]{1,0:T(8,128)(2,1)S(1)}, bf16[512,128]{1,0:T(8,128)(2,1)S(1)}, u32[]{:S(2)}, u32[]{:S(2)}) collective-permute-start(bf16[512,128]{1,0:T(8,128)(2,1)S(1)} %get-tuple-element.99), channel_id=1, source_target_pairs={{16,9},{17,8},{18,11},{19,10}} | collective-permute-start | bytes 393224 | tf_op jit(solution)/shard_map/ppermute | solution.py:345
  23.3 0.7 %collective-permute-start.14 = (bf16[1152,128]{1,0:T(8,128)(2,1)S(1)}, bf16[1152,128]{1,0:T(8,128)(2,1)S(1)}, u32[]{:S(2)}, u32[]{:S(2)}) collective-permute-start(bf16[1152,128]{1,0:T(8,128)(2,1)S(1)} %get-tuple-element.98), channel_id=1, source_target_pairs={{16,8},{17,9},{18,10},{19,11}} | collective-permute-start | bytes 884744 | tf_op jit(solution)/shard_map/ppermute | solution.py:345
  24.0 0.0 collective-permute-done.8.refs_4_
  24.0 0.7 %collective-permute-start.13 = (bf16[1536,128]{1,0:T(8,128)(2,1)S(1)}, bf16[1536,128]{1,0:T(8,128)(2,1)S(1)}, u32[]{:S(2)}, u32[]{:S(2)}) collective-permute-start(bf16[1536,128]{1,0:T(8,128)(2,1)S(1)} %get-tuple-element.97), channel_id=1, source_target_pairs={{16,8},{17,9},{18,10},{19,11}} | collective-permute-start | bytes 1179656 | tf_op jit(solution)/shard_map/ppermute | solution.py:345
  24.7 0.0 collective-permute-done.7.refs_6_
  24.8 0.2 pair_step.20
  25.0 0.7 %collective-permute-start.12 = (bf16[512,128]{1,0:T(8,128)(2,1)S(1)}, bf16[512,128]{1,0:T(8,128)(2,1)S(1)}, u32[]{:S(2)}, u32[]{:S(2)}) collective-permute-start(bf16[512,128]{1,0:T(8,128)(2,1)S(1)} %get-tuple-element.96), channel_id=1, source_target_pairs={{17,10},{18,9}} | collective-permute-start | bytes 393224 | tf_op jit(solution)/shard_map/ppermute | solution.py:345
  25.7 0.7 %collective-permute-start.11 = (bf16[1408,128]{1,0:T(8,128)(2,1)S(1)}, bf16[1408,128]{1,0:T(8,128)(2,1)S(1)}, u32[]{:S(2)}, u32[]{:S(2)}) collective-permute-start(bf16[1408,128]{1,0:T(8,128)(2,1)S(1)} %get-tuple-element.95), channel_id=1, source_target_pairs={{16,8},{17,9},{18,10},{19,11}} | collective-permute-start | bytes 1081352 | tf_op jit(solution)/shard_map/ppermute | solution.py:345
  26.4 0.7 %collective-permute-start.20 = (bf16[512,128]{1,0:T(8,128)(2,1)S(1)}, bf16[512,128]{1,0:T(8,128)(2,1)S(1)}, u32[]{:S(2)}, u32[]{:S(2)}) collective-permute-start(bf16[512,128]{1,0:T(8,128)(2,1)S(1)} %get-tuple-element.110), channel_id=1, source_target_pairs={{8,1},{9,0},{10,3},{11,2}} | collective-permute-start | bytes 393224 | tf_op jit(solution)/shard_map/ppermute | solution.py:345
  27.1 0.7 %collective-permute-start.19 = (bf16[640,128]{1,0:T(8,128)(2,1)S(1)}, bf16[640,128]{1,0:T(8,128)(2,1)S(1)}, u32[]{:S(2)}, u32[]{:S(2)}) collective-permute-start(bf16[640,128]{1,0:T(8,128)(2,1)S(1)} %get-tuple-element.109), channel_id=1, source_target_pairs={{8,0},{9,1},{10,2},{11,3}} | collective-permute-start | bytes 491528 | tf_op jit(solution)/shard_map/ppermute | solution.py:345
  27.8 0.7 %collective-permute-start.18 = (bf16[1536,128]{1,0:T(8,128)(2,1)S(1)}, bf16[1536,128]{1,0:T(8,128)(2,1)S(1)}, u32[]{:S(2)}, u32[]{:S(2)}) collective-permute-start(bf16[1536,128]{1,0:T(8,128)(2,1)S(1)} %get-tuple-element.108), channel_id=1, source_target_pairs={{8,0},{9,1},{10,2},{11,3}} | collective-permute-start | bytes 1179656 | tf_op jit(solution)/shard_map/ppermute | solution.py:345
  28.6 0.7 %collective-permute-start.17 = (bf16[512,128]{1,0:T(8,128)(2,1)S(1)}, bf16[512,128]{1,0:T(8,128)(2,1)S(1)}, u32[]{:S(2)}, u32[]{:S(2)}) collective-permute-start(bf16[512,128]{1,0:T(8,128)(2,1)S(1)} %get-tuple-element.107), channel_id=1, source_target_pairs={{9,2},{10,1}} | collective-permute-start | bytes 393224 | tf_op jit(solution)/shard_map/ppermute | solution.py:345
  29.3 0.7 %collective-permute-start.16 = (bf16[1920,128]{1,0:T(8,128)(2,1)S(1)}, bf16[1920,128]{1,0:T(8,128)(2,1)S(1)}, u32[]{:S(2)}, u32[]{:S(2)}) collective-permute-start(bf16[1920,128]{1,0:T(8,128)(2,1)S(1)} %get-tuple-element.106), channel_id=1, source_target_pairs={{8,0},{9,1},{10,2},{11,3}} | collective-permute-start | bytes 1474568 | tf_op jit(solution)/shard_map/ppermute | solution.py:345
  30.1 0.0 copy-start
  30.1 0.1 pair_step.25
  30.1 22.0 %collective-permute-start.22 = (bf16[1152,128]{1,0:T(8,128)(2,1)S(1)}, bf16[1152,128]{1,0:T(8,128)(2,1)S(1)}, u32[]{:S(2)}, u32[]{:S(2)}) collective-permute-start(bf16[1152,128]{1,0:T(8,128)(2,1)S(1)} %get-tuple-element.116), channel_id=1, source_target_pairs={{0,4},{1,5},{2,6},{3,7},{4,0},{5,1},{6,2},{7,3},{8,12},{9,13},{10,... | collective-permute-start | bytes 884744 | tf_op jit(solution)/shard_map/ppermute | solution.py:345
  52.1 0.1 collective-permute-start.21
  52.2 0.1 finish.4
  52.4 1.0 %collective-permute-done.22.refs_2_ = bf16[1152,128]{1,0:T(8,128)(2,1)S(1)} collective-permute-done((bf16[1152,128]{1,0:T(8,128)(2,1)S(1)}, bf16[1152,128]{1,0:T(8,128)(2,1)S(1)}, u32[]{:S(2)}, u32[]{:S(2)}) %collective-permute-start.22) | collective-permute-done | bytes 294944 | tf_op jit(solution)/shard_map/ppermute | solution.py:345
  53.3 0.5 collective-permute-done.21.refs_1_
  53.8 2.6 %finish.5 = (bf16[4608,128]{1,0:T(8,128)(2,1)S(1)}, bf16[4096,128]{1,0:T(8,128)(2,1)}, bf16[4096,4,128]{2,1,0:T(4,128)(2,1)}) custom-call(s32[4,32]{1,0:T(4,128)S(1)} %bitcast.27, bf16[1920,512]{1,0:T(8,128)(2,1)S(1)} %get-tuple-element.71.refs_0_, ...), custom_call_target="tpu_custom_call", output_to_operand_aliasing={{0}: (5, {}), {1}: (6, {}), {2}: (7, {})} | custom-call | flops 1875000064 | tf_op jit(solution)/shard_map/finish/pallas_call | solution.py:310
  56.5 0.1 pair_step.26
  56.5 2.3 %collective-permute-start.23 = (bf16[2176,128]{1,0:T(8,128)(2,1)S(1)}, bf16[2176,128]{1,0:T(8,128)(2,1)S(1)}, u32[]{:S(2)}, u32[]{:S(2)}) collective-permute-start(bf16[2176,128]{1,0:T(8,128)(2,1)S(1)} %get-tuple-element.123), channel_id=1, source_target_pairs={{0,4},{1,5},{2,6},{3,7},{4,0},{5,1},{6,2},{7,3},{8,12},{9,13},{10,... | collective-permute-start | bytes 1671176 | tf_op jit(solution)/shard_map/ppermute | solution.py:345
  58.9 0.2 finish.6
  59.1 1.4 %collective-permute-done.23.refs_2_ = bf16[2176,128]{1,0:T(8,128)(2,1)S(1)} collective-permute-done((bf16[2176,128]{1,0:T(8,128)(2,1)S(1)}, bf16[2176,128]{1,0:T(8,128)(2,1)S(1)}, u32[]{:S(2)}, u32[]{:S(2)}) %collective-permute-start.23) | collective-permute-done | bytes 557088 | tf_op jit(solution)/shard_map/ppermute | solution.py:345
  60.4 2.8 %finish.7 = (bf16[4608,128]{1,0:T(8,128)(2,1)S(1)}, bf16[4096,128]{1,0:T(8,128)(2,1)}, bf16[4096,4,128]{2,1,0:T(4,128)(2,1)}) custom-call(s32[4,32]{1,0:T(4,128)S(1)} %bitcast.31, bf16[1536,512]{1,0:T(8,128)(2,1)S(1)} %prepare.3.refs_1_.refs_0_, ...), custom_call_target="tpu_custom_call", output_to_operand_aliasing={{0}: (5, {}), {1}: (6, {}), {2}: (7, {})} | custom-call | flops 2124999936 | tf_op jit(solution)/shard_map/finish/pallas_call | solution.py:310
  (26 shorter events, 0.5 us)
Async XLA Ops:
  2.0 5.2 %copy-start.1 = (s32[1,1,32,4]{2,3,1,0:T(4,128)S(1)}, s32[1,1,32,4]{2,3,1,0:T(4,128)}, u32[]{:S(2)}) copy-start(s32[1,1,32,4]{2,3,1,0:T(4,128)} %param.6) | copy-start | bytes 1540
  2.0 13.4 %collective-permute-start.2 = (bf16[384,640]{1,0:T(8,128)(2,1)S(1)}, bf16[384,640]{1,0:T(8,128)(2,1)S(1)}, u32[]{:S(2)}, u32[]{:S(2)}) collective-permute-start(bf16[384,640]{1,0:T(8,128)(2,1)S(1)} %get-tuple-element.73), channel_id=1, source_target_pairs={{4,1},{5,0},{6,3},{7,2},{12,9},{13,8},{14,11},{15,10},{20,17},{21,... | collective-permute-start | bytes 1474568 | tf_op jit(solution)/shard_map/ppermute | solution.py:345
  6.5 9.0 %collective-permute-start.1 = (bf16[1920,512]{1,0:T(8,128)(2,1)S(1)}, bf16[1920,512]{1,0:T(8,128)(2,1)S(1)}, u32[]{:S(2)}, u32[]{:S(2)}) collective-permute-start(bf16[1920,512]{1,0:T(8,128)(2,1)S(1)} %get-tuple-element.71.refs_0_), channel_id=1, source_target_pairs={{0,4},{1,5},{2,6},{3,7},{4,0},{5,1},{6,2},{7,3},{8,12},{9,13},{10,... | collective-permute-start | bytes 5898248 | tf_op jit(solution)/shard_map/ppermute | solution.py:345
  7.2 8.2 %collective-permute-start = (s32[4,32]{1,0:T(4,128)S(1)}, s32[4,32]{1,0:T(4,128)S(1)}, u32[]{:S(2)}, u32[]{:S(2)}) collective-permute-start(s32[4,32]{1,0:T(4,128)S(1)} %bitcast.13), channel_id=1, source_target_pairs={{0,4},{1,5},{2,6},{3,7},{4,0},{5,1},{6,2},{7,3},{8,12},{9,13},{10,... | collective-permute-start | bytes 1544 | tf_op jit(solution)/shard_map/ppermute | solution.py:345
  9.7 9.1 %collective-permute-start.3 = (bf16[1536,512]{1,0:T(8,128)(2,1)S(1)}, bf16[1536,512]{1,0:T(8,128)(2,1)S(1)}, u32[]{:S(2)}, u32[]{:S(2)}) collective-permute-start(bf16[1536,512]{1,0:T(8,128)(2,1)S(1)} %prepare.3.refs_1_.refs_0_), channel_id=1, source_target_pairs={{0,4},{1,5},{2,6},{3,7},{4,0},{5,1},{6,2},{7,3},{8,12},{9,13},{10,... | collective-permute-start | bytes 4718600 | tf_op jit(solution)/shard_map/ppermute | solution.py:345
  10.1 11.0 %collective-permute-start.5 = (bf16[384,640]{1,0:T(8,128)(2,1)S(1)}, bf16[384,640]{1,0:T(8,128)(2,1)S(1)}, u32[]{:S(2)}, u32[]{:S(2)}) collective-permute-start(bf16[384,640]{1,0:T(8,128)(2,1)S(1)} %get-tuple-element.80), channel_id=1, source_target_pairs={{5,2},{6,1},{13,10},{14,9},{21,18},{22,17},{29,26},{30,25}} | collective-permute-start | bytes 1474568 | tf_op jit(solution)/shard_map/ppermute | solution.py:345
  15.6 7.0 %collective-permute-start.9 = (bf16[1664,128]{1,0:T(8,128)(2,1)S(1)}, bf16[1664,128]{1,0:T(8,128)(2,1)S(1)}, u32[]{:S(2)}, u32[]{:S(2)}) collective-permute-start(bf16[1664,128]{1,0:T(8,128)(2,1)S(1)} %get-tuple-element.77), channel_id=1, source_target_pairs={{24,16},{25,17},{26,18},{27,19}} | collective-permute-start | bytes 1277960 | tf_op jit(solution)/shard_map/ppermute | solution.py:345
  16.2 6.3 %collective-permute-start.10 = (bf16[512,128]{1,0:T(8,128)(2,1)S(1)}, bf16[512,128]{1,0:T(8,128)(2,1)S(1)}, u32[]{:S(2)}, u32[]{:S(2)}) collective-permute-start(bf16[512,128]{1,0:T(8,128)(2,1)S(1)} %get-tuple-element.88), channel_id=1, source_target_pairs={{24,17},{25,16},{26,19},{27,18}} | collective-permute-start | bytes 393224 | tf_op jit(solution)/shard_map/ppermute | solution.py:345
  18.7 2.4 %collective-permute-start.4 = (bf16[640,512]{1,0:T(8,128)(2,1)S(1)}, bf16[640,512]{1,0:T(8,128)(2,1)S(1)}, u32[]{:S(2)}, u32[]{:S(2)}) collective-permute-start(bf16[640,512]{1,0:T(8,128)(2,1)S(1)} %prepare.5.refs_1_.refs_2_), channel_id=1, source_target_pairs={{0,4},{1,5},{2,6},{3,7},{4,0},{5,1},{6,2},{7,3},{8,12},{9,13},{10,... | collective-permute-start | bytes 1966088 | tf_op jit(solution)/shard_map/ppermute | solution.py:345
  18.9 5.1 %collective-permute-start.8 = (bf16[1536,128]{1,0:T(8,128)(2,1)S(1)}, bf16[1536,128]{1,0:T(8,128)(2,1)S(1)}, u32[]{:S(2)}, u32[]{:S(2)}) collective-permute-start(bf16[1536,128]{1,0:T(8,128)(2,1)S(1)} %get-tuple-element.87), channel_id=1, source_target_pairs={{24,16},{25,17},{26,18},{27,19}} | collective-permute-start | bytes 1179656 | tf_op jit(solution)/shard_map/ppermute | solution.py:345
  21.2 3.6 %collective-permute-start.7 = (bf16[512,128]{1,0:T(8,128)(2,1)S(1)}, bf16[512,128]{1,0:T(8,128)(2,1)S(1)}, u32[]{:S(2)}, u32[]{:S(2)}) collective-permute-start(bf16[512,128]{1,0:T(8,128)(2,1)S(1)} %get-tuple-element.86), channel_id=1, source_target_pairs={{25,18},{26,17}} | collective-permute-start | bytes 393224 | tf_op jit(solution)/shard_map/ppermute | solution.py:345
  21.9 2.9 %collective-permute-start.6 = (bf16[896,128]{1,0:T(8,128)(2,1)S(1)}, bf16[896,128]{1,0:T(8,128)(2,1)S(1)}, u32[]{:S(2)}, u32[]{:S(2)}) collective-permute-start(bf16[896,128]{1,0:T(8,128)(2,1)S(1)} %get-tuple-element.85), channel_id=1, source_target_pairs={{24,16},{25,17},{26,18},{27,19}} | collective-permute-start | bytes 688136 | tf_op jit(solution)/shard_map/ppermute | solution.py:345
  22.6 3.7 %collective-permute-start.15 = (bf16[512,128]{1,0:T(8,128)(2,1)S(1)}, bf16[512,128]{1,0:T(8,128)(2,1)S(1)}, u32[]{:S(2)}, u32[]{:S(2)}) collective-permute-start(bf16[512,128]{1,0:T(8,128)(2,1)S(1)} %get-tuple-element.99), channel_id=1, source_target_pairs={{16,9},{17,8},{18,11},{19,10}} | collective-permute-start | bytes 393224 | tf_op jit(solution)/shard_map/ppermute | solution.py:345
  23.3 3.1 %collective-permute-start.14 = (bf16[1152,128]{1,0:T(8,128)(2,1)S(1)}, bf16[1152,128]{1,0:T(8,128)(2,1)S(1)}, u32[]{:S(2)}, u32[]{:S(2)}) collective-permute-start(bf16[1152,128]{1,0:T(8,128)(2,1)S(1)} %get-tuple-element.98), channel_id=1, source_target_pairs={{16,8},{17,9},{18,10},{19,11}} | collective-permute-start | bytes 884744 | tf_op jit(solution)/shard_map/ppermute | solution.py:345
  24.0 3.7 %collective-permute-start.13 = (bf16[1536,128]{1,0:T(8,128)(2,1)S(1)}, bf16[1536,128]{1,0:T(8,128)(2,1)S(1)}, u32[]{:S(2)}, u32[]{:S(2)}) collective-permute-start(bf16[1536,128]{1,0:T(8,128)(2,1)S(1)} %get-tuple-element.97), channel_id=1, source_target_pairs={{16,8},{17,9},{18,10},{19,11}} | collective-permute-start | bytes 1179656 | tf_op jit(solution)/shard_map/ppermute | solution.py:345
  25.0 3.6 %collective-permute-start.12 = (bf16[512,128]{1,0:T(8,128)(2,1)S(1)}, bf16[512,128]{1,0:T(8,128)(2,1)S(1)}, u32[]{:S(2)}, u32[]{:S(2)}) collective-permute-start(bf16[512,128]{1,0:T(8,128)(2,1)S(1)} %get-tuple-element.96), channel_id=1, source_target_pairs={{17,10},{18,9}} | collective-permute-start | bytes 393224 | tf_op jit(solution)/shard_map/ppermute | solution.py:345
  25.7 2.9 %collective-permute-start.11 = (bf16[1408,128]{1,0:T(8,128)(2,1)S(1)}, bf16[1408,128]{1,0:T(8,128)(2,1)S(1)}, u32[]{:S(2)}, u32[]{:S(2)}) collective-permute-start(bf16[1408,128]{1,0:T(8,128)(2,1)S(1)} %get-tuple-element.95), channel_id=1, source_target_pairs={{16,8},{17,9},{18,10},{19,11}} | collective-permute-start | bytes 1081352 | tf_op jit(solution)/shard_map/ppermute | solution.py:345
  26.4 3.6 %collective-permute-start.20 = (bf16[512,128]{1,0:T(8,128)(2,1)S(1)}, bf16[512,128]{1,0:T(8,128)(2,1)S(1)}, u32[]{:S(2)}, u32[]{:S(2)}) collective-permute-start(bf16[512,128]{1,0:T(8,128)(2,1)S(1)} %get-tuple-element.110), channel_id=1, source_target_pairs={{8,1},{9,0},{10,3},{11,2}} | collective-permute-start | bytes 393224 | tf_op jit(solution)/shard_map/ppermute | solution.py:345
  27.1 2.9 %collective-permute-start.19 = (bf16[640,128]{1,0:T(8,128)(2,1)S(1)}, bf16[640,128]{1,0:T(8,128)(2,1)S(1)}, u32[]{:S(2)}, u32[]{:S(2)}) collective-permute-start(bf16[640,128]{1,0:T(8,128)(2,1)S(1)} %get-tuple-element.109), channel_id=1, source_target_pairs={{8,0},{9,1},{10,2},{11,3}} | collective-permute-start | bytes 491528 | tf_op jit(solution)/shard_map/ppermute | solution.py:345
  27.8 2.2 %collective-permute-start.18 = (bf16[1536,128]{1,0:T(8,128)(2,1)S(1)}, bf16[1536,128]{1,0:T(8,128)(2,1)S(1)}, u32[]{:S(2)}, u32[]{:S(2)}) collective-permute-start(bf16[1536,128]{1,0:T(8,128)(2,1)S(1)} %get-tuple-element.108), channel_id=1, source_target_pairs={{8,0},{9,1},{10,2},{11,3}} | collective-permute-start | bytes 1179656 | tf_op jit(solution)/shard_map/ppermute | solution.py:345
  28.6 23.6 %collective-permute-start.17 = (bf16[512,128]{1,0:T(8,128)(2,1)S(1)}, bf16[512,128]{1,0:T(8,128)(2,1)S(1)}, u32[]{:S(2)}, u32[]{:S(2)}) collective-permute-start(bf16[512,128]{1,0:T(8,128)(2,1)S(1)} %get-tuple-element.107), channel_id=1, source_target_pairs={{9,2},{10,1}} | collective-permute-start | bytes 393224 | tf_op jit(solution)/shard_map/ppermute | solution.py:345
  29.3 27.2 %collective-permute-start.16 = (bf16[1920,128]{1,0:T(8,128)(2,1)S(1)}, bf16[1920,128]{1,0:T(8,128)(2,1)S(1)}, u32[]{:S(2)}, u32[]{:S(2)}) collective-permute-start(bf16[1920,128]{1,0:T(8,128)(2,1)S(1)} %get-tuple-element.106), channel_id=1, source_target_pairs={{8,0},{9,1},{10,2},{11,3}} | collective-permute-start | bytes 1474568 | tf_op jit(solution)/shard_map/ppermute | solution.py:345
  30.1 22.1 %copy-start = (bf16[1,1,4096,128]{3,2,1,0:T(8,128)(2,1)S(1)}, bf16[1,1,4096,128]{3,2,1,0:T(8,128)(2,1)}, u32[]{:S(2)}) copy-start(bf16[1,1,4096,128]{3,2,1,0:T(8,128)(2,1)} %param.7) | copy-start | bytes 3145732
  30.1 23.2 %collective-permute-start.22 = (bf16[1152,128]{1,0:T(8,128)(2,1)S(1)}, bf16[1152,128]{1,0:T(8,128)(2,1)S(1)}, u32[]{:S(2)}, u32[]{:S(2)}) collective-permute-start(bf16[1152,128]{1,0:T(8,128)(2,1)S(1)} %get-tuple-element.116), channel_id=1, source_target_pairs={{0,4},{1,5},{2,6},{3,7},{4,0},{5,1},{6,2},{7,3},{8,12},{9,13},{10,... | collective-permute-start | bytes 884744 | tf_op jit(solution)/shard_map/ppermute | solution.py:345
  52.1 1.7 %collective-permute-start.21 = (bf16[1280,128]{1,0:T(8,128)(2,1)S(1)}, bf16[1280,128]{1,0:T(8,128)(2,1)S(1)}, u32[]{:S(2)}, u32[]{:S(2)}) collective-permute-start(bf16[1280,128]{1,0:T(8,128)(2,1)S(1)} %get-tuple-element.115), channel_id=1, source_target_pairs={{0,4},{1,5},{2,6},{3,7},{4,0},{5,1},{6,2},{7,3},{8,12},{9,13},{10,... | collective-permute-start | bytes 983048 | tf_op jit(solution)/shard_map/ppermute | solution.py:345
  56.5 3.9 %collective-permute-start.23 = (bf16[2176,128]{1,0:T(8,128)(2,1)S(1)}, bf16[2176,128]{1,0:T(8,128)(2,1)S(1)}, u32[]{:S(2)}, u32[]{:S(2)}) collective-permute-start(bf16[2176,128]{1,0:T(8,128)(2,1)S(1)} %get-tuple-element.123), channel_id=1, source_target_pairs={{0,4},{1,5},{2,6},{3,7},{4,0},{5,1},{6,2},{7,3},{8,12},{9,13},{10,... | collective-permute-start | bytes 1671176 | tf_op jit(solution)/shard_map/ppermute | solution.py:345
